TPU v7x, 32 devices: a whole 2x2x4 slice. The times are simulated.
32 devices in a mesh: gz: 16 (over z, x, core), ord: 2 (over y).
Axes of the slice: x: 2, y: 2, z: 4, core: 2. Of those that a mesh axis runs over, the one named last changes fastest.
Arguments:
- initial: float32 [96, 32, 128, 128], P('ord', 'gz'), may hold values from -1 to 1
- cotangent: float32 [96, 32, 128, 128], P('ord', 'gz'), may hold values from -6 to 6
- mobility: float32 [96], P('ord'), may hold values from 0.05 to 0.15
- stiffness: float32 [96], P('ord'), may hold values from 0.5 to 1
Outputs:
- adjoint_initial: float32 [96, 32, 128, 128], P('ord', 'gz')
All inputs are finite; a program needn't handle non-finite values.
Results may differ from a plain program's by a relative error of at most 0.00002.
Values sent between devices are 32-bit elements; how exact they have to be, the bound alone decides.
No kernel may reach another device: no remote copies, remote signals or barrier semaphores. Data moves between devices by JAX's collectives and lax.ppermute only.
A program may use at most 192 MiB of HBM per device.

v0:
```python
import jax
import jax.numpy as jnp
from jax import lax
from jax.sharding import PartitionSpec as P

P_SIZE = 96


couple_scale = 2.0


def extended(block, sides, width):
    for axis, dim in sides:
        count = lax.axis_size(axis)
        forward = [(i, i + 1) for i in range(count - 1)]
        forward.append((count - 1, 0))
        backward = [(target, source) for source, target in forward]
        low = lax.ppermute(
            lax.slice_in_dim(block, block.shape[dim] - width, None, axis=dim), axis, forward
        )
        high = lax.ppermute(lax.slice_in_dim(block, 0, width, axis=dim), axis, backward)
        block = jnp.concatenate([low, block, high], axis=dim)
    return block


def inner_laplacian(values_ext):
    centre = values_ext[:, 1:-1]
    summed = values_ext[:, 2:] + values_ext[:, :-2] - 6.0 * centre
    for axis_num in (2, 3):
        summed = summed + jnp.roll(centre, 1, axis_num) + jnp.roll(centre, -1, axis_num)
    return summed


def well_slope(values, squares, coupling):
    return (
        -1.0 + 3.0 * values * values + 2.0 * coupling * squares - 6.0 * coupling * values * values
    )


def on_device(initial, cotangent, mobility, stiffness):
    order_dev = initial.shape[0]
    coupling = couple_scale / P_SIZE
    rate_col = mobility.reshape(-1, 1, 1, 1)
    stiff_col = stiffness.reshape(-1, 1, 1, 1)
    margin = 1
    joined = extended(jnp.concatenate((initial, cotangent), 0), (("gz", 1),), margin)
    field_ext = joined[:order_dev]
    adjoint_ext = joined[order_dev:]
    centre = field_ext[:, 1:-1]
    squares_first = lax.psum(jnp.sum(centre * centre, 0), "ord")
    potential = (
        -centre
        + centre * centre * centre
        + 2.0 * coupling * centre * (squares_first - centre * centre)
        - stiff_col * inner_laplacian(field_ext)
    )
    middle = centre - rate_col * potential
    scaled_ext = rate_col * adjoint_ext
    scaled = scaled_ext[:, 1:-1]
    squares_second, coupled_second = lax.psum(
        (jnp.sum(middle * middle, 0), jnp.sum(middle * scaled, 0)), "ord"
    )
    adjoint_middle = adjoint_ext[:, 1:-1] - (
        well_slope(middle, squares_second, coupling) * scaled
        + 4.0 * coupling * middle * coupled_second
        - stiff_col * inner_laplacian(scaled_ext)
    )
    scaled_middle = rate_col * adjoint_middle
    scaled_middle_ext = extended(scaled_middle, (("gz", 1),), 1)
    scaled_inner = scaled_middle_ext[:, 1:-1]
    coupled_first = lax.psum(jnp.sum(initial * scaled_inner, 0), "ord")
    return adjoint_middle - (
        well_slope(initial, squares_first, coupling) * scaled_inner
        + 4.0 * coupling * initial * coupled_first
        - stiff_col * inner_laplacian(scaled_middle_ext)
    )


def solution(mesh):
    return jax.shard_map(
        on_device,
        mesh=mesh,
        in_specs=(P("ord", "gz", None, None), P("ord", "gz", None, None), P("ord"), P("ord")),
        out_specs=P("ord", "gz", None, None),
        check_vma=False,
    )
```

profile of v0, /device:TPU:1, one launch (start us, length us, event | category | flops | bytes accessed | tf_op | source)
XLA Modules:
  0.0 394.5 jit_solution(5556632861140238494)
XLA Ops:
  6.5 7.3 %multiply_reduce_fusion = (f32[2,128,128]{2,1,0:T(8,128)}, f32[96,2,128,128]{3,2,1,0:T(8,128)}) fusion(f32[48,2,128,128]{3,2,1,0:T(8,128)} %param.4), kind=kLoop, calls=%fused_computation.8 | loop fusion | flops 3112959 | bytes 12713984 | tf_op jit(solution)/shard_map/reduce_sum | solution.py:50
  13.8 3.4 constant_dynamic-update-slice_fusion
  17.2 11.7 %fusion.47 = (f32[96,1,128,128]{3,2,1,0:T(8,128)}, f32[96,1,128,128]{3,2,1,0:T(8,128)}) fusion(f32[96,2,128,128]{3,2,1,0:T(8,128)} %constant_dynamic-update-slice_fusion), kind=kLoop, calls=%fused_computation.69 | loop fusion | bytes 25165824 | tf_op jit(solution)/shard_map/slice | solution.py:19
  28.8 0.1 collective-permute-start
  28.9 2.5 collective-permute-start.1
  31.5 0.0 all-reduce.9.cloned.1.call-start
  31.5 1.2 fusion.53
  32.7 12.2 %fusion.54 = (f32[48,2,127,128]{3,2,1,0:T(8,128)}, f32[48,2,127,128]{3,2,1,0:T(8,128)}) fusion(f32[48,2,128,128]{3,2,1,0:T(8,128)} %param.4), kind=kLoop, calls=%fused_computation.76 | loop fusion | bytes 24969216 | tf_op jit(solution)/shard_map/jit(_roll_static)/slice | solution.py:30
  44.9 11.1 %fusion.55 = (f32[48,2,128,1]{3,2,1,0:T(8,128)}, f32[48,2,128,1]{3,2,1,0:T(8,128)}) fusion(f32[48,2,128,128]{3,2,1,0:T(8,128)} %param.4), kind=kLoop, calls=%fused_computation.77 | loop fusion | bytes 196608 | tf_op jit(solution)/shard_map/jit(_roll_static)/slice | solution.py:30
  56.0 6.8 %fusion.56 = (f32[48,2,128,127]{3,2,1,0:T(8,128)}, f32[48,2,128,127]{3,2,1,0:T(8,128)}) fusion(f32[48,2,128,128]{3,2,1,0:T(8,128)S(1)} %bitcast.1), kind=kLoop, calls=%fused_computation.78 | loop fusion | bytes 24969216 | tf_op jit(solution)/shard_map/jit(_roll_static)/slice | solution.py:30
  62.8 105.0 %collective-permute-done = f32[96,1,128,128]{3,2,1,0:T(8,128)} collective-permute-done((f32[96,1,128,128]{3,2,1,0:T(8,128)}, f32[96,1,128,128]{3,2,1,0:T(8,128)}, u32[]{:S(2)}, u32[]{:S(2)}) %collective-permute-start) | collective-permute-done | bytes 6291488 | tf_op jit(solution)/shard_map/ppermute | solution.py:21
  167.8 10.9 %fusion = f32[48,4,128,128]{3,2,1,0:T(8,128)} fusion(f32[96,1,128,128]{3,2,1,0:T(8,128)} %collective-permute-done, f32[96,2,128,128]{3,2,1,0:T(8,128)} %constant_dynamic-update-slice_fusion, f32[96,1,128,128]{3,2,1,0:T(8,128)} %collective-permute-done.1, f32[48]{0:T(128)S(1)} %copy-done.2), kind=kLoop, calls=%fused_computation.1 | loop fusion | flops 9437184 | bytes 37748928 | tf_op jit(solution)/shard_map/mul | solution.py:58
  178.7 12.0 %fusion.44 = (f32[48,2,127,128]{3,2,1,0:T(8,128)}, f32[48,2,127,128]{3,2,1,0:T(8,128)}) fusion(f32[48,4,128,128]{3,2,1,0:T(8,128)} %fusion), kind=kLoop, calls=%fused_computation.66 | loop fusion | bytes 24969216 | tf_op jit(solution)/shard_map/jit(_roll_static)/slice | solution.py:30
  190.7 11.2 %fusion.45 = (f32[48,2,128,1]{3,2,1,0:T(8,128)}, f32[48,2,128,1]{3,2,1,0:T(8,128)}) fusion(f32[48,4,128,128]{3,2,1,0:T(8,128)} %fusion), kind=kLoop, calls=%fused_computation.67 | loop fusion | bytes 196608 | tf_op jit(solution)/shard_map/jit(_roll_static)/slice | solution.py:30
  202.0 24.9 %multiply_reduce_fusion.3 = (f32[2,128,128]{2,1,0:T(8,128)}, f32[2,128,128]{2,1,0:T(8,128)}, f32[48,2,128,128]{3,2,1,0:T(8,128)}) fusion(f32[48,4,128,128]{3,2,1,0:T(8,128)} %fusion, f32[48,2,128,128]{3,2,1,0:T(8,128)} %param.4, f32[48,2,128,1]{3,2,1,0:T(8,128)} %get-tuple-element.40, f32[48,2,128,127]{3,2,1,0:T(8,128)} %get-tuple-element.42, ...), kind=kLoop, calls=%fused_computation.57 | loop fusion | flops 45547520 | bytes 69599616 | tf_op jit(solution)/shard_map/reduce_sum | solution.py:61
  226.9 0.0 all-reduce.7.cloned.1.call-start
  227.0 11.0 %fusion.46 = (f32[48,2,128,127]{3,2,1,0:T(8,128)}, f32[48,2,128,127]{3,2,1,0:T(8,128)}) fusion(f32[48,4,128,128]{3,2,1,0:T(8,128)} %fusion), kind=kLoop, calls=%fused_computation.68 | loop fusion | bytes 24969216 | tf_op jit(solution)/shard_map/jit(_roll_static)/slice | solution.py:30
  238.0 1.2 fusion.43
  239.2 11.8 %all-reduce.9.cloned.1.call-done = (f32[2,128,128]{2,1,0:T(8,128)}, f32[2,128,128]{2,1,0:T(8,128)}) async-done(((f32[2,128,128]{2,1,0:T(8,128)}, f32[2,128,128]{2,1,0:T(8,128)}), (f32[2,128,128]{2,1,0:T(8,128)}, f32[2,128,128]{2,1,0:T(8,128)})) %all-reduce.9.cloned.1.call-update) | async-done | bytes 262160 | tf_op jit(solution)/shard_map/psum | solution.py:60
  251.0 1.0 broadcast_multiply_fusion.2
  252.0 31.8 %multiply_reduce_fusion.1 = (f32[2,128,128]{2,1,0:T(8,128)}, f32[48,2,128,128]{3,2,1,0:T(8,128)}, f32[48,2,128,128]{3,2,1,0:T(8,128)}) fusion(f32[48,2,128,128]{3,2,1,0:T(8,128)} %param.4, f32[48]{0:T(128)S(1)} %copy-done.2, f32[48,2,128,128]{3,2,1,0:T(8,128)} %param.5, f32[48,2,128,1]{3,2,1,0:T(8,128)} %get-tuple-element.18, ...), kind=kLoop, calls=%fused_computation.55 | loop fusion | flops 42434560 | bytes 75891072 | tf_op jit(solution)/shard_map/reduce_sum | solution.py:71
  283.8 6.4 %fusion.52 = (f32[48,1,128,128]{3,2,1,0:T(8,128)}, f32[48,1,128,128]{3,2,1,0:T(8,128)}) fusion(f32[48,2,128,128]{3,2,1,0:T(8,128)} %get-tuple-element.10), kind=kLoop, calls=%fused_computation.74 | loop fusion | bytes 12582912 | tf_op jit(solution)/shard_map/slice | solution.py:21
  290.1 1.1 collective-permute-start.2
  291.3 1.1 collective-permute-start.3
  292.4 11.2 %fusion.48 = (f32[48,2,128,127]{3,2,1,0:T(8,128)}, f32[48,2,128,127]{3,2,1,0:T(8,128)}) fusion(f32[48,2,128,128]{3,2,1,0:T(8,128)} %get-tuple-element.10), kind=kLoop, calls=%fused_computation.70 | loop fusion | bytes 24969216 | tf_op jit(solution)/shard_map/jit(_roll_static)/slice | solution.py:30
  303.6 6.7 %fusion.49 = (f32[48,2,128,1]{3,2,1,0:T(8,128)}, f32[48,2,128,1]{3,2,1,0:T(8,128)}) fusion(f32[48,2,128,128]{3,2,1,0:T(8,128)S(1)} %bitcast.3), kind=kLoop, calls=%fused_computation.71 | loop fusion | bytes 196608 | tf_op jit(solution)/shard_map/jit(_roll_static)/slice | solution.py:30
  310.3 6.3 %fusion.50 = (f32[48,2,127,128]{3,2,1,0:T(8,128)}, f32[48,2,127,128]{3,2,1,0:T(8,128)}) fusion(f32[48,2,128,128]{3,2,1,0:T(8,128)S(1)} %bitcast.3), kind=kLoop, calls=%fused_computation.72 | loop fusion | bytes 24969216 | tf_op jit(solution)/shard_map/jit(_roll_static)/slice | solution.py:30
  316.6 0.1 fusion.51
  316.7 0.0 all-reduce.7.cloned.1.call-done
  316.7 0.9 broadcast_multiply_fusion.1
  317.6 43.7 %collective-permute-done.2 = f32[48,1,128,128]{3,2,1,0:T(8,128)} collective-permute-done((f32[48,1,128,128]{3,2,1,0:T(8,128)}, f32[48,1,128,128]{3,2,1,0:T(8,128)}, u32[]{:S(2)}, u32[]{:S(2)}) %collective-permute-start.2) | collective-permute-done | bytes 3145760 | tf_op jit(solution)/shard_map/ppermute | solution.py:21
  361.3 26.6 %fusion.20 = f32[48,2,128,128]{3,2,1,0:T(8,128)} fusion(f32[48,2,128,128]{3,2,1,0:T(8,128)} %get-tuple-element.11, f32[48,2,128,128]{3,2,1,0:T(8,128)} %get-tuple-element.10, f32[48,2,128,128]{3,2,1,0:T(8,128)} %param.4, f32[48,1,128,128]{3,2,1,0:T(8,128)} %collective-permute-done.3, f32[48,1,128,128]{3,2,1,0:T(8,128)} %collective-permute-done.2, ...), kind=kLoop, calls=%fused_computation.29 | loop fusion | flops 40894464 | bytes 56885440 | tf_op jit(solution)/shard_map/sub | solution.py:72
  (26 shorter events, 0.1 us)
Async XLA Ops:
  6.5 195.5 %all-reduce.5.cloned.1.call-start = ((), (), s32[]{:S(2)}) async-start(), calls=%async_computation | async-start | bytes 262144 | tf_op jit(solution)/shard_map/psum | solution.py:50
  6.5 7.3 %copy-start = (f32[48,2,128,128]{3,2,1,0:T(8,128)S(1)}, f32[48,2,128,128]{3,2,1,0:T(8,128)}, u32[]{:S(2)}) copy-start(f32[48,2,128,128]{3,2,1,0:T(8,128)} %param.5) | copy-start | bytes 18874372
  17.2 38.8 %slice-start = ((s8[6291456]{0:T(1024)(128)(4,1)}), s8[2097152]{0:T(1024)(128)(4,1)S(1)}, s32[]{:S(2)}) async-start(s8[6291456]{0:T(1024)(128)(4,1)} %bitcast), calls=%async_computation.3 | async-start | bytes 4194304
  28.8 139.0 %collective-permute-start = (f32[96,1,128,128]{3,2,1,0:T(8,128)}, f32[96,1,128,128]{3,2,1,0:T(8,128)}, u32[]{:S(2)}, u32[]{:S(2)}) collective-permute-start(f32[96,1,128,128]{3,2,1,0:T(8,128)} %get-tuple-element.22), channel_id=1, source_target_pairs={{2,0},{4,2},{6,4},{8,6},{10,8},{12,10},{14,12},{16,14},{18,16},{20... | collective-permute-start | bytes 18874376 | tf_op jit(solution)/shard_map/ppermute | solution.py:21
  28.9 138.9 %collective-permute-start.1 = (f32[96,1,128,128]{3,2,1,0:T(8,128)}, f32[96,1,128,128]{3,2,1,0:T(8,128)}, u32[]{:S(2)}, u32[]{:S(2)}) collective-permute-start(f32[96,1,128,128]{3,2,1,0:T(8,128)} %get-tuple-element.21), channel_id=1, source_target_pairs={{0,2},{2,4},{4,6},{6,8},{8,10},{10,12},{12,14},{14,16},{16,18},{18... | collective-permute-start | bytes 18874376 | tf_op jit(solution)/shard_map/ppermute | solution.py:18
  31.5 219.5 %all-reduce.9.cloned.1.call-start = ((), (), s32[]{:S(2)}) async-start(), calls=%async_computation.2 | async-start | bytes 524288 | tf_op jit(solution)/shard_map/psum | solution.py:60
  32.7 23.3 %slice-start.1 = ((s8[6291456]{0:T(1024)(128)(4,1)}), s8[4194304]{0:T(1024)(128)(4,1)S(1)}, s32[]{:S(2)}) async-start(s8[6291456]{0:T(1024)(128)(4,1)} %bitcast), calls=%async_computation.4 | async-start | bytes 8388608
  56.0 111.8 %copy-start.2 = (f32[48]{0:T(128)S(1)}, f32[48]{0:T(128)}, u32[]{:S(2)}) copy-start(f32[48]{0:T(128)} %param.6) | copy-start | bytes 580
  190.7 11.3 %copy-start.3 = (f32[48]{0:T(128)S(1)}, f32[48]{0:T(128)}, u32[]{:S(2)}) copy-start(f32[48]{0:T(128)} %param.7) | copy-start | bytes 580
  226.9 89.8 %all-reduce.7.cloned.1.call-start = ((), (), s32[]{:S(2)}) async-start(), calls=%async_computation.1 | async-start | bytes 262144 | tf_op jit(solution)/shard_map/psum | solution.py:71
  283.8 8.6 %copy-start.1 = (f32[2,128,128]{2,1,0:T(8,128)S(1)}, f32[2,128,128]{2,1,0:T(8,128)}, u32[]{:S(2)}) copy-start(f32[2,128,128]{2,1,0:T(8,128)} %all-reduce.5.cloned.1.call-done) | copy-start | bytes 393220
  290.1 71.2 %collective-permute-start.2 = (f32[48,1,128,128]{3,2,1,0:T(8,128)}, f32[48,1,128,128]{3,2,1,0:T(8,128)}, u32[]{:S(2)}, u32[]{:S(2)}) collective-permute-start(f32[48,1,128,128]{3,2,1,0:T(8,128)} %get-tuple-element.31), channel_id=1, source_target_pairs={{2,0},{4,2},{6,4},{8,6},{10,8},{12,10},{14,12},{16,14},{18,16},{20... | collective-permute-start | bytes 9437192 | tf_op jit(solution)/shard_map/ppermute | solution.py:21
  291.3 70.1 %collective-permute-start.3 = (f32[48,1,128,128]{3,2,1,0:T(8,128)}, f32[48,1,128,128]{3,2,1,0:T(8,128)}, u32[]{:S(2)}, u32[]{:S(2)}) collective-permute-start(f32[48,1,128,128]{3,2,1,0:T(8,128)} %get-tuple-element.32), channel_id=1, source_target_pairs={{0,2},{2,4},{4,6},{6,8},{8,10},{10,12},{12,14},{14,16},{16,18},{18... | collective-permute-start | bytes 9437192 | tf_op jit(solution)/shard_map/ppermute | solution.py:18
  292.3 11.3 %slice-start.2 = ((s8[6291456]{0:T(1024)(128)(4,1)}), s8[2097152]{0:T(1024)(128)(4,1)S(1)}, s32[]{:S(2)}) async-start(s8[6291456]{0:T(1024)(128)(4,1)} %bitcast.2), calls=%async_computation.5 | async-start | bytes 4194304
  292.4 11.2 %slice-start.3 = ((s8[6291456]{0:T(1024)(128)(4,1)}), s8[4194304]{0:T(1024)(128)(4,1)S(1)}, s32[]{:S(2)}) async-start(s8[6291456]{0:T(1024)(128)(4,1)} %bitcast.2), calls=%async_computation.6 | async-start | bytes 8388608
Sparse Core Ops, SparseCore 0:
  31.6 24.6 all-reduce.4
  227.0 23.9 all-reduce.8
  292.5 22.9 all-reduce.6
where the time goes:
time: 395 us; the launch traced here: 394 us
  waiting for transfers between devices  161 us (41%)
  local copies, waits for them, and re-layouts  112 us (28%)
  other arithmetic  103 us (26%)
  between operations  13.2 us (3%)
  starting transfers between devices  4.9 us (1%)
    ppermute x2, waiting for transfers between devices, extended(): lax.ppermute(lax.slice_in_dim(block, 0, width, axis=dim), axis, backward)  149 us
    slice x8, local copies, waits for them, and re-layouts, inner_laplacian(): jnp.roll(centre, 1, axis_num)  66.7 us
    reduce_sum x1, other arithmetic, on_device(): coupled_first = lax.psum(jnp.sum(initial * scaled_inner, 0), 'ord')  31.8 us
    sub x1, other arithmetic, on_device(): adjoint_middle - (well_slope(initial, squares_first, coupling) * scaled_i...  26.6 us
    reduce_sum x1, other arithmetic, on_device(): jnp.sum(middle * middle, 0)  24.9 us
    slice x4, local copies, waits for them, and re-layouts, inner_laplacian(): jnp.roll(centre, -1, axis_num)  24.3 us
    psum x1, waiting for transfers between devices, on_device(): lax.psum((jnp.sum(middle * middle, 0), jnp.sum(middle * scaled, 0)), 'ord')  11.8 us
    slice x1, local copies, waits for them, and re-layouts, extended(): lax.slice_in_dim(block, block.shape[dim] - width, None, axis=dim)  11.7 us
  transfers between devices with their start and end apart: 7, of which 3 were waited for; matrix products, arithmetic and copies ran while one was open for 26% of the time, Pallas kernels for 0%

commit v1 on v0

v1 whole, which is shorter than its diff:
```python
import functools

import jax
import jax.numpy as jnp
from jax import lax
from jax.experimental import pallas as pl
from jax.experimental.pallas import tpu as pltpu
from jax.sharding import PartitionSpec as P

couple_scale = 2.0
PIECES = 8
IN_FLIGHT = 4


def pieces_of(orders):
    count = min(PIECES, orders)
    while orders % count:
        count -= 1
    return count, orders // count


def inner_pairs(count):
    return [(i, i ^ 1) for i in range(count)]


def outer_pairs(count):
    return [(i, (i + 1) % count if i % 2 else (i - 1) % count) for i in range(count)]


def order_sum(values):
    count = lax.axis_size("ord")
    if count & (count - 1):
        return lax.psum(values, "ord")
    step = 1
    while step < count:
        values = values + lax.ppermute(values, "ord", [(i, i ^ step) for i in range(count)])
        step *= 2
    return values


def in_plane(plane):
    rows, columns = plane.shape
    return (
        pltpu.roll(plane, 1, 0)
        + pltpu.roll(plane, rows - 1, 0)
        + pltpu.roll(plane, 1, 1)
        + pltpu.roll(plane, columns - 1, 1)
    )


def place(odd, position, planes):
    return position + odd * (planes - 1 - 2 * position)


def middle_kernel(base, planes, coupling, fresh, odd_ref, rate_ref, stiff_ref, field, adjoint, far, near, squares, *rest):
    if fresh:
        middle, sums = rest
    else:
        sums_before, middle, sums = rest
    step = pl.program_id(0)
    rate = rate_ref[base + step]
    stiff = rate * stiff_ref[base + step]
    odd = odd_ref[0]

    @pl.when(step == 0)
    def _():
        sums[...] = jnp.zeros_like(sums) if fresh else sums_before[...]

    for position in range(planes):
        z = place(odd, position, planes)
        centre = field[0, z]
        before = far[0] if position == 0 else field[0, place(odd, position - 1, planes)]
        after = near[0] if position == planes - 1 else field[0, place(odd, position + 1, planes)]
        around = in_plane(centre) + (before + after)
        factor = (1.0 + rate - 6.0 * stiff) - rate * (
            (2.0 * coupling) * squares[z] + (1.0 - 2.0 * coupling) * (centre * centre)
        )
        value = centre * factor + stiff * around
        middle[0, z] = value
        sums[0, z] += value * value
        sums[1, z] += value * (rate * adjoint[0, z])


def pulled_back(rate, stiff, coupling, value, adjoint, around, squares, coupled):
    factor = (1.0 + rate - 6.0 * stiff) - rate * (
        (2.0 * coupling) * squares + (3.0 - 6.0 * coupling) * (value * value)
    )
    return adjoint * factor - (4.0 * coupling) * (value * coupled) + stiff * around


def adjoint_kernel(base, planes, coupling, fresh, odd_ref, rate_ref, stiff_ref, field, middle, adjoint, far, near, sums, *rest):
    if fresh:
        outs, coupled = rest[:planes], rest[planes]
    else:
        coupled_before, outs, coupled = rest[0], rest[1:planes + 1], rest[planes + 1]
    step = pl.program_id(0)
    rate = rate_ref[base + step]
    stiff = rate * stiff_ref[base + step]
    odd = odd_ref[0]

    @pl.when(step == 0)
    def _():
        coupled[...] = jnp.zeros_like(coupled) if fresh else coupled_before[...]

    for position in range(planes):
        z = place(odd, position, planes)
        centre = adjoint[0, z]
        before = far[0] if position == 0 else adjoint[0, place(odd, position - 1, planes)]
        after = near[0] if position == planes - 1 else adjoint[0, place(odd, position + 1, planes)]
        around = in_plane(centre) + (before + after)
        value = pulled_back(rate, stiff, coupling, middle[0, z], centre, around, sums[0, z], sums[1, z])
        outs[position][0] = value
        coupled[z] += field[0, z] * (rate * value)


def last_kernel(base, planes, coupling, fresh, odd_ref, rate_ref, stiff_ref, field, far, near, squares, coupled, *rest):
    adjoint = rest[:planes]
    out = rest[-1]
    step = pl.program_id(0)
    rate = rate_ref[base + step]
    stiff = rate * stiff_ref[base + step]
    odd = odd_ref[0]
    for position in range(planes):
        z = place(odd, position, planes)
        centre = adjoint[position][0]
        before = far[0] if position == 0 else adjoint[position - 1][0]
        after = near[0] if position == planes - 1 else adjoint[position + 1][0]
        around = in_plane(centre) + (before + after)
        out[0, z] = pulled_back(rate, stiff, coupling, field[0, z], centre, around, squares[z], coupled[z])


def on_device(initial, cotangent, mobility, stiffness):
    orders, planes, rows, columns = initial.shape
    coupling = couple_scale / (orders * lax.axis_size("ord"))
    count, size = pieces_of(orders)
    ring = lax.axis_size("gz")
    odd = lax.rem(lax.axis_index("gz"), 2)
    odd_arr = odd.reshape(1).astype(jnp.int32)
    far_plane = odd * (planes - 1)
    near_plane = (planes - 1) - far_plane

    def send_far(plane):
        return lax.ppermute(plane, "gz", outer_pairs(ring))

    def send_near(plane):
        return lax.ppermute(plane, "gz", inner_pairs(ring))

    def cut(array, plane, start, length):
        return lax.dynamic_slice(array, (start, plane, 0, 0), (length, 1, rows, columns)).reshape(length, rows, columns)

    sent = []

    def queue(plane):
        if len(sent) >= IN_FLIGHT:
            plane, _ = lax.optimization_barrier((plane, sent[-IN_FLIGHT]))
        sent.append(send_far(plane))
        return sent[-1]

    scalar = pl.BlockSpec(memory_space=pltpu.SMEM)
    one_slab = (1, planes, rows, columns)
    one_plane = (1, rows, columns)
    slab = jax.ShapeDtypeStruct((size, planes, rows, columns), jnp.float32)
    plane_out = jax.ShapeDtypeStruct((size, rows, columns), jnp.float32)
    whole = jax.ShapeDtypeStruct(initial.shape, jnp.float32)
    cell = jax.ShapeDtypeStruct((planes, rows, columns), jnp.float32)
    cells = jax.ShapeDtypeStruct((2, planes, rows, columns), jnp.float32)
    own_slab = pl.BlockSpec(one_slab, lambda i: (i, 0, 0, 0))
    own_plane = pl.BlockSpec(one_plane, lambda i: (i, 0, 0))
    cell_spec = pl.BlockSpec(cell.shape, lambda i: (0, 0, 0))
    cells_spec = pl.BlockSpec(cells.shape, lambda i: (0, 0, 0, 0))

    def slab_at(base):
        return pl.BlockSpec(one_slab, lambda i: (base + i, 0, 0, 0))

    def plane_at(base):
        return pl.BlockSpec(one_plane, lambda i: (base + i, 0, 0))

    def call(kernel, piece, fresh, in_specs, args, out_specs, out_shape, alias, work):
        elements = size * planes * rows * columns
        return pl.pallas_call(
            functools.partial(kernel, piece * size, planes, coupling, fresh),
            grid=(size,),
            in_specs=[scalar] * 3 + in_specs,
            out_specs=out_specs,
            out_shape=out_shape,
            input_output_aliases=alias,
            cost_estimate=pl.CostEstimate(flops=work * elements, bytes_accessed=20 * elements, transcendentals=0),
            compiler_params=pltpu.CompilerParams(
                dimension_semantics=("arbitrary",), vmem_limit_bytes=32 * 1024 * 1024
            ),
        )(odd_arr, mobility, stiffness, *args)

    field_far = [queue(cut(initial, far_plane, k * size, size)) for k in range(count)]
    field_near = send_near(cut(initial, near_plane, 0, orders))
    squares_first = order_sum(jnp.sum(initial * initial, 0))
    adjoint_far = [queue(cut(cotangent, far_plane, k * size, size)) for k in range(count)]
    adjoint_near = send_near(cut(cotangent, near_plane, 0, orders))

    middle, sums = [], None
    for k in range(count):
        fresh = k == 0
        value, sums = call(
            middle_kernel, k, fresh,
            [slab_at(k * size), slab_at(k * size), own_plane, plane_at(k * size), cell_spec] + ([] if fresh else [cells_spec]),
            [initial, cotangent, field_far[k], field_near, squares_first] + ([] if fresh else [sums]),
            [own_slab, cells_spec], [slab, cells], {} if fresh else {8: 1}, 30,
        )
        middle.append(value)
    sums = order_sum(sums)

    outs, coupled = [], None
    far, near = [], []
    for k in range(count):
        fresh = k == 0
        *values, coupled = call(
            adjoint_kernel, k, fresh,
            [slab_at(k * size), own_slab, slab_at(k * size), own_plane, plane_at(k * size), cells_spec]
            + ([] if fresh else [cell_spec]),
            [initial, middle[k], cotangent, adjoint_far[k], adjoint_near, sums] + ([] if fresh else [coupled]),
            [own_plane] * planes + [cell_spec], [plane_out] * planes + [cell], {} if fresh else {9: planes}, 30,
        )
        outs.append(values)
        far.append(queue(values[0]))
        near.append(send_near(values[-1]))
    coupled = order_sum(coupled)

    result = None
    for k in range(count):
        fresh = k == 0
        result = call(
            last_kernel, k, fresh,
            [slab_at(k * size), own_plane, own_plane, cell_spec, cell_spec] + [own_plane] * planes
            + ([] if fresh else [pl.BlockSpec(memory_space=pl.ANY)]),
            [initial, far[k], near[k], squares_first, coupled] + outs[k] + ([] if fresh else [result]),
            slab_at(k * size), whole, {} if fresh else {8 + planes: 0}, 30,
        )
    return result


def solution(mesh):
    return jax.shard_map(
        on_device,
        mesh=mesh,
        in_specs=(P("ord", "gz", None, None), P("ord", "gz", None, None), P("ord"), P("ord")),
        out_specs=P("ord", "gz", None, None),
        check_vma=False,
    )
```

time: 395 us -> 262 us (0.66)
  local copies, waits for them, and re-layouts: 112 us -> 8.9 us
  other arithmetic: 103 us -> 3.54 us
  Pallas kernels: 0 us -> 78.6 us
  starting transfers between devices: 4.9 us -> 57.9 us
  waiting for transfers between devices: 161 us -> 110 us
  between operations: 13.2 us -> 0.31 us
    slice x14 -> x0, local copies, waits for them, and re-layouts: 109 us -> none  [the longest x8 66.7 us: inner_laplacian(): jnp.roll(centre, 1, axis_num)]
    pallas_call x0 -> x24, Pallas kernels: none -> 78.6 us  [call(): pl.pallas_call(functools.partial(kernel, piece * size, planes, coupling,...]
    reduce_sum x3 -> x1, other arithmetic: 63.9 us -> 3.48 us  [on_device(): squares_first = order_sum(jnp.sum(initial * initial, 0))]
    ppermute x4 -> x37, starting transfers between devices: 4.81 us -> 57.9 us  [the longest x24 36.8 us: send_far(): return lax.ppermute(plane, 'gz', outer_pairs(ring))]
    ppermute x4 -> x37, waiting for transfers between devices: 149 us -> 110 us  [the longest x24 107 us: send_far(): return lax.ppermute(plane, 'gz', outer_pairs(ring))]
    sub x1 -> x0, other arithmetic: 26.6 us -> none  [on_device(): adjoint_middle - (well_slope(initial, squares_first, coupling) * scaled_i...]
    mul x4 -> x0, other arithmetic: 12.8 us -> none  [the longest x1 10.9 us: on_device(): scaled_ext = rate_col * adjoint_ext]
    psum x3 -> x0, waiting for transfers between devices: 11.8 us -> none  [the longest x1 11.8 us: on_device(): lax.psum((jnp.sum(middle * middle, 0), jnp.sum(middle * scaled, 0)), 'ord')]
  transfers between devices with their start and end apart: 7 -> 37, of which waited for: 3 -> 14; matrix products, arithmetic and copies ran while one was open for 26% -> 3% of each run, Pallas kernels for 0% -> 29%
where the time goes in v1:
time: 262 us; the launch traced here: 260 us
  waiting for transfers between devices  110 us (42%)
  Pallas kernels  78.6 us (30%)
  starting transfers between devices  57.9 us (22%)
  local copies, waits for them, and re-layouts  8.9 us (3%)
  other arithmetic  3.54 us (1%)
    ppermute x24, waiting for transfers between devices, send_far(): return lax.ppermute(plane, 'gz', outer_pairs(ring))  107 us
    pallas_call x24, Pallas kernels, call(): pl.pallas_call(functools.partial(kernel, piece * size, planes, coupling,...  78.6 us
    ppermute x24, starting transfers between devices, send_far(): return lax.ppermute(plane, 'gz', outer_pairs(ring))  36.8 us
    ppermute x10, starting transfers between devices, send_near(): return lax.ppermute(plane, 'gz', inner_pairs(ring))  16.1 us
    reshape x4, local copies, waits for them, and re-layouts, cut(): lax.dynamic_slice(array, (start, plane, 0, 0), (length, 1, rows, columns))  8.41 us
  transfers between devices with their start and end apart: 37, of which 14 were waited for; matrix products, arithmetic and copies ran while one was open for 3% of the time, Pallas kernels for 29%

profile of v1, /device:TPU:1, one launch (start us, length us, event | category | flops | bytes accessed | tf_op | source)
XLA Modules:
  0.0 259.5 jit_solution(6508614645610584738)
XLA Ops:
  0.0 4.1 %dynamic-slice_bitcast_fusion.1 = f32[48,128,128]{2,1,0:T(8,128)} fusion(f32[48,2,128,128]{3,2,1,0:T(8,128)} %field.47, s32[]{:T(128)S(6)} %select_n.5), kind=kLoop, calls=%fused_computation.2 | loop fusion | bytes 6291460 | tf_op jit(solution)/shard_map/reshape | solution.py:149
  11.5 3.5 %multiply_reduce_fusion = f32[2,128,128]{2,1,0:T(8,128)S(1)} fusion(f32[48,2,128,128]{3,2,1,0:T(8,128)} %field.47), kind=kLoop, calls=%fused_computation | loop fusion | flops 3112960 | bytes 6422528 | tf_op jit(solution)/shard_map/reduce_sum | solution.py:195
  19.4 3.2 %collective-permute-start.4 = (f32[6,128,128]{2,1,0:T(8,128)S(1)}, f32[6,128,128]{2,1,0:T(8,128)S(1)}, u32[]{:S(2)}, u32[]{:S(2)}) collective-permute-start(f32[6,128,128]{2,1,0:T(8,128)S(1)} %get-tuple-element.137), channel_id=1, source_target_pairs={{0,30},{2,4},{4,2},{6,8},{8,6},{10,12},{12,10},{14,16},{16,14},{18... | collective-permute-start | bytes 1179656 | tf_op jit(solution)/shard_map/ppermute | solution.py:143
  27.1 44.6 %collective-permute-done.6.far = f32[6,128,128]{2,1,0:T(8,128)S(1)} collective-permute-done((f32[6,128,128]{2,1,0:T(8,128)S(1)}, f32[6,128,128]{2,1,0:T(8,128)S(1)}, u32[]{:S(2)}, u32[]{:S(2)}) %collective-permute-start.6) | collective-permute-done | bytes 393248 | tf_op jit(solution)/shard_map/ppermute | solution.py:143
  86.2 22.6 %collective-permute-done.7.far = f32[6,128,128]{2,1,0:T(8,128)S(1)} collective-permute-done((f32[6,128,128]{2,1,0:T(8,128)S(1)}, f32[6,128,128]{2,1,0:T(8,128)S(1)}, u32[]{:S(2)}, u32[]{:S(2)}) %collective-permute-start.7) | collective-permute-done | bytes 393248 | tf_op jit(solution)/shard_map/ppermute | solution.py:143
  119.8 3.3 %shard_map.46 = (f32[6,2,128,128]{3,2,1,0:T(8,128)S(1)}, f32[2,2,128,128]{3,2,1,0:T(8,128)S(1)}) custom-call(s32[1]{0:T(128)} %bitcast.odd_ref, f32[48]{0:T(128)S(1)} %copy-done.1, f32[48]{0:T(128)S(1)} %copy-done.2, f32[48,2,128,128]{3,2,1,0:T(8,128)S(1)} %bitcast.38, f32[48,2,128,128]{3,2,1,0:T(8,128)S(1)} %bitcast.40, ...), custom_call_target="tpu_custom_call" | custom-call | flops 5898240 | bytes 3932160 | tf_op jit(solution)/shard_map/pallas_call | solution.py:180
  123.2 3.4 %shard_map.47 = (f32[6,2,128,128]{3,2,1,0:T(8,128)S(1)}, f32[2,2,128,128]{3,2,1,0:T(8,128)S(1)}) custom-call(s32[1]{0:T(128)} %bitcast.odd_ref, f32[48]{0:T(128)S(1)} %copy-done.1, f32[48]{0:T(128)S(1)} %copy-done.2, f32[48,2,128,128]{3,2,1,0:T(8,128)S(1)} %bitcast.38, f32[48,2,128,128]{3,2,1,0:T(8,128)S(1)} %bitcast.40, ...), custom_call_target="tpu_custom_call", output_to_operand_aliasing={{1}: (8, {})} | custom-call | flops 5898240 | bytes 3932160 | tf_op jit(solution)/shard_map/pallas_call | solution.py:180
  126.5 3.4 %shard_map.48 = (f32[6,2,128,128]{3,2,1,0:T(8,128)S(1)}, f32[2,2,128,128]{3,2,1,0:T(8,128)S(1)}) custom-call(s32[1]{0:T(128)} %bitcast.odd_ref, f32[48]{0:T(128)S(1)} %copy-done.1, f32[48]{0:T(128)S(1)} %copy-done.2, f32[48,2,128,128]{3,2,1,0:T(8,128)S(1)} %bitcast.38, f32[48,2,128,128]{3,2,1,0:T(8,128)S(1)} %bitcast.40, ...), custom_call_target="tpu_custom_call", output_to_operand_aliasing={{1}: (8, {})} | custom-call | flops 5898240 | bytes 3932160 | tf_op jit(solution)/shard_map/pallas_call | solution.py:180
  129.9 3.4 %shard_map.49 = (f32[6,2,128,128]{3,2,1,0:T(8,128)S(1)}, f32[2,2,128,128]{3,2,1,0:T(8,128)S(1)}) custom-call(s32[1]{0:T(128)} %bitcast.odd_ref, f32[48]{0:T(128)S(1)} %copy-done.1, f32[48]{0:T(128)S(1)} %copy-done.2, f32[48,2,128,128]{3,2,1,0:T(8,128)S(1)} %bitcast.38, f32[48,2,128,128]{3,2,1,0:T(8,128)S(1)} %bitcast.40, ...), custom_call_target="tpu_custom_call", output_to_operand_aliasing={{1}: (8, {})} | custom-call | flops 5898240 | bytes 3932160 | tf_op jit(solution)/shard_map/pallas_call | solution.py:180
  133.3 3.4 %shard_map.50 = (f32[6,2,128,128]{3,2,1,0:T(8,128)S(1)}, f32[2,2,128,128]{3,2,1,0:T(8,128)S(1)}) custom-call(s32[1]{0:T(128)} %bitcast.odd_ref, f32[48]{0:T(128)S(1)} %copy-done.1, f32[48]{0:T(128)S(1)} %copy-done.2, f32[48,2,128,128]{3,2,1,0:T(8,128)S(1)} %bitcast.38, f32[48,2,128,128]{3,2,1,0:T(8,128)S(1)} %bitcast.40, ...), custom_call_target="tpu_custom_call", output_to_operand_aliasing={{1}: (8, {})} | custom-call | flops 5898240 | bytes 3932160 | tf_op jit(solution)/shard_map/pallas_call | solution.py:180
  136.6 3.4 %shard_map.51 = (f32[6,2,128,128]{3,2,1,0:T(8,128)S(1)}, f32[2,2,128,128]{3,2,1,0:T(8,128)S(1)}) custom-call(s32[1]{0:T(128)} %bitcast.odd_ref, f32[48]{0:T(128)S(1)} %copy-done.1, f32[48]{0:T(128)S(1)} %copy-done.2, f32[48,2,128,128]{3,2,1,0:T(8,128)S(1)} %bitcast.38, f32[48,2,128,128]{3,2,1,0:T(8,128)S(1)} %bitcast.40, ...), custom_call_target="tpu_custom_call", output_to_operand_aliasing={{1}: (8, {})} | custom-call | flops 5898240 | bytes 3932160 | tf_op jit(solution)/shard_map/pallas_call | solution.py:180
  140.0 3.4 %shard_map.52 = (f32[6,2,128,128]{3,2,1,0:T(8,128)S(1)}, f32[2,2,128,128]{3,2,1,0:T(8,128)S(1)}) custom-call(s32[1]{0:T(128)} %bitcast.odd_ref, f32[48]{0:T(128)S(1)} %copy-done.1, f32[48]{0:T(128)S(1)} %copy-done.2, f32[48,2,128,128]{3,2,1,0:T(8,128)S(1)} %bitcast.38, f32[48,2,128,128]{3,2,1,0:T(8,128)S(1)} %bitcast.40, ...), custom_call_target="tpu_custom_call", output_to_operand_aliasing={{1}: (8, {})} | custom-call | flops 5898240 | bytes 3932160 | tf_op jit(solution)/shard_map/pallas_call | solution.py:180
  143.4 3.4 %shard_map.53 = (f32[6,2,128,128]{3,2,1,0:T(8,128)S(1)}, f32[2,2,128,128]{3,2,1,0:T(8,128)S(1)}) custom-call(s32[1]{0:T(128)} %bitcast.odd_ref, f32[48]{0:T(128)S(1)} %copy-done.1, f32[48]{0:T(128)S(1)} %copy-done.2, f32[48,2,128,128]{3,2,1,0:T(8,128)S(1)} %bitcast.38, f32[48,2,128,128]{3,2,1,0:T(8,128)S(1)} %bitcast.40, ...), custom_call_target="tpu_custom_call", output_to_operand_aliasing={{1}: (8, {})} | custom-call | flops 5898240 | bytes 3932160 | tf_op jit(solution)/shard_map/pallas_call | solution.py:180
  154.9 3.3 %shard_map.54 = (f32[6,128,128]{2,1,0:T(8,128)S(1)}, f32[6,128,128]{2,1,0:T(8,128)S(1)}, f32[2,128,128]{2,1,0:T(8,128)S(1)}) custom-call(s32[1]{0:T(128)} %bitcast.odd_ref, f32[48]{0:T(128)S(1)} %copy-done.1, f32[48]{0:T(128)S(1)} %copy-done.2, f32[48,2,128,128]{3,2,1,0:T(8,128)S(1)} %bitcast.38, f32[6,2,128,128]{3,2,1,0:T(8,128)S(1)} %get-tuple-element.92.middle, ...), custom_call_target="tpu_custom_call" | custom-call | flops 5898240 | bytes 3932160 | tf_op jit(solution)/shard_map/pallas_call | solution.py:180
  158.3 3.3 %shard_map.55 = (f32[6,128,128]{2,1,0:T(8,128)S(1)}, f32[6,128,128]{2,1,0:T(8,128)S(1)}, f32[2,128,128]{2,1,0:T(8,128)S(1)}) custom-call(s32[1]{0:T(128)} %bitcast.odd_ref, f32[48]{0:T(128)S(1)} %copy-done.1, f32[48]{0:T(128)S(1)} %copy-done.2, f32[48,2,128,128]{3,2,1,0:T(8,128)S(1)} %bitcast.38, ...), custom_call_target="tpu_custom_call", output_to_operand_aliasing={{2}: (9, {})} | custom-call | flops 5898240 | bytes 3932160 | tf_op jit(solution)/shard_map/pallas_call | solution.py:180
  161.7 3.3 %shard_map.56 = (f32[6,128,128]{2,1,0:T(8,128)S(1)}, f32[6,128,128]{2,1,0:T(8,128)S(1)}, f32[2,128,128]{2,1,0:T(8,128)S(1)}) custom-call(s32[1]{0:T(128)} %bitcast.odd_ref, f32[48]{0:T(128)S(1)} %copy-done.1, f32[48]{0:T(128)S(1)} %copy-done.2, f32[48,2,128,128]{3,2,1,0:T(8,128)S(1)} %bitcast.38, ...), custom_call_target="tpu_custom_call", output_to_operand_aliasing={{2}: (9, {})} | custom-call | flops 5898240 | bytes 3932160 | tf_op jit(solution)/shard_map/pallas_call | solution.py:180
  165.0 3.3 %shard_map.57 = (f32[6,128,128]{2,1,0:T(8,128)S(1)}, f32[6,128,128]{2,1,0:T(8,128)S(1)}, f32[2,128,128]{2,1,0:T(8,128)S(1)}) custom-call(s32[1]{0:T(128)} %bitcast.odd_ref, f32[48]{0:T(128)S(1)} %copy-done.1, f32[48]{0:T(128)S(1)} %copy-done.2, f32[48,2,128,128]{3,2,1,0:T(8,128)S(1)} %bitcast.38, ...), custom_call_target="tpu_custom_call", output_to_operand_aliasing={{2}: (9, {})} | custom-call | flops 5898240 | bytes 3932160 | tf_op jit(solution)/shard_map/pallas_call | solution.py:180
  168.3 3.3 %shard_map.58 = (f32[6,128,128]{2,1,0:T(8,128)S(1)}, f32[6,128,128]{2,1,0:T(8,128)S(1)}, f32[2,128,128]{2,1,0:T(8,128)S(1)}) custom-call(s32[1]{0:T(128)} %bitcast.odd_ref, f32[48]{0:T(128)S(1)} %copy-done.1, f32[48]{0:T(128)S(1)} %copy-done.2, f32[48,2,128,128]{3,2,1,0:T(8,128)S(1)} %bitcast.38, ...), custom_call_target="tpu_custom_call", output_to_operand_aliasing={{2}: (9, {})} | custom-call | flops 5898240 | bytes 3932160 | tf_op jit(solution)/shard_map/pallas_call | solution.py:180
  171.7 3.3 %shard_map.59 = (f32[6,128,128]{2,1,0:T(8,128)S(1)}, f32[6,128,128]{2,1,0:T(8,128)S(1)}, f32[2,128,128]{2,1,0:T(8,128)S(1)}) custom-call(s32[1]{0:T(128)} %bitcast.odd_ref, f32[48]{0:T(128)S(1)} %copy-done.1, f32[48]{0:T(128)S(1)} %copy-done.2, f32[48,2,128,128]{3,2,1,0:T(8,128)S(1)} %bitcast.38, ...), custom_call_target="tpu_custom_call", output_to_operand_aliasing={{2}: (9, {})} | custom-call | flops 5898240 | bytes 3932160 | tf_op jit(solution)/shard_map/pallas_call | solution.py:180
  175.0 3.3 %shard_map.60 = (f32[6,128,128]{2,1,0:T(8,128)S(1)}, f32[6,128,128]{2,1,0:T(8,128)S(1)}, f32[2,128,128]{2,1,0:T(8,128)S(1)}) custom-call(s32[1]{0:T(128)} %bitcast.odd_ref, f32[48]{0:T(128)S(1)} %copy-done.1, f32[48]{0:T(128)S(1)} %copy-done.2, f32[48,2,128,128]{3,2,1,0:T(8,128)S(1)} %bitcast.38, ...), custom_call_target="tpu_custom_call", output_to_operand_aliasing={{2}: (9, {})} | custom-call | flops 5898240 | bytes 3932160 | tf_op jit(solution)/shard_map/pallas_call | solution.py:180
  178.4 3.3 %shard_map.61 = (f32[6,128,128]{2,1,0:T(8,128)S(1)}, f32[6,128,128]{2,1,0:T(8,128)S(1)}, f32[2,128,128]{2,1,0:T(8,128)S(1)}) custom-call(s32[1]{0:T(128)} %bitcast.odd_ref, f32[48]{0:T(128)S(1)} %copy-done.1, f32[48]{0:T(128)S(1)} %copy-done.2, f32[48,2,128,128]{3,2,1,0:T(8,128)S(1)} %bitcast.38, ...), custom_call_target="tpu_custom_call", output_to_operand_aliasing={{2}: (9, {})} | custom-call | flops 5898240 | bytes 3932160 | tf_op jit(solution)/shard_map/pallas_call | solution.py:180
  185.0 3.5 %collective-permute-start.35 = (f32[6,128,128]{2,1,0:T(8,128)S(1)}, f32[6,128,128]{2,1,0:T(8,128)S(1)}, u32[]{:S(2)}, u32[]{:S(2)}) collective-permute-start(f32[6,128,128]{2,1,0:T(8,128)S(1)} %get-tuple-element.123.rest_1_), channel_id=1, source_target_pairs={{0,2},{2,0},{4,6},{6,4},{8,10},{10,8},{12,14},{14,12},{16,18},{18,... | collective-permute-start | bytes 1179656 | tf_op jit(solution)/shard_map/ppermute | solution.py:146
  190.4 12.7 %collective-permute-done.27.far = f32[6,128,128]{2,1,0:T(8,128)S(1)} collective-permute-done((f32[6,128,128]{2,1,0:T(8,128)S(1)}, f32[6,128,128]{2,1,0:T(8,128)S(1)}, u32[]{:S(2)}, u32[]{:S(2)}) %collective-permute-start.27) | collective-permute-done | bytes 393248 | tf_op jit(solution)/shard_map/ppermute | solution.py:143
  203.6 3.7 %collective-permute-done.24.far = f32[6,128,128]{2,1,0:T(8,128)S(1)} collective-permute-done((f32[6,128,128]{2,1,0:T(8,128)S(1)}, f32[6,128,128]{2,1,0:T(8,128)S(1)}, u32[]{:S(2)}, u32[]{:S(2)}) %collective-permute-start.24) | collective-permute-done | bytes 393248 | tf_op jit(solution)/shard_map/ppermute | solution.py:143
  213.4 11.9 %collective-permute-start.22 = (f32[6,128,128]{2,1,0:T(8,128)S(1)}, f32[6,128,128]{2,1,0:T(8,128)S(1)}, u32[]{:S(2)}, u32[]{:S(2)}) collective-permute-start(f32[6,128,128]{2,1,0:T(8,128)S(1)} %get-tuple-element.104.rest_1_), channel_id=1, source_target_pairs={{0,2},{2,0},{4,6},{6,4},{8,10},{10,8},{12,14},{14,12},{16,18},{18,... | collective-permute-start | bytes 1179656 | tf_op jit(solution)/shard_map/ppermute | solution.py:146
  225.3 6.6 %collective-permute-done.31.far = f32[6,128,128]{2,1,0:T(8,128)S(1)} collective-permute-done((f32[6,128,128]{2,1,0:T(8,128)S(1)}, f32[6,128,128]{2,1,0:T(8,128)S(1)}, u32[]{:S(2)}, u32[]{:S(2)}) %collective-permute-start.31) | collective-permute-done | bytes 393248 | tf_op jit(solution)/shard_map/ppermute | solution.py:143
  234.4 3.2 %shard_map.62.rest_2_ = f32[48,2,128,128]{3,2,1,0:T(8,128)} custom-call(s32[1]{0:T(128)} %bitcast.odd_ref, f32[48]{0:T(128)S(1)} %copy-done.1, f32[48]{0:T(128)S(1)} %copy-done.2, f32[48,2,128,128]{3,2,1,0:T(8,128)S(1)} %bitcast.38, f32[6,128,128]{2,1,0:T(8,128)S(1)} %collective-permute-done.30.far, f32[6,128,128]{2,1,0:T(8,128)S(1)} %collective-permute-done.36.near, ...), custom_call_target="tpu_custom_call" | custom-call | flops 5898240 | bytes 3932160 | tf_op jit(solution)/shard_map/pallas_call | solution.py:180
  243.8 3.1 %shard_map.65.rest_2_ = f32[48,2,128,128]{3,2,1,0:T(8,128)} custom-call(s32[1]{0:T(128)} %bitcast.odd_ref, f32[48]{0:T(128)S(1)} %copy-done.1, f32[48]{0:T(128)S(1)} %copy-done.2, f32[48,2,128,128]{3,2,1,0:T(8,128)S(1)} %bitcast.38, f32[6,128,128]{2,1,0:T(8,128)S(1)} %collective-permute-done.20.far, ...), custom_call_target="tpu_custom_call", output_to_operand_aliasing={{}: (10, {})} | custom-call | flops 5898240 | bytes 3932160 | tf_op jit(solution)/shard_map/pallas_call | solution.py:180
  246.9 3.1 %shard_map.66.rest_2_ = f32[48,2,128,128]{3,2,1,0:T(8,128)} custom-call(s32[1]{0:T(128)} %bitcast.odd_ref, f32[48]{0:T(128)S(1)} %copy-done.1, f32[48]{0:T(128)S(1)} %copy-done.2, f32[48,2,128,128]{3,2,1,0:T(8,128)S(1)} %bitcast.38, f32[6,128,128]{2,1,0:T(8,128)S(1)} %collective-permute-done.31.far, ...), custom_call_target="tpu_custom_call", output_to_operand_aliasing={{}: (10, {})} | custom-call | flops 5898240 | bytes 3932160 | tf_op jit(solution)/shard_map/pallas_call | solution.py:180
  250.1 3.1 %shard_map.67.rest_2_ = f32[48,2,128,128]{3,2,1,0:T(8,128)} custom-call(s32[1]{0:T(128)} %bitcast.odd_ref, f32[48]{0:T(128)S(1)} %copy-done.1, f32[48]{0:T(128)S(1)} %copy-done.2, f32[48,2,128,128]{3,2,1,0:T(8,128)S(1)} %bitcast.38, f32[6,128,128]{2,1,0:T(8,128)S(1)} %collective-permute-done.28.far, ...), custom_call_target="tpu_custom_call", output_to_operand_aliasing={{}: (10, {})} | custom-call | flops 5898240 | bytes 3932160 | tf_op jit(solution)/shard_map/pallas_call | solution.py:180
  253.2 3.2 %shard_map.68.rest_2_ = f32[48,2,128,128]{3,2,1,0:T(8,128)} custom-call(s32[1]{0:T(128)} %bitcast.odd_ref, f32[48]{0:T(128)S(1)} %copy-done.1, f32[48]{0:T(128)S(1)} %copy-done.2, f32[48,2,128,128]{3,2,1,0:T(8,128)S(1)} %bitcast.38, f32[6,128,128]{2,1,0:T(8,128)S(1)} %collective-permute-done.25.far, ...), custom_call_target="tpu_custom_call", output_to_operand_aliasing={{}: (10, {})} | custom-call | flops 5898240 | bytes 3932160 | tf_op jit(solution)/shard_map/pallas_call | solution.py:180
  256.4 3.2 %shard_map.69 = f32[48,2,128,128]{3,2,1,0:T(8,128)} custom-call(s32[1]{0:T(128)} %bitcast.odd_ref, f32[48]{0:T(128)S(1)} %copy-done.1, f32[48]{0:T(128)S(1)} %copy-done.2, f32[48,2,128,128]{3,2,1,0:T(8,128)S(1)} %bitcast.38, f32[6,128,128]{2,1,0:T(8,128)S(1)} %collective-permute-done.21.far, ...), custom_call_target="tpu_custom_call", output_to_operand_aliasing={{}: (10, {})} | custom-call | flops 5898240 | bytes 3932160 | tf_op jit(solution)/shard_map/pallas_call | solution.py:180
  (90 shorter events, 70.5 us)
Async XLA Ops:
  4.1 115.7 %collective-permute-start.2 = (f32[48,128,128]{2,1,0:T(8,128)}, f32[48,128,128]{2,1,0:T(8,128)}, u32[]{:S(2)}, u32[]{:S(2)}) collective-permute-start(f32[48,128,128]{2,1,0:T(8,128)} %dynamic-slice_bitcast_fusion.1), channel_id=1, source_target_pairs={{0,2},{2,0},{4,6},{6,4},{8,10},{10,8},{12,14},{14,12},{16,18},{18,... | collective-permute-start | bytes 9437192 | tf_op jit(solution)/shard_map/ppermute | solution.py:146
  6.5 148.4 %collective-permute-start.12 = (f32[48,128,128]{2,1,0:T(8,128)}, f32[48,128,128]{2,1,0:T(8,128)}, u32[]{:S(2)}, u32[]{:S(2)}) collective-permute-start(f32[48,128,128]{2,1,0:T(8,128)} %dynamic-slice_bitcast_fusion), channel_id=1, source_target_pairs={{0,2},{2,0},{4,6},{6,4},{8,10},{10,8},{12,14},{14,12},{16,18},{18,... | collective-permute-start | bytes 9437192 | tf_op jit(solution)/shard_map/ppermute | solution.py:146
  8.8 16.5 %collective-permute-start.8 = (f32[6,128,128]{2,1,0:T(8,128)S(1)}, f32[6,128,128]{2,1,0:T(8,128)S(1)}, u32[]{:S(2)}, u32[]{:S(2)}) collective-permute-start(f32[6,128,128]{2,1,0:T(8,128)S(1)} %get-tuple-element.133), channel_id=1, source_target_pairs={{0,30},{2,4},{4,2},{6,8},{8,6},{10,12},{12,10},{14,16},{16,14},{18... | collective-permute-start | bytes 1179656 | tf_op jit(solution)/shard_map/ppermute | solution.py:143
  11.4 60.2 %collective-permute-start.6 = (f32[6,128,128]{2,1,0:T(8,128)S(1)}, f32[6,128,128]{2,1,0:T(8,128)S(1)}, u32[]{:S(2)}, u32[]{:S(2)}) collective-permute-start(f32[6,128,128]{2,1,0:T(8,128)S(1)} %get-tuple-element.135), channel_id=1, source_target_pairs={{0,30},{2,4},{4,2},{6,8},{8,6},{10,12},{12,10},{14,16},{16,14},{18... | collective-permute-start | bytes 1179656 | tf_op jit(solution)/shard_map/ppermute | solution.py:143
  19.4 56.5 %collective-permute-start.4 = (f32[6,128,128]{2,1,0:T(8,128)S(1)}, f32[6,128,128]{2,1,0:T(8,128)S(1)}, u32[]{:S(2)}, u32[]{:S(2)}) collective-permute-start(f32[6,128,128]{2,1,0:T(8,128)S(1)} %get-tuple-element.137), channel_id=1, source_target_pairs={{0,30},{2,4},{4,2},{6,8},{8,6},{10,12},{12,10},{14,16},{16,14},{18... | collective-permute-start | bytes 1179656 | tf_op jit(solution)/shard_map/ppermute | solution.py:143
  25.3 54.8 %collective-permute-start = (f32[6,128,128]{2,1,0:T(8,128)S(1)}, f32[6,128,128]{2,1,0:T(8,128)S(1)}, u32[]{:S(2)}, u32[]{:S(2)}) collective-permute-start(f32[6,128,128]{2,1,0:T(8,128)S(1)} %get-tuple-element.139), channel_id=1, source_target_pairs={{0,30},{2,4},{4,2},{6,8},{8,6},{10,12},{12,10},{14,16},{16,14},{18... | collective-permute-start | bytes 1179656 | tf_op jit(solution)/shard_map/ppermute | solution.py:143
  71.7 12.6 %collective-permute-start.9 = (f32[6,128,128]{2,1,0:T(8,128)S(1)}, f32[6,128,128]{2,1,0:T(8,128)S(1)}, u32[]{:S(2)}, u32[]{:S(2)}) collective-permute-start(f32[6,128,128]{2,1,0:T(8,128)S(1)} %get-tuple-element.68), channel_id=1, source_target_pairs={{0,30},{2,4},{4,2},{6,8},{8,6},{10,12},{12,10},{14,16},{16,14},{18... | collective-permute-start | bytes 1179656 | tf_op jit(solution)/shard_map/ppermute | solution.py:143
  75.9 33.0 %collective-permute-start.7 = (f32[6,128,128]{2,1,0:T(8,128)S(1)}, f32[6,128,128]{2,1,0:T(8,128)S(1)}, u32[]{:S(2)}, u32[]{:S(2)}) collective-permute-start(f32[6,128,128]{2,1,0:T(8,128)S(1)} %get-tuple-element.67), channel_id=1, source_target_pairs={{0,30},{2,4},{4,2},{6,8},{8,6},{10,12},{12,10},{14,16},{16,14},{18... | collective-permute-start | bytes 1179656 | tf_op jit(solution)/shard_map/ppermute | solution.py:143
  80.1 33.0 %collective-permute-start.5 = (f32[6,128,128]{2,1,0:T(8,128)S(1)}, f32[6,128,128]{2,1,0:T(8,128)S(1)}, u32[]{:S(2)}, u32[]{:S(2)}) collective-permute-start(f32[6,128,128]{2,1,0:T(8,128)S(1)} %get-tuple-element.66), channel_id=1, source_target_pairs={{0,30},{2,4},{4,2},{6,8},{8,6},{10,12},{12,10},{14,16},{16,14},{18... | collective-permute-start | bytes 1179656 | tf_op jit(solution)/shard_map/ppermute | solution.py:143
  84.3 33.7 %collective-permute-start.1 = (f32[6,128,128]{2,1,0:T(8,128)S(1)}, f32[6,128,128]{2,1,0:T(8,128)S(1)}, u32[]{:S(2)}, u32[]{:S(2)}) collective-permute-start(f32[6,128,128]{2,1,0:T(8,128)S(1)} %get-tuple-element.65), channel_id=1, source_target_pairs={{0,30},{2,4},{4,2},{6,8},{8,6},{10,12},{12,10},{14,16},{16,14},{18... | collective-permute-start | bytes 1179656 | tf_op jit(solution)/shard_map/ppermute | solution.py:143
  108.8 37.9 %collective-permute-start.18 = (f32[6,128,128]{2,1,0:T(8,128)S(1)}, f32[6,128,128]{2,1,0:T(8,128)S(1)}, u32[]{:S(2)}, u32[]{:S(2)}) collective-permute-start(f32[6,128,128]{2,1,0:T(8,128)S(1)} %get-tuple-element.87), channel_id=1, source_target_pairs={{0,30},{2,4},{4,2},{6,8},{8,6},{10,12},{12,10},{14,16},{16,14},{18... | collective-permute-start | bytes 1179656 | tf_op jit(solution)/shard_map/ppermute | solution.py:143
  113.0 35.6 %collective-permute-start.16 = (f32[6,128,128]{2,1,0:T(8,128)S(1)}, f32[6,128,128]{2,1,0:T(8,128)S(1)}, u32[]{:S(2)}, u32[]{:S(2)}) collective-permute-start(f32[6,128,128]{2,1,0:T(8,128)S(1)} %get-tuple-element.84), channel_id=1, source_target_pairs={{0,30},{2,4},{4,2},{6,8},{8,6},{10,12},{12,10},{14,16},{16,14},{18... | collective-permute-start | bytes 1179656 | tf_op jit(solution)/shard_map/ppermute | solution.py:143
  118.0 32.0 %collective-permute-start.14 = (f32[6,128,128]{2,1,0:T(8,128)S(1)}, f32[6,128,128]{2,1,0:T(8,128)S(1)}, u32[]{:S(2)}, u32[]{:S(2)}) collective-permute-start(f32[6,128,128]{2,1,0:T(8,128)S(1)} %get-tuple-element.81), channel_id=1, source_target_pairs={{0,30},{2,4},{4,2},{6,8},{8,6},{10,12},{12,10},{14,16},{16,14},{18... | collective-permute-start | bytes 1179656 | tf_op jit(solution)/shard_map/ppermute | solution.py:143
  119.7 30.7 %collective-permute-start.10 = (f32[6,128,128]{2,1,0:T(8,128)S(1)}, f32[6,128,128]{2,1,0:T(8,128)S(1)}, u32[]{:S(2)}, u32[]{:S(2)}) collective-permute-start(f32[6,128,128]{2,1,0:T(8,128)S(1)} %get-tuple-element.77), channel_id=1, source_target_pairs={{0,30},{2,4},{4,2},{6,8},{8,6},{10,12},{12,10},{14,16},{16,14},{18... | collective-permute-start | bytes 1179656 | tf_op jit(solution)/shard_map/ppermute | solution.py:143
  148.7 9.6 %collective-permute-start.19 = (f32[6,128,128]{2,1,0:T(8,128)S(1)}, f32[6,128,128]{2,1,0:T(8,128)S(1)}, u32[]{:S(2)}, u32[]{:S(2)}) collective-permute-start(f32[6,128,128]{2,1,0:T(8,128)S(1)} %get-tuple-element.88), channel_id=1, source_target_pairs={{0,30},{2,4},{4,2},{6,8},{8,6},{10,12},{12,10},{14,16},{16,14},{18... | collective-permute-start | bytes 1179656 | tf_op jit(solution)/shard_map/ppermute | solution.py:143
  150.0 21.7 %collective-permute-start.17 = (f32[6,128,128]{2,1,0:T(8,128)S(1)}, f32[6,128,128]{2,1,0:T(8,128)S(1)}, u32[]{:S(2)}, u32[]{:S(2)}) collective-permute-start(f32[6,128,128]{2,1,0:T(8,128)S(1)} %get-tuple-element.85), channel_id=1, source_target_pairs={{0,30},{2,4},{4,2},{6,8},{8,6},{10,12},{12,10},{14,16},{16,14},{18... | collective-permute-start | bytes 1179656 | tf_op jit(solution)/shard_map/ppermute | solution.py:143
  150.4 24.6 %collective-permute-start.15 = (f32[6,128,128]{2,1,0:T(8,128)S(1)}, f32[6,128,128]{2,1,0:T(8,128)S(1)}, u32[]{:S(2)}, u32[]{:S(2)}) collective-permute-start(f32[6,128,128]{2,1,0:T(8,128)S(1)} %get-tuple-element.82), channel_id=1, source_target_pairs={{0,30},{2,4},{4,2},{6,8},{8,6},{10,12},{12,10},{14,16},{16,14},{18... | collective-permute-start | bytes 1179656 | tf_op jit(solution)/shard_map/ppermute | solution.py:143
  152.4 26.0 %collective-permute-start.11 = (f32[6,128,128]{2,1,0:T(8,128)S(1)}, f32[6,128,128]{2,1,0:T(8,128)S(1)}, u32[]{:S(2)}, u32[]{:S(2)}) collective-permute-start(f32[6,128,128]{2,1,0:T(8,128)S(1)} %get-tuple-element.78), channel_id=1, source_target_pairs={{0,30},{2,4},{4,2},{6,8},{8,6},{10,12},{12,10},{14,16},{16,14},{18... | collective-permute-start | bytes 1179656 | tf_op jit(solution)/shard_map/ppermute | solution.py:143
  158.2 30.3 %collective-permute-start.30 = (f32[6,128,128]{2,1,0:T(8,128)S(1)}, f32[6,128,128]{2,1,0:T(8,128)S(1)}, u32[]{:S(2)}, u32[]{:S(2)}) collective-permute-start(f32[6,128,128]{2,1,0:T(8,128)S(1)} %get-tuple-element.118.rest_0_), channel_id=1, source_target_pairs={{0,30},{2,4},{4,2},{6,8},{8,6},{10,12},{12,10},{14,16},{16,14},{18... | collective-permute-start | bytes 1179656 | tf_op jit(solution)/shard_map/ppermute | solution.py:143
  183.0 20.1 %collective-permute-start.27 = (f32[6,128,128]{2,1,0:T(8,128)S(1)}, f32[6,128,128]{2,1,0:T(8,128)S(1)}, u32[]{:S(2)}, u32[]{:S(2)}) collective-permute-start(f32[6,128,128]{2,1,0:T(8,128)S(1)} %get-tuple-element.113.rest_0_), channel_id=1, source_target_pairs={{0,30},{2,4},{4,2},{6,8},{8,6},{10,12},{12,10},{14,16},{16,14},{18... | collective-permute-start | bytes 1179656 | tf_op jit(solution)/shard_map/ppermute | solution.py:143
  185.0 18.1 %collective-permute-start.35 = (f32[6,128,128]{2,1,0:T(8,128)S(1)}, f32[6,128,128]{2,1,0:T(8,128)S(1)}, u32[]{:S(2)}, u32[]{:S(2)}) collective-permute-start(f32[6,128,128]{2,1,0:T(8,128)S(1)} %get-tuple-element.123.rest_1_), channel_id=1, source_target_pairs={{0,2},{2,0},{4,6},{6,4},{8,10},{10,8},{12,14},{14,12},{16,18},{18,... | collective-permute-start | bytes 1179656 | tf_op jit(solution)/shard_map/ppermute | solution.py:146
  188.6 18.8 %collective-permute-start.24 = (f32[6,128,128]{2,1,0:T(8,128)S(1)}, f32[6,128,128]{2,1,0:T(8,128)S(1)}, u32[]{:S(2)}, u32[]{:S(2)}) collective-permute-start(f32[6,128,128]{2,1,0:T(8,128)S(1)} %get-tuple-element.108.rest_0_), channel_id=1, source_target_pairs={{0,30},{2,4},{4,2},{6,8},{8,6},{10,12},{12,10},{14,16},{16,14},{18... | collective-permute-start | bytes 1179656 | tf_op jit(solution)/shard_map/ppermute | solution.py:143
  188.6 18.8 %collective-permute-start.34 = (f32[6,128,128]{2,1,0:T(8,128)S(1)}, f32[6,128,128]{2,1,0:T(8,128)S(1)}, u32[]{:S(2)}, u32[]{:S(2)}) collective-permute-start(f32[6,128,128]{2,1,0:T(8,128)S(1)} %get-tuple-element.122.rest_1_), channel_id=1, source_target_pairs={{0,2},{2,0},{4,6},{6,4},{8,10},{10,8},{12,14},{14,12},{16,18},{18,... | collective-permute-start | bytes 1179656 | tf_op jit(solution)/shard_map/ppermute | solution.py:146
  188.7 22.9 %collective-permute-start.20 = (f32[6,128,128]{2,1,0:T(8,128)S(1)}, f32[6,128,128]{2,1,0:T(8,128)S(1)}, u32[]{:S(2)}, u32[]{:S(2)}) collective-permute-start(f32[6,128,128]{2,1,0:T(8,128)S(1)} %get-tuple-element.102.rest_0_), channel_id=1, source_target_pairs={{0,30},{2,4},{4,2},{6,8},{8,6},{10,12},{12,10},{14,16},{16,14},{18... | collective-permute-start | bytes 1179656 | tf_op jit(solution)/shard_map/ppermute | solution.py:143
  203.1 10.2 %collective-permute-start.33 = (f32[6,128,128]{2,1,0:T(8,128)S(1)}, f32[6,128,128]{2,1,0:T(8,128)S(1)}, u32[]{:S(2)}, u32[]{:S(2)}) collective-permute-start(f32[6,128,128]{2,1,0:T(8,128)S(1)} %get-tuple-element.121.rest_1_), channel_id=1, source_target_pairs={{0,2},{2,0},{4,6},{6,4},{8,10},{10,8},{12,14},{14,12},{16,18},{18,... | collective-permute-start | bytes 1179656 | tf_op jit(solution)/shard_map/ppermute | solution.py:146
  203.1 10.2 %collective-permute-start.32 = (f32[6,128,128]{2,1,0:T(8,128)S(1)}, f32[6,128,128]{2,1,0:T(8,128)S(1)}, u32[]{:S(2)}, u32[]{:S(2)}) collective-permute-start(f32[6,128,128]{2,1,0:T(8,128)S(1)} %get-tuple-element.120.rest_1_), channel_id=1, source_target_pairs={{0,2},{2,0},{4,6},{6,4},{8,10},{10,8},{12,14},{14,12},{16,18},{18,... | collective-permute-start | bytes 1179656 | tf_op jit(solution)/shard_map/ppermute | solution.py:146
  207.3 24.5 %collective-permute-start.31 = (f32[6,128,128]{2,1,0:T(8,128)S(1)}, f32[6,128,128]{2,1,0:T(8,128)S(1)}, u32[]{:S(2)}, u32[]{:S(2)}) collective-permute-start(f32[6,128,128]{2,1,0:T(8,128)S(1)} %get-tuple-element.119.rest_0_), channel_id=1, source_target_pairs={{0,30},{2,4},{4,2},{6,8},{8,6},{10,12},{12,10},{14,16},{16,14},{18... | collective-permute-start | bytes 1179656 | tf_op jit(solution)/shard_map/ppermute | solution.py:143
  211.6 38.5 %collective-permute-start.28 = (f32[6,128,128]{2,1,0:T(8,128)S(1)}, f32[6,128,128]{2,1,0:T(8,128)S(1)}, u32[]{:S(2)}, u32[]{:S(2)}) collective-permute-start(f32[6,128,128]{2,1,0:T(8,128)S(1)} %get-tuple-element.114.rest_0_), channel_id=1, source_target_pairs={{0,30},{2,4},{4,2},{6,8},{8,6},{10,12},{12,10},{14,16},{16,14},{18... | collective-permute-start | bytes 1179656 | tf_op jit(solution)/shard_map/ppermute | solution.py:143
  213.3 39.9 %collective-permute-start.26 = (f32[6,128,128]{2,1,0:T(8,128)S(1)}, f32[6,128,128]{2,1,0:T(8,128)S(1)}, u32[]{:S(2)}, u32[]{:S(2)}) collective-permute-start(f32[6,128,128]{2,1,0:T(8,128)S(1)} %get-tuple-element.110.rest_1_), channel_id=1, source_target_pairs={{0,2},{2,0},{4,6},{6,4},{8,10},{10,8},{12,14},{14,12},{16,18},{18,... | collective-permute-start | bytes 1179656 | tf_op jit(solution)/shard_map/ppermute | solution.py:146
  213.3 39.9 %collective-permute-start.25 = (f32[6,128,128]{2,1,0:T(8,128)S(1)}, f32[6,128,128]{2,1,0:T(8,128)S(1)}, u32[]{:S(2)}, u32[]{:S(2)}) collective-permute-start(f32[6,128,128]{2,1,0:T(8,128)S(1)} %get-tuple-element.109.rest_0_), channel_id=1, source_target_pairs={{0,30},{2,4},{4,2},{6,8},{8,6},{10,12},{12,10},{14,16},{16,14},{18... | collective-permute-start | bytes 1179656 | tf_op jit(solution)/shard_map/ppermute | solution.py:143
  213.4 43.0 %collective-permute-start.22 = (f32[6,128,128]{2,1,0:T(8,128)S(1)}, f32[6,128,128]{2,1,0:T(8,128)S(1)}, u32[]{:S(2)}, u32[]{:S(2)}) collective-permute-start(f32[6,128,128]{2,1,0:T(8,128)S(1)} %get-tuple-element.104.rest_1_), channel_id=1, source_target_pairs={{0,2},{2,0},{4,6},{6,4},{8,10},{10,8},{12,14},{14,12},{16,18},{18,... | collective-permute-start | bytes 1179656 | tf_op jit(solution)/shard_map/ppermute | solution.py:146
  231.9 24.5 %collective-permute-start.21 = (f32[6,128,128]{2,1,0:T(8,128)S(1)}, f32[6,128,128]{2,1,0:T(8,128)S(1)}, u32[]{:S(2)}, u32[]{:S(2)}) collective-permute-start(f32[6,128,128]{2,1,0:T(8,128)S(1)} %get-tuple-element.103.rest_0_), channel_id=1, source_target_pairs={{0,30},{2,4},{4,2},{6,8},{8,6},{10,12},{12,10},{14,16},{16,14},{18... | collective-permute-start | bytes 1179656 | tf_op jit(solution)/shard_map/ppermute | solution.py:143
  (12 other events, 632.6 us)

commit v2 on v1

v2 whole, which is shorter than its diff:
```python
import functools
import math

import jax
import jax.numpy as jnp
from jax import lax
from jax.experimental import pallas as pl
from jax.experimental.pallas import tpu as pltpu
from jax.sharding import PartitionSpec as P

couple_scale = 2.0
PIECES = 8
IN_FLIGHT = 3
STEP_ORDERS = 3
WORK = 30
BYTES = 120
BACK = 6
NEAR_SHARE = 1
NEAR_LAG = 2
FIRST = True
BACK_SHARE = 8
BACK_LAG = 0
AHEAD = 4


def pieces_of(orders):
    count = min(PIECES, orders)
    while orders % count:
        count -= 1
    return count, orders // count


def inner_pairs(count):
    return [(i, i ^ 1) for i in range(count)]


def outer_pairs(count):
    return [(i, (i + 1) % count if i % 2 else (i - 1) % count) for i in range(count)]


def order_sum(values):
    count = lax.axis_size("ord")
    if count & (count - 1):
        return lax.psum(values, "ord")
    step = 1
    while step < count:
        values = values + lax.ppermute(values, "ord", [(i, i ^ step) for i in range(count)])
        step *= 2
    return values


def in_plane(plane):
    rows, columns = plane.shape
    return (
        pltpu.roll(plane, 1, 0)
        + pltpu.roll(plane, rows - 1, 0)
        + pltpu.roll(plane, 1, 1)
        + pltpu.roll(plane, columns - 1, 1)
    )


def place(odd, position, planes):
    return position + odd * (planes - 1 - 2 * position)


def middle_kernel(base, planes, coupling, fresh, odd_ref, rate_ref, stiff_ref, field, adjoint, far, near, squares, *rest):
    if fresh:
        middle, sums = rest
    else:
        sums_before, middle, sums = rest
    step = pl.program_id(0)
    block = field.shape[0]
    odd = odd_ref[0]

    @pl.when(step == 0)
    def _():
        sums[...] = jnp.zeros_like(sums) if fresh else sums_before[...]

    for position in range(planes):
        z = place(odd, position, planes)
        squared, coupled = sums[0, z], sums[1, z]
        scaled_squares = (2.0 * coupling) * squares[z]
        for p in range(block):
            rate = rate_ref[base + step * block + p]
            stiff = rate * stiff_ref[base + step * block + p]
            centre = field[p, z]
            before = far[p] if position == 0 else field[p, place(odd, position - 1, planes)]
            after = near[p] if position == planes - 1 else field[p, place(odd, position + 1, planes)]
            around = in_plane(centre) + (before + after)
            factor = (1.0 + rate - 6.0 * stiff) - rate * (
                scaled_squares + (1.0 - 2.0 * coupling) * (centre * centre)
            )
            value = centre * factor + stiff * around
            middle[p, z] = value
            squared = squared + value * value
            coupled = coupled + value * (rate * adjoint[p, z])
        sums[0, z] = squared
        sums[1, z] = coupled


def pulled_back(rate, stiff, coupling, value, adjoint, around, squares, coupled):
    factor = (1.0 + rate - 6.0 * stiff) - rate * (squares + (3.0 - 6.0 * coupling) * (value * value))
    return adjoint * factor - value * coupled + stiff * around


def adjoint_kernel(base, planes, coupling, fresh, odd_ref, rate_ref, stiff_ref, field, middle, adjoint, far, near, sums, *rest):
    if fresh:
        outs, coupled = rest[-planes - 1:-1], rest[-1]
    else:
        coupled_before, outs, coupled = rest[0], rest[-planes - 1:-1], rest[-1]
    step = pl.program_id(0)
    block = field.shape[0]
    odd = odd_ref[0]

    @pl.when(step == 0)
    def _():
        coupled[...] = jnp.zeros_like(coupled) if fresh else coupled_before[...]

    for position in range(planes):
        z = place(odd, position, planes)
        total = coupled[z]
        squares, pull = (2.0 * coupling) * sums[0, z], (4.0 * coupling) * sums[1, z]
        for p in range(block):
            rate = rate_ref[base + step * block + p]
            stiff = rate * stiff_ref[base + step * block + p]
            centre = adjoint[p, z]
            before = far[p] if position == 0 else adjoint[p, place(odd, position - 1, planes)]
            after = near[p] if position == planes - 1 else adjoint[p, place(odd, position + 1, planes)]
            around = in_plane(centre) + (before + after)
            value = pulled_back(rate, stiff, coupling, middle[p, z], centre, around, squares, pull)
            outs[position][p] = value
            total = total + field[p, z] * (rate * value)
        coupled[z] = total


def last_kernel(base, planes, coupling, fresh, odd_ref, rate_ref, stiff_ref, field, far, near, squares, coupled, *rest):
    adjoint = rest[:planes]
    out, token = rest[-2:]
    token[...] = jnp.zeros_like(token)
    step = pl.program_id(0)
    block = field.shape[0]
    odd = odd_ref[0]
    for position in range(planes):
        z = place(odd, position, planes)
        scaled, pull = (2.0 * coupling) * squares[z], (4.0 * coupling) * coupled[z]
        for p in range(block):
            rate = rate_ref[base + step * block + p]
            stiff = rate * stiff_ref[base + step * block + p]
            centre = adjoint[position][p]
            before = far[p] if position == 0 else adjoint[position - 1][p]
            after = near[p] if position == planes - 1 else adjoint[position + 1][p]
            around = in_plane(centre) + (before + after)
            out[p, z] = pulled_back(rate, stiff, coupling, field[p, z], centre, around, scaled, pull)


def on_device(initial, cotangent, mobility, stiffness):
    orders, planes, rows, columns = initial.shape
    coupling = couple_scale / (orders * lax.axis_size("ord"))
    count, size = pieces_of(orders)
    block = math.gcd(size, STEP_ORDERS)
    ring = lax.axis_size("gz")
    odd = lax.rem(lax.axis_index("gz"), 2)
    odd_arr = odd.reshape(1).astype(jnp.int32)
    far_plane = odd * (planes - 1)
    near_plane = (planes - 1) - far_plane

    def send_far(plane):
        return lax.ppermute(plane, "gz", outer_pairs(ring))

    def send_near(plane):
        return lax.ppermute(plane, "gz", inner_pairs(ring))

    def cut(array, plane, start, length):
        return lax.dynamic_slice(array, (start, plane, 0, 0), (length, 1, rows, columns)).reshape(length, rows, columns)

    def after(value, *before):
        return lax.optimization_barrier((value, before))[0] if before else value

    scalar = pl.BlockSpec(memory_space=pltpu.SMEM)
    anywhere = pl.BlockSpec(memory_space=pl.ANY)
    one_slab = (block, planes, rows, columns)
    one_plane = (block, rows, columns)

    def shape(*dims):
        return jax.ShapeDtypeStruct(dims, jnp.float32)

    slab = shape(size, planes, rows, columns)
    plane_out = shape(size, rows, columns)
    cell = shape(planes, rows, columns)
    cells = shape(2, planes, rows, columns)
    cell_spec = pl.BlockSpec(cell.shape, lambda i: (0, 0, 0))
    cells_spec = pl.BlockSpec(cells.shape, lambda i: (0, 0, 0, 0))

    def slab_at(base):
        return pl.BlockSpec(one_slab, lambda i: (base // block + i, 0, 0, 0))

    def plane_at(base):
        return pl.BlockSpec(one_plane, lambda i: (base // block + i, 0, 0))

    def call(kernel, piece, fresh, in_specs, args, out_specs, out_shape, alias):
        elements = size * planes * rows * columns
        return pl.pallas_call(
            functools.partial(kernel, piece * size, planes, coupling, fresh),
            grid=(size // block,),
            in_specs=[scalar] * 3 + in_specs,
            out_specs=out_specs,
            out_shape=out_shape,
            input_output_aliases=alias,
            cost_estimate=pl.CostEstimate(flops=WORK * elements, bytes_accessed=BYTES * elements, transcendentals=0),
            compiler_params=pltpu.CompilerParams(
                dimension_semantics=("arbitrary",), vmem_limit_bytes=32 * 1024 * 1024
            ),
        )(odd_arr, mobility, stiffness, *args)

    far, sums_at = [], []

    def field_piece(index):
        array = initial if index < count else cotangent
        return cut(array, far_plane, (index % count) * size, size)

    def start_until(limit):
        while len(far) < min(limit, 2 * count):
            index = len(far)
            piece = field_piece(index) if index else first
            before = []
            if index >= IN_FLIGHT:
                before.append(far[index - IN_FLIGHT])
            if index > IN_FLIGHT and len(sums_at) > index - IN_FLIGHT - 1:
                before.append(sums_at[index - IN_FLIGHT - 1])
            far.append(send_far(after(piece, *before)))

    first = cut(initial, far_plane, 0, size)
    squares_first = order_sum(jnp.sum(initial * initial, 0))
    near_share = NEAR_SHARE if count % NEAR_SHARE == 0 else 1
    near = []

    def near_until(index):
        while len(near) * near_share <= index:
            piece = len(near) * near_share
            array = initial if piece < count else cotangent
            plane = cut(array, near_plane, (piece % count) * size, near_share * size)
            before = [far[piece - NEAR_LAG]] if piece >= NEAR_LAG else ([first] if FIRST else [])
            near.append(send_near(after(plane, *before)))

    start_until(IN_FLIGHT)

    middle, sums = [], None
    for k in range(count):
        start_until(IN_FLIGHT + k)
        near_until(k)
        fresh = k == 0
        value, sums = call(
            middle_kernel, k, fresh,
            [slab_at(k * size), slab_at(k * size), plane_at(0), plane_at((k % near_share) * size), cell_spec]
            + ([] if fresh else [cells_spec]),
            [initial, cotangent, far[k], near[k // near_share], squares_first] + ([] if fresh else [sums]),
            [slab_at(0), cells_spec], [slab, cells], {} if fresh else {8: 1},
        )
        middle.append(value)
        sums_at.append(sums)
    start_until(2 * count)
    near_until(2 * count - 1)
    sums = order_sum(sums)

    outs, coupled, held = [], None, None
    back, back_near, helds = [], [], []
    share = BACK_SHARE if count % BACK_SHARE == 0 else 1
    for k in range(count):
        fresh, inside = k == 0, (k % share) * size
        specs = [slab_at(k * size), slab_at(0), slab_at(k * size), plane_at(0), plane_at((k % near_share) * size), cells_spec]
        args = [initial, middle[k], cotangent, far[count + k], near[(count + k) // near_share], sums]
        if BACK and k >= BACK and k - BACK < len(back):
            args[1] = after(middle[k], back[k - BACK])
        alias = {}
        if not fresh:
            specs, args = specs + [cell_spec], args + [coupled]
            alias[3 + len(args) - 1] = planes
        if k % share:
            for position in range(1, planes):
                specs, args = specs + [anywhere], args + [held[position - 1]]
                alias[3 + len(args) - 1] = position
        outer, *held, coupled = call(
            adjoint_kernel, k, fresh, specs, args,
            [plane_at(0)] + [plane_at(inside)] * (planes - 1) + [cell_spec],
            [plane_out] + [shape(share * size, rows, columns)] * (planes - 1) + [cell], alias,
        )
        outs.append(outer)
        if k <= AHEAD:
            back.append(send_far(outer))
        if (k + 1) % share == 0:
            plane = held[-1]
            if BACK_LAG and k >= BACK_LAG:
                plane = after(plane, back[min(k - BACK_LAG, len(back) - 1)])
            back_near.append(send_near(plane))
            helds.append(held)
    coupled = order_sum(coupled)

    result = None
    for k in range(count):
        fresh, inside = k == 0, (k % share) * size
        result, token = call(
            last_kernel, k, fresh,
            [slab_at(k * size), plane_at(0), plane_at(inside), cell_spec, cell_spec, plane_at(0)]
            + [plane_at(inside)] * (planes - 1) + ([] if fresh else [anywhere]),
            [initial, back[k], back_near[k // share], squares_first, coupled, outs[k]] + helds[k // share]
            + ([] if fresh else [result]),
            [slab_at(k * size), pl.BlockSpec((8, 128), lambda i: (0, 0))],
            [shape(*initial.shape), shape(8, 128)], {} if fresh else {8 + planes: 0},
        )
        if len(back) < count:
            back.append(send_far(after(outs[len(back)], back[k + 1], token)))
    return result


def solution(mesh):
    return jax.shard_map(
        on_device,
        mesh=mesh,
        in_specs=(P("ord", "gz", None, None), P("ord", "gz", None, None), P("ord"), P("ord")),
        out_specs=P("ord", "gz", None, None),
        check_vma=False,
    )
```

time: 262 us -> 216 us (0.82); the launches traced: 260 us -> 216 us
  Pallas kernels: 78.6 us -> 37.6 us
  waiting for transfers between devices: 110 us -> 120 us
  local copies, waits for them, and re-layouts: 8.9 us -> 4.11 us
  starting transfers between devices: 57.9 us -> 53.5 us
  other arithmetic: 3.54 us -> 0.65 us
    pallas_call x24, Pallas kernels: 78.6 us -> 37.6 us  [call(): pl.pallas_call(functools.partial(kernel, piece * size, planes, coupling,...]
    ppermute x24, waiting for transfers between devices: 107 us -> 120 us  [send_far(): return lax.ppermute(plane, 'gz', outer_pairs(ring))]
    reshape x4 -> x2, local copies, waits for them, and re-layouts: 8.41 us -> 4.09 us  [cut(): lax.dynamic_slice(array, (start, plane, 0, 0), (length, 1, rows, columns))]
    ppermute x3, waiting for transfers between devices: 3.28 us -> 0.01 us  [order_sum(): lax.ppermute(values, 'ord', [(i, i ^ step) for i in range(count)])]
    ppermute x24, starting transfers between devices: 36.8 us -> 33.8 us  [send_far(): return lax.ppermute(plane, 'gz', outer_pairs(ring))]
    reduce_sum x1, other arithmetic: 3.48 us -> 0.57 us  [on_device(): squares_first = order_sum(jnp.sum(initial * initial, 0))]
    ppermute x10 -> x17, starting transfers between devices: 16.1 us -> 15.9 us  [send_near(): return lax.ppermute(plane, 'gz', inner_pairs(ring))]
  transfers between devices with their start and end apart: 37 -> 44, of which waited for: 14 -> 19; matrix products, arithmetic and copies ran while one was open for 3% -> 1% of each run, Pallas kernels for 29% -> 16%
where the time goes in v2:
time: 216 us
  waiting for transfers between devices  120 us (56%)
  starting transfers between devices  53.5 us (25%)
  Pallas kernels  37.6 us (17%)
  local copies, waits for them, and re-layouts  4.11 us (2%)
    ppermute x24, waiting for transfers between devices, send_far(): return lax.ppermute(plane, 'gz', outer_pairs(ring))  120 us
    pallas_call x24, Pallas kernels, call(): pl.pallas_call(functools.partial(kernel, piece * size, planes, coupling,...  37.6 us
    ppermute x24, starting transfers between devices, send_far(): return lax.ppermute(plane, 'gz', outer_pairs(ring))  33.8 us
    ppermute x17, starting transfers between devices, send_near(): return lax.ppermute(plane, 'gz', inner_pairs(ring))  15.9 us
  transfers between devices with their start and end apart: 44, of which 19 were waited for; matrix products, arithmetic and copies ran while one was open for 1% of the time, Pallas kernels for 16%

profile of v2, /device:TPU:1, one launch (start us, length us, event | category | flops | bytes accessed | tf_op | source)
XLA Modules:
  0.0 216.3 jit_solution(125618572032273116)
XLA Ops:
  0.0 3.6 %dynamic-slice_bitcast_fusion.16 = (f32[6,128,128]{2,1,0:T(8,128)S(1)}, f32[6,128,128]{2,1,0:T(8,128)S(1)}, f32[6,128,128]{2,1,0:T(8,128)S(1)}, f32[6,128,128]{2...) fusion(f32[48,2,128,128]{3,2,1,0:T(8,128)} %field.47, ...), kind=kLoop, calls=%fused_computation.17 | loop fusion | bytes 12582920 | tf_op jit(solution)/shard_map/reshape | solution.py:174
  3.7 2.7 %collective-permute-start.1 = (f32[6,128,128]{2,1,0:T(8,128)S(1)}, f32[6,128,128]{2,1,0:T(8,128)S(1)}, u32[]{:S(2)}, u32[]{:S(2)}) collective-permute-start(f32[6,128,128]{2,1,0:T(8,128)S(1)} %get-tuple-element.197), channel_id=1, source_target_pairs={{0,30},{2,4},{4,2},{6,8},{8,6},{10,12},{12,10},{14,16},{16,14},{18... | collective-permute-start | bytes 1179656 | tf_op jit(solution)/shard_map/ppermute | solution.py:168
  8.2 3.2 %collective-permute-start.2 = (f32[6,128,128]{2,1,0:T(8,128)S(1)}, f32[6,128,128]{2,1,0:T(8,128)S(1)}, u32[]{:S(2)}, u32[]{:S(2)}) collective-permute-start(f32[6,128,128]{2,1,0:T(8,128)S(1)} %get-tuple-element.87), channel_id=1, source_target_pairs={{0,2},{2,0},{4,6},{6,4},{8,10},{10,8},{12,14},{14,12},{16,18},{18,... | collective-permute-start | bytes 1179656 | tf_op jit(solution)/shard_map/ppermute | solution.py:171
  13.1 14.8 %collective-permute-done.1.far = f32[6,128,128]{2,1,0:T(8,128)S(1)} collective-permute-done((f32[6,128,128]{2,1,0:T(8,128)S(1)}, f32[6,128,128]{2,1,0:T(8,128)S(1)}, u32[]{:S(2)}, u32[]{:S(2)}) %collective-permute-start.1) | collective-permute-done | bytes 393248 | tf_op jit(solution)/shard_map/ppermute | solution.py:168
  27.9 2.5 %collective-permute-start.7 = (f32[6,128,128]{2,1,0:T(8,128)S(1)}, f32[6,128,128]{2,1,0:T(8,128)S(1)}, u32[]{:S(2)}, u32[]{:S(2)}) collective-permute-start(f32[6,128,128]{2,1,0:T(8,128)S(1)} %get-tuple-element.193), channel_id=1, source_target_pairs={{0,30},{2,4},{4,2},{6,8},{8,6},{10,12},{12,10},{14,16},{16,14},{18... | collective-permute-start | bytes 1179656 | tf_op jit(solution)/shard_map/ppermute | solution.py:168
  36.9 7.9 %collective-permute-done.7.far = f32[6,128,128]{2,1,0:T(8,128)S(1)} collective-permute-done((f32[6,128,128]{2,1,0:T(8,128)S(1)}, f32[6,128,128]{2,1,0:T(8,128)S(1)}, u32[]{:S(2)}, u32[]{:S(2)}) %collective-permute-start.7) | collective-permute-done | bytes 393248 | tf_op jit(solution)/shard_map/ppermute | solution.py:168
  44.7 2.5 %collective-permute-start.11 = (f32[6,128,128]{2,1,0:T(8,128)S(1)}, f32[6,128,128]{2,1,0:T(8,128)S(1)}, u32[]{:S(2)}, u32[]{:S(2)}) collective-permute-start(f32[6,128,128]{2,1,0:T(8,128)S(1)} %get-tuple-element.98), channel_id=1, source_target_pairs={{0,30},{2,4},{4,2},{6,8},{8,6},{10,12},{12,10},{14,16},{16,14},{18... | collective-permute-start | bytes 1179656 | tf_op jit(solution)/shard_map/ppermute | solution.py:168
  47.2 2.5 %collective-permute-done.5.far = f32[6,128,128]{2,1,0:T(8,128)S(1)} collective-permute-done((f32[6,128,128]{2,1,0:T(8,128)S(1)}, f32[6,128,128]{2,1,0:T(8,128)S(1)}, u32[]{:S(2)}, u32[]{:S(2)}) %collective-permute-start.5) | collective-permute-done | bytes 393248 | tf_op jit(solution)/shard_map/ppermute | solution.py:168
  51.6 2.3 %collective-permute-done.4.far = f32[6,128,128]{2,1,0:T(8,128)S(1)} collective-permute-done((f32[6,128,128]{2,1,0:T(8,128)S(1)}, f32[6,128,128]{2,1,0:T(8,128)S(1)}, u32[]{:S(2)}, u32[]{:S(2)}) %collective-permute-start.4) | collective-permute-done | bytes 393248 | tf_op jit(solution)/shard_map/ppermute | solution.py:168
  57.8 8.0 %collective-permute-done.11.far = f32[6,128,128]{2,1,0:T(8,128)S(1)} collective-permute-done((f32[6,128,128]{2,1,0:T(8,128)S(1)}, f32[6,128,128]{2,1,0:T(8,128)S(1)}, u32[]{:S(2)}, u32[]{:S(2)}) %collective-permute-start.11) | collective-permute-done | bytes 393248 | tf_op jit(solution)/shard_map/ppermute | solution.py:168
  65.8 2.5 %collective-permute-start.10 = (f32[6,128,128]{2,1,0:T(8,128)S(1)}, f32[6,128,128]{2,1,0:T(8,128)S(1)}, u32[]{:S(2)}, u32[]{:S(2)}) collective-permute-start(f32[6,128,128]{2,1,0:T(8,128)S(1)} %get-tuple-element.97), channel_id=1, source_target_pairs={{0,30},{2,4},{4,2},{6,8},{8,6},{10,12},{12,10},{14,16},{16,14},{18... | collective-permute-start | bytes 1179656 | tf_op jit(solution)/shard_map/ppermute | solution.py:168
  74.8 12.1 %collective-permute-done.10.far = f32[6,128,128]{2,1,0:T(8,128)S(1)} collective-permute-done((f32[6,128,128]{2,1,0:T(8,128)S(1)}, f32[6,128,128]{2,1,0:T(8,128)S(1)}, u32[]{:S(2)}, u32[]{:S(2)}) %collective-permute-start.10) | collective-permute-done | bytes 393248 | tf_op jit(solution)/shard_map/ppermute | solution.py:168
  86.9 2.5 %collective-permute-start.25 = (f32[6,128,128]{2,1,0:T(8,128)S(1)}, f32[6,128,128]{2,1,0:T(8,128)S(1)}, u32[]{:S(2)}, u32[]{:S(2)}) collective-permute-start(f32[6,128,128]{2,1,0:T(8,128)S(1)} %get-tuple-element.121), channel_id=1, source_target_pairs={{0,30},{2,4},{4,2},{6,8},{8,6},{10,12},{12,10},{14,16},{16,14},{18... | collective-permute-start | bytes 1179656 | tf_op jit(solution)/shard_map/ppermute | solution.py:168
  92.6 3.5 %collective-permute-done.17.far = f32[6,128,128]{2,1,0:T(8,128)S(1)} collective-permute-done((f32[6,128,128]{2,1,0:T(8,128)S(1)}, f32[6,128,128]{2,1,0:T(8,128)S(1)}, u32[]{:S(2)}, u32[]{:S(2)}) %collective-permute-start.17) | collective-permute-done | bytes 393248 | tf_op jit(solution)/shard_map/ppermute | solution.py:168
  97.8 2.5 %collective-permute-done.25.far = f32[6,128,128]{2,1,0:T(8,128)S(1)} collective-permute-done((f32[6,128,128]{2,1,0:T(8,128)S(1)}, f32[6,128,128]{2,1,0:T(8,128)S(1)}, u32[]{:S(2)}, u32[]{:S(2)}) %collective-permute-start.25) | collective-permute-done | bytes 393248 | tf_op jit(solution)/shard_map/ppermute | solution.py:168
  103.5 6.0 %collective-permute-start.33 = (f32[6,128,128]{2,1,0:T(8,128)S(1)}, f32[6,128,128]{2,1,0:T(8,128)S(1)}, u32[]{:S(2)}, u32[]{:S(2)}) collective-permute-start(f32[6,128,128]{2,1,0:T(8,128)S(1)} %get-tuple-element.133), channel_id=1, source_target_pairs={{0,2},{2,0},{4,6},{6,4},{8,10},{10,8},{12,14},{14,12},{16,18},{18,... | collective-permute-start | bytes 1179656 | tf_op jit(solution)/shard_map/ppermute | solution.py:171
  110.8 14.0 %collective-permute-done.29.far = f32[6,128,128]{2,1,0:T(8,128)S(1)} collective-permute-done((f32[6,128,128]{2,1,0:T(8,128)S(1)}, f32[6,128,128]{2,1,0:T(8,128)S(1)}, u32[]{:S(2)}, u32[]{:S(2)}) %collective-permute-start.29) | collective-permute-done | bytes 393248 | tf_op jit(solution)/shard_map/ppermute | solution.py:168
  124.8 2.5 %collective-permute-start.28 = (f32[6,128,128]{2,1,0:T(8,128)S(1)}, f32[6,128,128]{2,1,0:T(8,128)S(1)}, u32[]{:S(2)}, u32[]{:S(2)}) collective-permute-start(f32[6,128,128]{2,1,0:T(8,128)S(1)} %get-tuple-element.125.rest_0_), channel_id=1, source_target_pairs={{0,30},{2,4},{4,2},{6,8},{8,6},{10,12},{12,10},{14,16},{16,14},{18... | collective-permute-start | bytes 1179656 | tf_op jit(solution)/shard_map/ppermute | solution.py:168
  127.3 2.4 %collective-permute-done.23.far = f32[6,128,128]{2,1,0:T(8,128)S(1)} collective-permute-done((f32[6,128,128]{2,1,0:T(8,128)S(1)}, f32[6,128,128]{2,1,0:T(8,128)S(1)}, u32[]{:S(2)}, u32[]{:S(2)}) %collective-permute-start.23) | collective-permute-done | bytes 393248 | tf_op jit(solution)/shard_map/ppermute | solution.py:168
  131.5 2.5 %collective-permute-done.26.far = f32[6,128,128]{2,1,0:T(8,128)S(1)} collective-permute-done((f32[6,128,128]{2,1,0:T(8,128)S(1)}, f32[6,128,128]{2,1,0:T(8,128)S(1)}, u32[]{:S(2)}, u32[]{:S(2)}) %collective-permute-start.26) | collective-permute-done | bytes 393248 | tf_op jit(solution)/shard_map/ppermute | solution.py:168
  135.0 7.3 %collective-permute-done.28.far = f32[6,128,128]{2,1,0:T(8,128)S(1)} collective-permute-done((f32[6,128,128]{2,1,0:T(8,128)S(1)}, f32[6,128,128]{2,1,0:T(8,128)S(1)}, u32[]{:S(2)}, u32[]{:S(2)}) %collective-permute-start.28) | collective-permute-done | bytes 393248 | tf_op jit(solution)/shard_map/ppermute | solution.py:168
  142.4 4.2 %collective-permute-done.22.far = f32[6,128,128]{2,1,0:T(8,128)S(1)} collective-permute-done((f32[6,128,128]{2,1,0:T(8,128)S(1)}, f32[6,128,128]{2,1,0:T(8,128)S(1)}, u32[]{:S(2)}, u32[]{:S(2)}) %collective-permute-start.22) | collective-permute-done | bytes 393248 | tf_op jit(solution)/shard_map/ppermute | solution.py:168
  156.4 2.9 %collective-permute-done.24.far = f32[6,128,128]{2,1,0:T(8,128)S(1)} collective-permute-done((f32[6,128,128]{2,1,0:T(8,128)S(1)}, f32[6,128,128]{2,1,0:T(8,128)S(1)}, u32[]{:S(2)}, u32[]{:S(2)}) %collective-permute-start.24) | collective-permute-done | bytes 393248 | tf_op jit(solution)/shard_map/ppermute | solution.py:168
  165.7 27.5 %collective-permute-done.40.far = f32[6,128,128]{2,1,0:T(8,128)S(1)} collective-permute-done((f32[6,128,128]{2,1,0:T(8,128)S(1)}, f32[6,128,128]{2,1,0:T(8,128)S(1)}, u32[]{:S(2)}, u32[]{:S(2)}) %collective-permute-start.40) | collective-permute-done | bytes 393248 | tf_op jit(solution)/shard_map/ppermute | solution.py:168
  194.9 2.5 %collective-permute-done.36.far = f32[6,128,128]{2,1,0:T(8,128)S(1)} collective-permute-done((f32[6,128,128]{2,1,0:T(8,128)S(1)}, f32[6,128,128]{2,1,0:T(8,128)S(1)}, u32[]{:S(2)}, u32[]{:S(2)}) %collective-permute-start.36) | collective-permute-done | bytes 393248 | tf_op jit(solution)/shard_map/ppermute | solution.py:168
  199.2 2.0 shard_map.62
  201.2 2.0 shard_map.63
  203.3 2.0 shard_map.64
  207.2 2.0 shard_map.66
  209.2 2.0 shard_map.67
  211.3 2.0 shard_map.68
  214.3 2.0 shard_map.69
  (97 shorter events, 57.3 us)
Async XLA Ops:
  3.7 24.2 %collective-permute-start.1 = (f32[6,128,128]{2,1,0:T(8,128)S(1)}, f32[6,128,128]{2,1,0:T(8,128)S(1)}, u32[]{:S(2)}, u32[]{:S(2)}) collective-permute-start(f32[6,128,128]{2,1,0:T(8,128)S(1)} %get-tuple-element.197), channel_id=1, source_target_pairs={{0,30},{2,4},{4,2},{6,8},{8,6},{10,12},{12,10},{14,16},{16,14},{18... | collective-permute-start | bytes 1179656 | tf_op jit(solution)/shard_map/ppermute | solution.py:168
  6.9 23.5 %collective-permute-start.3 = (f32[2,128,128]{2,1,0:T(8,128)S(1)}, f32[2,128,128]{2,1,0:T(8,128)S(1)}, u32[]{:S(2)}, u32[]{:S(2)}) collective-permute-start(f32[2,128,128]{2,1,0:T(8,128)S(1)} %multiply_reduce_fusion), channel_id=1, source_target_pairs={{0,1},{1,0},{2,3},{3,2},{4,5},{5,4},{6,7},{7,6},{8,9},{9,8},{10,11... | collective-permute-start | bytes 393224 | tf_op jit(solution)/shard_map/ppermute | solution.py:47
  8.2 22.2 %collective-permute-start.2 = (f32[6,128,128]{2,1,0:T(8,128)S(1)}, f32[6,128,128]{2,1,0:T(8,128)S(1)}, u32[]{:S(2)}, u32[]{:S(2)}) collective-permute-start(f32[6,128,128]{2,1,0:T(8,128)S(1)} %get-tuple-element.87), channel_id=1, source_target_pairs={{0,2},{2,0},{4,6},{6,4},{8,10},{10,8},{12,14},{14,12},{16,18},{18,... | collective-permute-start | bytes 1179656 | tf_op jit(solution)/shard_map/ppermute | solution.py:171
  11.3 21.5 %collective-permute-start = (f32[6,128,128]{2,1,0:T(8,128)S(1)}, f32[6,128,128]{2,1,0:T(8,128)S(1)}, u32[]{:S(2)}, u32[]{:S(2)}) collective-permute-start(f32[6,128,128]{2,1,0:T(8,128)S(1)} %get-tuple-element.198), channel_id=1, source_target_pairs={{0,30},{2,4},{4,2},{6,8},{8,6},{10,12},{12,10},{14,16},{16,14},{18... | collective-permute-start | bytes 1179656 | tf_op jit(solution)/shard_map/ppermute | solution.py:168
  11.3 23.2 %collective-permute-start.9 = (f32[6,128,128]{2,1,0:T(8,128)S(1)}, f32[6,128,128]{2,1,0:T(8,128)S(1)}, u32[]{:S(2)}, u32[]{:S(2)}) collective-permute-start(f32[6,128,128]{2,1,0:T(8,128)S(1)} %get-tuple-element.93), channel_id=1, source_target_pairs={{0,2},{2,0},{4,6},{6,4},{8,10},{10,8},{12,14},{14,12},{16,18},{18,... | collective-permute-start | bytes 1179656 | tf_op jit(solution)/shard_map/ppermute | solution.py:171
  30.4 19.3 %collective-permute-start.5 = (f32[6,128,128]{2,1,0:T(8,128)S(1)}, f32[6,128,128]{2,1,0:T(8,128)S(1)}, u32[]{:S(2)}, u32[]{:S(2)}) collective-permute-start(f32[6,128,128]{2,1,0:T(8,128)S(1)} %get-tuple-element.90), channel_id=1, source_target_pairs={{0,30},{2,4},{4,2},{6,8},{8,6},{10,12},{12,10},{14,16},{16,14},{18... | collective-permute-start | bytes 1179656 | tf_op jit(solution)/shard_map/ppermute | solution.py:168
  30.4 19.3 %collective-permute-start.8 = (f32[6,128,128]{2,1,0:T(8,128)S(1)}, f32[6,128,128]{2,1,0:T(8,128)S(1)}, u32[]{:S(2)}, u32[]{:S(2)}) collective-permute-start(f32[6,128,128]{2,1,0:T(8,128)S(1)} %get-tuple-element.92), channel_id=1, source_target_pairs={{0,2},{2,0},{4,6},{6,4},{8,10},{10,8},{12,14},{14,12},{16,18},{18,... | collective-permute-start | bytes 1179656 | tf_op jit(solution)/shard_map/ppermute | solution.py:171
  32.8 21.1 %collective-permute-start.4 = (f32[6,128,128]{2,1,0:T(8,128)S(1)}, f32[6,128,128]{2,1,0:T(8,128)S(1)}, u32[]{:S(2)}, u32[]{:S(2)}) collective-permute-start(f32[6,128,128]{2,1,0:T(8,128)S(1)} %get-tuple-element.89), channel_id=1, source_target_pairs={{0,30},{2,4},{4,2},{6,8},{8,6},{10,12},{12,10},{14,16},{16,14},{18... | collective-permute-start | bytes 1179656 | tf_op jit(solution)/shard_map/ppermute | solution.py:168
  34.6 21.1 %collective-permute-start.6 = (f32[6,128,128]{2,1,0:T(8,128)S(1)}, f32[6,128,128]{2,1,0:T(8,128)S(1)}, u32[]{:S(2)}, u32[]{:S(2)}) collective-permute-start(f32[6,128,128]{2,1,0:T(8,128)S(1)} %get-tuple-element.91), channel_id=1, source_target_pairs={{0,2},{2,0},{4,6},{6,4},{8,10},{10,8},{12,14},{14,12},{16,18},{18,... | collective-permute-start | bytes 1179656 | tf_op jit(solution)/shard_map/ppermute | solution.py:171
  44.7 21.1 %collective-permute-start.11 = (f32[6,128,128]{2,1,0:T(8,128)S(1)}, f32[6,128,128]{2,1,0:T(8,128)S(1)}, u32[]{:S(2)}, u32[]{:S(2)}) collective-permute-start(f32[6,128,128]{2,1,0:T(8,128)S(1)} %get-tuple-element.98), channel_id=1, source_target_pairs={{0,30},{2,4},{4,2},{6,8},{8,6},{10,12},{12,10},{14,16},{16,14},{18... | collective-permute-start | bytes 1179656 | tf_op jit(solution)/shard_map/ppermute | solution.py:168
  49.7 18.6 %collective-permute-start.16 = (f32[6,128,128]{2,1,0:T(8,128)S(1)}, f32[6,128,128]{2,1,0:T(8,128)S(1)}, u32[]{:S(2)}, u32[]{:S(2)}) collective-permute-start(f32[6,128,128]{2,1,0:T(8,128)S(1)} %get-tuple-element.103), channel_id=1, source_target_pairs={{0,2},{2,0},{4,6},{6,4},{8,10},{10,8},{12,14},{14,12},{16,18},{18,... | collective-permute-start | bytes 1179656 | tf_op jit(solution)/shard_map/ppermute | solution.py:171
  49.7 20.5 %collective-permute-start.15 = (f32[6,128,128]{2,1,0:T(8,128)S(1)}, f32[6,128,128]{2,1,0:T(8,128)S(1)}, u32[]{:S(2)}, u32[]{:S(2)}) collective-permute-start(f32[6,128,128]{2,1,0:T(8,128)S(1)} %get-tuple-element.102), channel_id=1, source_target_pairs={{0,2},{2,0},{4,6},{6,4},{8,10},{10,8},{12,14},{14,12},{16,18},{18,... | collective-permute-start | bytes 1179656 | tf_op jit(solution)/shard_map/ppermute | solution.py:171
  53.9 17.7 %collective-permute-start.13 = (f32[6,128,128]{2,1,0:T(8,128)S(1)}, f32[6,128,128]{2,1,0:T(8,128)S(1)}, u32[]{:S(2)}, u32[]{:S(2)}) collective-permute-start(f32[6,128,128]{2,1,0:T(8,128)S(1)} %get-tuple-element.100), channel_id=1, source_target_pairs={{0,30},{2,4},{4,2},{6,8},{8,6},{10,12},{12,10},{14,16},{16,14},{18... | collective-permute-start | bytes 1179656 | tf_op jit(solution)/shard_map/ppermute | solution.py:168
  55.7 17.8 %collective-permute-start.14 = (f32[6,128,128]{2,1,0:T(8,128)S(1)}, f32[6,128,128]{2,1,0:T(8,128)S(1)}, u32[]{:S(2)}, u32[]{:S(2)}) collective-permute-start(f32[6,128,128]{2,1,0:T(8,128)S(1)} %get-tuple-element.101), channel_id=1, source_target_pairs={{0,2},{2,0},{4,6},{6,4},{8,10},{10,8},{12,14},{14,12},{16,18},{18,... | collective-permute-start | bytes 1179656 | tf_op jit(solution)/shard_map/ppermute | solution.py:171
  65.8 21.1 %collective-permute-start.10 = (f32[6,128,128]{2,1,0:T(8,128)S(1)}, f32[6,128,128]{2,1,0:T(8,128)S(1)}, u32[]{:S(2)}, u32[]{:S(2)}) collective-permute-start(f32[6,128,128]{2,1,0:T(8,128)S(1)} %get-tuple-element.97), channel_id=1, source_target_pairs={{0,30},{2,4},{4,2},{6,8},{8,6},{10,12},{12,10},{14,16},{16,14},{18... | collective-permute-start | bytes 1179656 | tf_op jit(solution)/shard_map/ppermute | solution.py:168
  68.3 21.1 %collective-permute-start.12 = (f32[6,128,128]{2,1,0:T(8,128)S(1)}, f32[6,128,128]{2,1,0:T(8,128)S(1)}, u32[]{:S(2)}, u32[]{:S(2)}) collective-permute-start(f32[6,128,128]{2,1,0:T(8,128)S(1)} %get-tuple-element.99), channel_id=1, source_target_pairs={{0,2},{2,0},{4,6},{6,4},{8,10},{10,8},{12,14},{14,12},{16,18},{18,... | collective-permute-start | bytes 1179656 | tf_op jit(solution)/shard_map/ppermute | solution.py:171
  70.2 21.9 %collective-permute-start.20 = (f32[6,128,128]{2,1,0:T(8,128)S(1)}, f32[6,128,128]{2,1,0:T(8,128)S(1)}, u32[]{:S(2)}, u32[]{:S(2)}) collective-permute-start(f32[6,128,128]{2,1,0:T(8,128)S(1)} %get-tuple-element.113), channel_id=1, source_target_pairs={{0,30},{2,4},{4,2},{6,8},{8,6},{10,12},{12,10},{14,16},{16,14},{18... | collective-permute-start | bytes 1179656 | tf_op jit(solution)/shard_map/ppermute | solution.py:168
  71.7 24.4 %collective-permute-start.17 = (f32[6,128,128]{2,1,0:T(8,128)S(1)}, f32[6,128,128]{2,1,0:T(8,128)S(1)}, u32[]{:S(2)}, u32[]{:S(2)}) collective-permute-start(f32[6,128,128]{2,1,0:T(8,128)S(1)} %get-tuple-element.109), channel_id=1, source_target_pairs={{0,30},{2,4},{4,2},{6,8},{8,6},{10,12},{12,10},{14,16},{16,14},{18... | collective-permute-start | bytes 1179656 | tf_op jit(solution)/shard_map/ppermute | solution.py:168
  96.1 28.7 %collective-permute-start.29 = (f32[6,128,128]{2,1,0:T(8,128)S(1)}, f32[6,128,128]{2,1,0:T(8,128)S(1)}, u32[]{:S(2)}, u32[]{:S(2)}) collective-permute-start(f32[6,128,128]{2,1,0:T(8,128)S(1)} %get-tuple-element.127), channel_id=1, source_target_pairs={{0,30},{2,4},{4,2},{6,8},{8,6},{10,12},{12,10},{14,16},{16,14},{18... | collective-permute-start | bytes 1179656 | tf_op jit(solution)/shard_map/ppermute | solution.py:168
  100.3 27.0 %collective-permute-start.34 = (f32[6,128,128]{2,1,0:T(8,128)S(1)}, f32[6,128,128]{2,1,0:T(8,128)S(1)}, u32[]{:S(2)}, u32[]{:S(2)}) collective-permute-start(f32[6,128,128]{2,1,0:T(8,128)S(1)} %get-tuple-element.135), channel_id=1, source_target_pairs={{0,2},{2,0},{4,6},{6,4},{8,10},{10,8},{12,14},{14,12},{16,18},{18,... | collective-permute-start | bytes 1179656 | tf_op jit(solution)/shard_map/ppermute | solution.py:171
  101.4 28.4 %collective-permute-start.23 = (f32[6,128,128]{2,1,0:T(8,128)S(1)}, f32[6,128,128]{2,1,0:T(8,128)S(1)}, u32[]{:S(2)}, u32[]{:S(2)}) collective-permute-start(f32[6,128,128]{2,1,0:T(8,128)S(1)} %get-tuple-element.119), channel_id=1, source_target_pairs={{0,30},{2,4},{4,2},{6,8},{8,6},{10,12},{12,10},{14,16},{16,14},{18... | collective-permute-start | bytes 1179656 | tf_op jit(solution)/shard_map/ppermute | solution.py:168
  103.5 26.3 %collective-permute-start.33 = (f32[6,128,128]{2,1,0:T(8,128)S(1)}, f32[6,128,128]{2,1,0:T(8,128)S(1)}, u32[]{:S(2)}, u32[]{:S(2)}) collective-permute-start(f32[6,128,128]{2,1,0:T(8,128)S(1)} %get-tuple-element.133), channel_id=1, source_target_pairs={{0,2},{2,0},{4,6},{6,4},{8,10},{10,8},{12,14},{14,12},{16,18},{18,... | collective-permute-start | bytes 1179656 | tf_op jit(solution)/shard_map/ppermute | solution.py:171
  109.4 24.5 %collective-permute-start.26 = (f32[6,128,128]{2,1,0:T(8,128)S(1)}, f32[6,128,128]{2,1,0:T(8,128)S(1)}, u32[]{:S(2)}, u32[]{:S(2)}) collective-permute-start(f32[6,128,128]{2,1,0:T(8,128)S(1)} %get-tuple-element.122), channel_id=1, source_target_pairs={{0,30},{2,4},{4,2},{6,8},{8,6},{10,12},{12,10},{14,16},{16,14},{18... | collective-permute-start | bytes 1179656 | tf_op jit(solution)/shard_map/ppermute | solution.py:168
  127.3 19.3 %collective-permute-start.22 = (f32[6,128,128]{2,1,0:T(8,128)S(1)}, f32[6,128,128]{2,1,0:T(8,128)S(1)}, u32[]{:S(2)}, u32[]{:S(2)}) collective-permute-start(f32[6,128,128]{2,1,0:T(8,128)S(1)} %get-tuple-element.117.rest_0_), channel_id=1, source_target_pairs={{0,30},{2,4},{4,2},{6,8},{8,6},{10,12},{12,10},{14,16},{16,14},{18... | collective-permute-start | bytes 1179656 | tf_op jit(solution)/shard_map/ppermute | solution.py:168
  129.8 22.6 %collective-permute-start.32 = (f32[6,128,128]{2,1,0:T(8,128)S(1)}, f32[6,128,128]{2,1,0:T(8,128)S(1)}, u32[]{:S(2)}, u32[]{:S(2)}) collective-permute-start(f32[6,128,128]{2,1,0:T(8,128)S(1)} %get-tuple-element.131), channel_id=1, source_target_pairs={{0,2},{2,0},{4,6},{6,4},{8,10},{10,8},{12,14},{14,12},{16,18},{18,... | collective-permute-start | bytes 1179656 | tf_op jit(solution)/shard_map/ppermute | solution.py:171
  129.8 25.3 %collective-permute-start.30 = (f32[6,128,128]{2,1,0:T(8,128)S(1)}, f32[6,128,128]{2,1,0:T(8,128)S(1)}, u32[]{:S(2)}, u32[]{:S(2)}) collective-permute-start(f32[6,128,128]{2,1,0:T(8,128)S(1)} %get-tuple-element.128), channel_id=1, source_target_pairs={{0,30},{2,4},{4,2},{6,8},{8,6},{10,12},{12,10},{14,16},{16,14},{18... | collective-permute-start | bytes 1179656 | tf_op jit(solution)/shard_map/ppermute | solution.py:168
  134.0 21.1 %collective-permute-start.31 = (f32[6,128,128]{2,1,0:T(8,128)S(1)}, f32[6,128,128]{2,1,0:T(8,128)S(1)}, u32[]{:S(2)}, u32[]{:S(2)}) collective-permute-start(f32[6,128,128]{2,1,0:T(8,128)S(1)} %get-tuple-element.129), channel_id=1, source_target_pairs={{0,2},{2,0},{4,6},{6,4},{8,10},{10,8},{12,14},{14,12},{16,18},{18,... | collective-permute-start | bytes 1179656 | tf_op jit(solution)/shard_map/ppermute | solution.py:171
  160.6 38.6 %collective-permute-start.38 = (f32[48,128,128]{2,1,0:T(8,128)S(1)}, f32[48,128,128]{2,1,0:T(8,128)S(1)}, u32[]{:S(2)}, u32[]{:S(2)}) collective-permute-start(f32[48,128,128]{2,1,0:T(8,128)S(1)} %get-tuple-element.153.rest_1_), channel_id=1, source_target_pairs={{0,2},{2,0},{4,6},{6,4},{8,10},{10,8},{12,14},{14,12},{16,18},{18,... | collective-permute-start | bytes 9437192 | tf_op jit(solution)/shard_map/ppermute | solution.py:171
  160.7 32.5 %collective-permute-start.40 = (f32[6,128,128]{2,1,0:T(8,128)S(1)}, f32[6,128,128]{2,1,0:T(8,128)S(1)}, u32[]{:S(2)}, u32[]{:S(2)}) collective-permute-start(f32[6,128,128]{2,1,0:T(8,128)S(1)} %get-tuple-element.156.rest_0_), channel_id=1, source_target_pairs={{0,30},{2,4},{4,2},{6,8},{8,6},{10,12},{12,10},{14,16},{16,14},{18... | collective-permute-start | bytes 1179656 | tf_op jit(solution)/shard_map/ppermute | solution.py:168
  162.5 35.0 %collective-permute-start.36 = (f32[6,128,128]{2,1,0:T(8,128)S(1)}, f32[6,128,128]{2,1,0:T(8,128)S(1)}, u32[]{:S(2)}, u32[]{:S(2)}) collective-permute-start(f32[6,128,128]{2,1,0:T(8,128)S(1)} %get-tuple-element.151.rest_0_), channel_id=1, source_target_pairs={{0,30},{2,4},{4,2},{6,8},{8,6},{10,12},{12,10},{14,16},{16,14},{18... | collective-permute-start | bytes 1179656 | tf_op jit(solution)/shard_map/ppermute | solution.py:168
  162.5 36.6 %collective-permute-start.39 = (f32[2,128,128]{2,1,0:T(8,128)S(1)}, f32[2,128,128]{2,1,0:T(8,128)S(1)}, u32[]{:S(2)}, u32[]{:S(2)}) collective-permute-start(f32[2,128,128]{2,1,0:T(8,128)S(1)} %get-tuple-element.154), channel_id=1, source_target_pairs={{0,1},{1,0},{2,3},{3,2},{4,5},{5,4},{6,7},{7,6},{8,9},{9,8},{10,11... | collective-permute-start | bytes 393224 | tf_op jit(solution)/shard_map/ppermute | solution.py:47
  163.8 43.4 %collective-permute-start.43 = (f32[6,128,128]{2,1,0:T(8,128)S(1)}, f32[6,128,128]{2,1,0:T(8,128)S(1)}, u32[]{:S(2)}, u32[]{:S(2)}) collective-permute-start(f32[6,128,128]{2,1,0:T(8,128)S(1)} %get-tuple-element.160.rest_0_), channel_id=1, source_target_pairs={{0,30},{2,4},{4,2},{6,8},{8,6},{10,12},{12,10},{14,16},{16,14},{18... | collective-permute-start | bytes 1179656 | tf_op jit(solution)/shard_map/ppermute | solution.py:168
  (17 other events, 280.1 us)

commit v3 on v2

--- a/solution.py
+++ b/solution.py
@@ -9,18 +9,20 @@
 from jax.sharding import PartitionSpec as P
 
 couple_scale = 2.0
-PIECES = 8
+PIECES = 6
 IN_FLIGHT = 3
-STEP_ORDERS = 3
+STEP_ORDERS = 4
 WORK = 30
-BYTES = 120
-BACK = 6
+BYTES = 20
+BACK = 0
 NEAR_SHARE = 1
-NEAR_LAG = 2
+NEAR_LAG = 16
 FIRST = True
-BACK_SHARE = 8
-BACK_LAG = 0
+BACK_GROUPS = (1, 1, 1, 1, 1, 1)
 AHEAD = 4
+CARRY = True
+EARLY = True
+FAR_FIRST = 2
 
 
 def pieces_of(orders):
@@ -103,60 +105,74 @@
     return adjoint * factor - value * coupled + stiff * around
 
 
-def adjoint_kernel(base, planes, coupling, fresh, odd_ref, rate_ref, stiff_ref, field, middle, adjoint, far, near, sums, *rest):
-    if fresh:
-        outs, coupled = rest[-planes - 1:-1], rest[-1]
-    else:
-        coupled_before, outs, coupled = rest[0], rest[-planes - 1:-1], rest[-1]
+def adjoint_kernel(base, planes, coupling, fresh, odd_ref, rate_ref, stiff_ref, field, middle, adjoint, far, near, squares, sums, *rest):
+    outer, inner, own, coupled = rest[-4:]
     step = pl.program_id(0)
     block = field.shape[0]
     odd = odd_ref[0]
 
     @pl.when(step == 0)
     def _():
-        coupled[...] = jnp.zeros_like(coupled) if fresh else coupled_before[...]
-
-    for position in range(planes):
-        z = place(odd, position, planes)
-        total = coupled[z]
-        squares, pull = (2.0 * coupling) * sums[0, z], (4.0 * coupling) * sums[1, z]
-        for p in range(block):
-            rate = rate_ref[base + step * block + p]
-            stiff = rate * stiff_ref[base + step * block + p]
+        coupled[...] = jnp.zeros_like(coupled) if fresh else rest[0][...]
+
+    zs = [place(odd, position, planes) for position in range(planes)]
+    totals = [coupled[z] for z in zs]
+    for p in range(block):
+        rate = rate_ref[base + step * block + p]
+        stiff = rate * stiff_ref[base + step * block + p]
+        values = []
+        for position, z in enumerate(zs):
             centre = adjoint[p, z]
-            before = far[p] if position == 0 else adjoint[p, place(odd, position - 1, planes)]
-            after = near[p] if position == planes - 1 else adjoint[p, place(odd, position + 1, planes)]
+            before = far[p] if position == 0 else adjoint[p, zs[position - 1]]
+            after = near[p] if position == planes - 1 else adjoint[p, zs[position + 1]]
             around = in_plane(centre) + (before + after)
-            value = pulled_back(rate, stiff, coupling, middle[p, z], centre, around, squares, pull)
-            outs[position][p] = value
-            total = total + field[p, z] * (rate * value)
-        coupled[z] = total
-
-
-def last_kernel(base, planes, coupling, fresh, odd_ref, rate_ref, stiff_ref, field, far, near, squares, coupled, *rest):
-    adjoint = rest[:planes]
-    out, token = rest[-2:]
-    token[...] = jnp.zeros_like(token)
+            value = pulled_back(
+                rate, stiff, coupling, middle[p, z], centre, around,
+                (2.0 * coupling) * sums[0, z], (4.0 * coupling) * sums[1, z],
+            )
+            values.append(value)
+            totals[position] = totals[position] + field[p, z] * (rate * value)
+        outer[p] = values[0]
+        inner[p] = values[-1]
+        for position, z in enumerate(zs):
+            around = in_plane(values[position])
+            if position > 0:
+                around = around + values[position - 1]
+            if position < planes - 1:
+                around = around + values[position + 1]
+            square = field[p, z] * field[p, z]
+            factor = (1.0 + rate - 6.0 * stiff) - rate * (
+                (2.0 * coupling) * squares[z] + (3.0 - 6.0 * coupling) * square
+            )
+            own[p, z] = values[position] * factor + stiff * around
+    for position, z in enumerate(zs):
+        coupled[z] = totals[position]
+
+
+def last_kernel(base, planes, coupling, fresh, odd_ref, rate_ref, stiff_ref, field, far, near, coupled, own, *rest):
+    out = rest[-1] if rest[-1].shape == field.shape else rest[-2]
     step = pl.program_id(0)
     block = field.shape[0]
     odd = odd_ref[0]
     for position in range(planes):
         z = place(odd, position, planes)
-        scaled, pull = (2.0 * coupling) * squares[z], (4.0 * coupling) * coupled[z]
+        pull = (4.0 * coupling) * coupled[z]
         for p in range(block):
             rate = rate_ref[base + step * block + p]
             stiff = rate * stiff_ref[base + step * block + p]
-            centre = adjoint[position][p]
-            before = far[p] if position == 0 else adjoint[position - 1][p]
-            after = near[p] if position == planes - 1 else adjoint[position + 1][p]
-            around = in_plane(centre) + (before + after)
-            out[p, z] = pulled_back(rate, stiff, coupling, field[p, z], centre, around, scaled, pull)
+            value = own[p, z] - field[p, z] * pull
+            if position == 0:
+                value = value + stiff * far[p]
+            if position == planes - 1:
+                value = value + stiff * near[p]
+            out[p, z] = value
 
 
 def on_device(initial, cotangent, mobility, stiffness):
     orders, planes, rows, columns = initial.shape
     coupling = couple_scale / (orders * lax.axis_size("ord"))
     count, size = pieces_of(orders)
+    joined = min(FAR_FIRST, count)
     block = math.gcd(size, STEP_ORDERS)
     ring = lax.axis_size("gz")
     odd = lax.rem(lax.axis_index("gz"), 2)
@@ -197,12 +213,12 @@
     def plane_at(base):
         return pl.BlockSpec(one_plane, lambda i: (base // block + i, 0, 0))
 
-    def call(kernel, piece, fresh, in_specs, args, out_specs, out_shape, alias):
+    def call(kernel, piece, fresh, in_specs, args, out_specs, out_shape, alias, tokens=()):
         elements = size * planes * rows * columns
         return pl.pallas_call(
             functools.partial(kernel, piece * size, planes, coupling, fresh),
             grid=(size // block,),
-            in_specs=[scalar] * 3 + in_specs,
+            in_specs=[scalar] * 3 + in_specs + [anywhere] * len(tokens),
             out_specs=out_specs,
             out_shape=out_shape,
             input_output_aliases=alias,
@@ -210,7 +226,7 @@
             compiler_params=pltpu.CompilerParams(
                 dimension_semantics=("arbitrary",), vmem_limit_bytes=32 * 1024 * 1024
             ),
-        )(odd_arr, mobility, stiffness, *args)
+        )(odd_arr, mobility, stiffness, *args, *tokens)
 
     far, sums_at = [], []
 
@@ -227,9 +243,10 @@
                 before.append(far[index - IN_FLIGHT])
             if index > IN_FLIGHT and len(sums_at) > index - IN_FLIGHT - 1:
                 before.append(sums_at[index - IN_FLIGHT - 1])
-            far.append(send_far(after(piece, *before)))
-
-    first = cut(initial, far_plane, 0, size)
+            sent = send_far(after(piece, *before))
+            far.extend([sent] * (joined if index == 0 else 1))
+
+    first = cut(initial, far_plane, 0, joined * size)
     squares_first = order_sum(jnp.sum(initial * initial, 0))
     near_share = NEAR_SHARE if count % NEAR_SHARE == 0 else 1
     near = []
@@ -243,6 +260,8 @@
             near.append(send_near(after(plane, *before)))
 
     start_until(IN_FLIGHT)
+    if EARLY:
+        near_until(2 * count - 1)
 
     middle, sums = [], None
     for k in range(count):
@@ -251,7 +270,8 @@
         fresh = k == 0
         value, sums = call(
             middle_kernel, k, fresh,
-            [slab_at(k * size), slab_at(k * size), plane_at(0), plane_at((k % near_share) * size), cell_spec]
+            [slab_at(k * size), slab_at(k * size), plane_at(k * size if k < joined else 0),
+             plane_at((k % near_share) * size), cell_spec]
             + ([] if fresh else [cells_spec]),
             [initial, cotangent, far[k], near[k // near_share], squares_first] + ([] if fresh else [sums]),
             [slab_at(0), cells_spec], [slab, cells], {} if fresh else {8: 1},
@@ -263,52 +283,57 @@
     sums = order_sum(sums)
 
     outs, coupled, held = [], None, None
-    back, back_near, helds = [], [], []
-    share = BACK_SHARE if count % BACK_SHARE == 0 else 1
+    back, back_near, owns = [], [], []
+    groups = BACK_GROUPS if sum(BACK_GROUPS) == count else (1,) * count
+    opens = [sum(groups[:g]) for g in range(len(groups))]
+    group_of = [g for g, members in enumerate(groups) for _ in range(members)]
     for k in range(count):
-        fresh, inside = k == 0, (k % share) * size
-        specs = [slab_at(k * size), slab_at(0), slab_at(k * size), plane_at(0), plane_at((k % near_share) * size), cells_spec]
-        args = [initial, middle[k], cotangent, far[count + k], near[(count + k) // near_share], sums]
+        fresh, group = k == 0, group_of[k]
+        inside = (k - opens[group]) * size
+        specs = [slab_at(k * size), slab_at(0), slab_at(k * size), plane_at(0), plane_at((k % near_share) * size), cell_spec, cells_spec]
+        args = [initial, middle[k], cotangent, far[count + k], near[(count + k) // near_share], squares_first, sums]
+        tokens = []
         if BACK and k >= BACK and k - BACK < len(back):
-            args[1] = after(middle[k], back[k - BACK])
+            tokens = [back[k - BACK]]
         alias = {}
         if not fresh:
             specs, args = specs + [cell_spec], args + [coupled]
-            alias[3 + len(args) - 1] = planes
-        if k % share:
-            for position in range(1, planes):
-                specs, args = specs + [anywhere], args + [held[position - 1]]
-                alias[3 + len(args) - 1] = position
-        outer, *held, coupled = call(
+            alias[3 + len(args) - 1] = 3
+        if k != opens[group]:
+            specs, args = specs + [anywhere], args + [held]
+            alias[3 + len(args) - 1] = 1
+        outer, held, own, coupled = call(
             adjoint_kernel, k, fresh, specs, args,
-            [plane_at(0)] + [plane_at(inside)] * (planes - 1) + [cell_spec],
-            [plane_out] + [shape(share * size, rows, columns)] * (planes - 1) + [cell], alias,
+            [plane_at(0), plane_at(inside), slab_at(0), cell_spec],
+            [plane_out, shape(groups[group] * size, rows, columns), slab, cell], alias, tokens,
         )
+        owns.append(own)
         outs.append(outer)
-        if k <= AHEAD:
+        if k <= AHEAD or not CARRY:
             back.append(send_far(outer))
-        if (k + 1) % share == 0:
-            plane = held[-1]
-            if BACK_LAG and k >= BACK_LAG:
-                plane = after(plane, back[min(k - BACK_LAG, len(back) - 1)])
+        if k + 1 == opens[group] + groups[group]:
+            plane = held
             back_near.append(send_near(plane))
-            helds.append(held)
     coupled = order_sum(coupled)
 
     result = None
     for k in range(count):
-        fresh, inside = k == 0, (k % share) * size
-        result, token = call(
-            last_kernel, k, fresh,
-            [slab_at(k * size), plane_at(0), plane_at(inside), cell_spec, cell_spec, plane_at(0)]
-            + [plane_at(inside)] * (planes - 1) + ([] if fresh else [anywhere]),
-            [initial, back[k], back_near[k // share], squares_first, coupled, outs[k]] + helds[k // share]
-            + ([] if fresh else [result]),
-            [slab_at(k * size), pl.BlockSpec((8, 128), lambda i: (0, 0))],
-            [shape(*initial.shape), shape(8, 128)], {} if fresh else {8 + planes: 0},
-        )
-        if len(back) < count:
-            back.append(send_far(after(outs[len(back)], back[k + 1], token)))
+        fresh, group = k == 0, group_of[k]
+        inside = (k - opens[group]) * size
+        later = len(back) if CARRY and len(back) < count else None
+        specs = [slab_at(k * size), plane_at(0), plane_at(inside), cell_spec, slab_at(0)]
+        args = [initial, back[k], back_near[group], coupled, owns[k]]
+        out_specs, out_shape, alias = [slab_at(k * size)], [shape(*initial.shape)], {}
+        if not fresh:
+            specs, args = specs + [anywhere], args + [result]
+            alias[3 + len(args) - 1] = 0
+        if later is not None:
+            specs, args = specs + [anywhere], args + [outs[later]]
+            out_specs, out_shape = out_specs + [anywhere], out_shape + [plane_out]
+            alias[3 + len(args) - 1] = 1
+        result, *handed = call(last_kernel, k, fresh, specs, args, out_specs, out_shape, alias)
+        if later is not None:
+            back.append(send_far(handed[0]))
     return result
 
 

time: 216 us -> 214 us (level)
  starting transfers between devices: 53.5 us -> 35.8 us
  waiting for transfers between devices: 120 us -> 132 us
  local copies, waits for them, and re-layouts: 4.11 us -> 11.9 us
  Pallas kernels: 37.6 us -> 33.6 us
    ppermute x24 -> x17, starting transfers between devices: 33.8 us -> 21 us  [send_far(): return lax.ppermute(plane, 'gz', outer_pairs(ring))]
    ppermute x3, waiting for transfers between devices: 0.01 us -> 9.4 us  [order_sum(): lax.ppermute(values, 'ord', [(i, i ^ step) for i in range(count)])]
    reshape x2 -> x3, local copies, waits for them, and re-layouts: 4.09 us -> 9.08 us  [cut(): lax.dynamic_slice(array, (start, plane, 0, 0), (length, 1, rows, columns))]
    ppermute x17 -> x18, starting transfers between devices: 15.9 us -> 11 us  [send_near(): return lax.ppermute(plane, 'gz', inner_pairs(ring))]
    pallas_call x24 -> x18, Pallas kernels: 37.6 us -> 33.6 us  [call(): pl.pallas_call(functools.partial(kernel, piece * size, planes, coupling,...]
    unnamed x10 -> x20, local copies, waits for them, and re-layouts: 0.02 us -> 2.82 us
    ppermute x24 -> x17, waiting for transfers between devices: 120 us -> 123 us  [send_far(): return lax.ppermute(plane, 'gz', outer_pairs(ring))]
  transfers between devices with their start and end apart: 44 -> 38, of which waited for: 19 -> 18; matrix products, arithmetic and copies ran while one was open for 1% -> 3% of each run, Pallas kernels for 16% -> 15%
where the time goes in v3:
time: 214 us
  waiting for transfers between devices  132 us (62%)
  starting transfers between devices  35.8 us (17%)
  Pallas kernels  33.6 us (16%)
  local copies, waits for them, and re-layouts  11.9 us (6%)
    ppermute x17, waiting for transfers between devices, send_far(): return lax.ppermute(plane, 'gz', outer_pairs(ring))  123 us
    pallas_call x18, Pallas kernels, call(): pl.pallas_call(functools.partial(kernel, piece * size, planes, coupling,...  33.6 us
    ppermute x17, starting transfers between devices, send_far(): return lax.ppermute(plane, 'gz', outer_pairs(ring))  21 us
    ppermute x18, starting transfers between devices, send_near(): return lax.ppermute(plane, 'gz', inner_pairs(ring))  11 us
    ppermute x3, waiting for transfers between devices, order_sum(): lax.ppermute(values, 'ord', [(i, i ^ step) for i in range(count)])  9.4 us
    reshape x3, local copies, waits for them, and re-layouts, cut(): lax.dynamic_slice(array, (start, plane, 0, 0), (length, 1, rows, columns))  9.08 us
  transfers between devices with their start and end apart: 38, of which 18 were waited for; matrix products, arithmetic and copies ran while one was open for 3% of the time, Pallas kernels for 15%

profile of v3, /device:TPU:1, one launch (start us, length us, event | category | flops | bytes accessed | tf_op | source)
XLA Modules:
  0.0 214.3 jit_solution(12393890223503937975)
XLA Ops:
  0.0 2.4 %dynamic-slice_bitcast_fusion = f32[16,128,128]{2,1,0:T(8,128)} fusion(f32[48,2,128,128]{3,2,1,0:T(8,128)} %field.35, s32[]{:T(128)S(6)} %select_n.4), kind=kLoop, calls=%fused_computation.1 | loop fusion | bytes 2097156 | tf_op jit(solution)/shard_map/reshape | solution.py:190
  2.4 2.6 %collective-permute-start = (f32[16,128,128]{2,1,0:T(8,128)}, f32[16,128,128]{2,1,0:T(8,128)S(1)}, u32[]{:S(2)}, u32[]{:S(2)}) collective-permute-start(f32[16,128,128]{2,1,0:T(8,128)} %dynamic-slice_bitcast_fusion), channel_id=1, source_target_pairs={{0,30},{2,4},{4,2},{6,8},{8,6},{10,12},{12,10},{14,16},{16,14},{18... | collective-permute-start | bytes 3145736 | tf_op jit(solution)/shard_map/ppermute | solution.py:184
  5.1 3.9 %dynamic-slice_bitcast_fusion.11 = (f32[8,128,128]{2,1,0:T(8,128)S(1)}, f32[8,128,128]{2,1,0:T(8,128)S(1)}, f32[8,128,128]{2,1,0:T(8,128)S(1)}, f32[8,128,128]{2...) fusion(f32[48,2,128,128]{3,2,1,0:T(8,128)} %field.35, ...), kind=kLoop, calls=%fused_computation.12 | loop fusion | bytes 10485768 | tf_op jit(solution)/shard_map/reshape | solution.py:190
  9.0 2.9 %collective-permute-start.1 = (f32[8,128,128]{2,1,0:T(8,128)S(1)}, f32[8,128,128]{2,1,0:T(8,128)S(1)}, u32[]{:S(2)}, u32[]{:S(2)}) collective-permute-start(f32[8,128,128]{2,1,0:T(8,128)S(1)} %get-tuple-element.64), channel_id=1, source_target_pairs={{0,2},{2,0},{4,6},{6,4},{8,10},{10,8},{12,14},{14,12},{16,18},{18,... | collective-permute-start | bytes 1572872 | tf_op jit(solution)/shard_map/ppermute | solution.py:187
  14.0 3.6 %collective-permute-done.2 = f32[2,128,128]{2,1,0:T(8,128)S(1)} collective-permute-done((f32[2,128,128]{2,1,0:T(8,128)S(1)}, f32[2,128,128]{2,1,0:T(8,128)S(1)}, u32[]{:S(2)}, u32[]{:S(2)}) %collective-permute-start.2) | collective-permute-done | bytes 131104 | tf_op jit(solution)/shard_map/ppermute | solution.py:49
  18.4 16.2 %collective-permute-done.far = f32[16,128,128]{2,1,0:T(8,128)S(1)} collective-permute-done((f32[16,128,128]{2,1,0:T(8,128)}, f32[16,128,128]{2,1,0:T(8,128)S(1)}, u32[]{:S(2)}, u32[]{:S(2)}) %collective-permute-start) | collective-permute-done | bytes 1048608 | tf_op jit(solution)/shard_map/ppermute | solution.py:184
  36.4 2.8 %copy-done = f32[48,2,128,128]{3,2,1,0:T(8,128)S(1)} copy-done((f32[48,2,128,128]{3,2,1,0:T(8,128)S(1)}, f32[48,2,128,128]{3,2,1,0:T(8,128)}, u32[]{:S(2)}) %copy-start) | copy-done | bytes 6291480
  42.4 8.3 %collective-permute-done.4.far = f32[8,128,128]{2,1,0:T(8,128)S(1)} collective-permute-done((f32[8,128,128]{2,1,0:T(8,128)S(1)}, f32[8,128,128]{2,1,0:T(8,128)S(1)}, u32[]{:S(2)}, u32[]{:S(2)}) %collective-permute-start.4) | collective-permute-done | bytes 524320 | tf_op jit(solution)/shard_map/ppermute | solution.py:184
  50.7 2.5 %collective-permute-start.9 = (f32[8,128,128]{2,1,0:T(8,128)S(1)}, f32[8,128,128]{2,1,0:T(8,128)S(1)}, u32[]{:S(2)}, u32[]{:S(2)}) collective-permute-start(f32[8,128,128]{2,1,0:T(8,128)S(1)} %get-tuple-element.74), channel_id=1, source_target_pairs={{0,30},{2,4},{4,2},{6,8},{8,6},{10,12},{12,10},{14,16},{16,14},{18... | collective-permute-start | bytes 1572872 | tf_op jit(solution)/shard_map/ppermute | solution.py:184
  54.8 2.7 %dynamic-slice_bitcast_fusion.1 = (f32[8,128,128]{2,1,0:T(8,128)}, f32[8,128,128]{2,1,0:T(8,128)}, f32[8,128,128]{2,1,0:T(8,128)}, f32[8,128,128]{2,1,0:T(8,128)...) fusion(f32[48,2,128,128]{3,2,1,0:T(8,128)S(1)} %copy-done, ...), kind=kLoop, calls=%fused_computation.2 | loop fusion | bytes 12582920 | tf_op jit(solution)/shard_map/reshape | solution.py:190
  57.6 5.1 %collective-permute-done.3.far = f32[8,128,128]{2,1,0:T(8,128)S(1)} collective-permute-done((f32[8,128,128]{2,1,0:T(8,128)S(1)}, f32[8,128,128]{2,1,0:T(8,128)S(1)}, u32[]{:S(2)}, u32[]{:S(2)}) %collective-permute-start.3) | collective-permute-done | bytes 524320 | tf_op jit(solution)/shard_map/ppermute | solution.py:184
  64.3 4.0 %collective-permute-done.11.far = f32[8,128,128]{2,1,0:T(8,128)S(1)} collective-permute-done((f32[8,128,128]{2,1,0:T(8,128)S(1)}, f32[8,128,128]{2,1,0:T(8,128)S(1)}, u32[]{:S(2)}, u32[]{:S(2)}) %collective-permute-start.11) | collective-permute-done | bytes 524320 | tf_op jit(solution)/shard_map/ppermute | solution.py:184
  80.5 3.7 %collective-permute-start.19 = (f32[8,128,128]{2,1,0:T(8,128)}, f32[8,128,128]{2,1,0:T(8,128)S(1)}, u32[]{:S(2)}, u32[]{:S(2)}) collective-permute-start(f32[8,128,128]{2,1,0:T(8,128)} %get-tuple-element.87), channel_id=1, source_target_pairs={{0,2},{2,0},{4,6},{6,4},{8,10},{10,8},{12,14},{14,12},{16,18},{18,... | collective-permute-start | bytes 1572872 | tf_op jit(solution)/shard_map/ppermute | solution.py:187
  84.2 2.9 %collective-permute-done.14 = f32[2,2,128,128]{3,2,1,0:T(8,128)S(1)} collective-permute-done((f32[2,2,128,128]{3,2,1,0:T(8,128)S(1)}, f32[2,2,128,128]{3,2,1,0:T(8,128)S(1)}, u32[]{:S(2)}, u32[]{:S(2)}) %collective-permute-start.14) | collective-permute-done | bytes 262176 | tf_op jit(solution)/shard_map/ppermute | solution.py:49
  87.7 8.7 %collective-permute-done.7.far = f32[8,128,128]{2,1,0:T(8,128)S(1)} collective-permute-done((f32[8,128,128]{2,1,0:T(8,128)}, f32[8,128,128]{2,1,0:T(8,128)S(1)}, u32[]{:S(2)}, u32[]{:S(2)}) %collective-permute-start.7) | collective-permute-done | bytes 524320 | tf_op jit(solution)/shard_map/ppermute | solution.py:184
  96.4 5.6 %collective-permute-done.20.far = f32[8,128,128]{2,1,0:T(8,128)S(1)} collective-permute-done((f32[8,128,128]{2,1,0:T(8,128)}, f32[8,128,128]{2,1,0:T(8,128)S(1)}, u32[]{:S(2)}, u32[]{:S(2)}) %collective-permute-start.20) | collective-permute-done | bytes 524320 | tf_op jit(solution)/shard_map/ppermute | solution.py:184
  102.0 27.3 %collective-permute-done.17.far = f32[8,128,128]{2,1,0:T(8,128)S(1)} collective-permute-done((f32[8,128,128]{2,1,0:T(8,128)S(1)}, f32[8,128,128]{2,1,0:T(8,128)S(1)}, u32[]{:S(2)}, u32[]{:S(2)}) %collective-permute-start.17) | collective-permute-done | bytes 524320 | tf_op jit(solution)/shard_map/ppermute | solution.py:184
  129.4 2.5 %collective-permute-start.21 = (f32[8,128,128]{2,1,0:T(8,128)}, f32[8,128,128]{2,1,0:T(8,128)S(1)}, u32[]{:S(2)}, u32[]{:S(2)}) collective-permute-start(f32[8,128,128]{2,1,0:T(8,128)} %get-tuple-element.90), channel_id=1, source_target_pairs={{0,30},{2,4},{4,2},{6,8},{8,6},{10,12},{12,10},{14,16},{16,14},{18... | collective-permute-start | bytes 1572872 | tf_op jit(solution)/shard_map/ppermute | solution.py:184
  131.9 2.3 %shard_map.52 = (f32[8,128,128]{2,1,0:T(8,128)S(1)}, f32[8,128,128]{2,1,0:T(8,128)S(1)}, f32[8,2,128,128]{3,2,1,0:T(8,128)S(1)}, f32[2,128,128]{2,1,0:T(8,128)S(1)}) custom-call(s32[1]{0:T(128)} %bitcast.odd_ref, f32[48]{0:T(128)S(1)} %copy-done.1, f32[48]{0:T(128)S(1)} %copy-done.2, f32[48,2,128,128]{3,2,1,0:T(8,128)S(1)} %bitcast.48, ...), custom_call_target="tpu_custom_call" | custom-call | flops 7864320 | bytes 5242880 | tf_op jit(solution)/shard_map/pallas_call | solution.py:218
  134.2 2.3 %shard_map.53 = (f32[8,128,128]{2,1,0:T(8,128)S(1)}, f32[8,128,128]{2,1,0:T(8,128)S(1)}, f32[8,2,128,128]{3,2,1,0:T(8,128)S(1)}, f32[2,128,128]{2,1,0:T(8,128)S(1)}) custom-call(s32[1]{0:T(128)} %bitcast.odd_ref, f32[48]{0:T(128)S(1)} %copy-done.1, f32[48]{0:T(128)S(1)} %copy-done.2, ...), custom_call_target="tpu_custom_call", output_to_operand_aliasing={{3}: (10, {})} | custom-call | flops 7864320 | bytes 5242880 | tf_op jit(solution)/shard_map/pallas_call | solution.py:218
  138.4 2.3 %shard_map.54 = (f32[8,128,128]{2,1,0:T(8,128)S(1)}, f32[8,128,128]{2,1,0:T(8,128)S(1)}, f32[8,2,128,128]{3,2,1,0:T(8,128)S(1)}, f32[2,128,128]{2,1,0:T(8,128)S(1)}) custom-call(s32[1]{0:T(128)} %bitcast.odd_ref, f32[48]{0:T(128)S(1)} %copy-done.1, f32[48]{0:T(128)S(1)} %copy-done.2, ...), custom_call_target="tpu_custom_call", output_to_operand_aliasing={{3}: (10, {})} | custom-call | flops 7864320 | bytes 5242880 | tf_op jit(solution)/shard_map/pallas_call | solution.py:218
  142.6 2.7 %collective-permute-done.18.far = f32[8,128,128]{2,1,0:T(8,128)S(1)} collective-permute-done((f32[8,128,128]{2,1,0:T(8,128)S(1)}, f32[8,128,128]{2,1,0:T(8,128)S(1)}, u32[]{:S(2)}, u32[]{:S(2)}) %collective-permute-start.18) | collective-permute-done | bytes 524320 | tf_op jit(solution)/shard_map/ppermute | solution.py:184
  146.3 15.8 %collective-permute-done.23.far = f32[8,128,128]{2,1,0:T(8,128)S(1)} collective-permute-done((f32[8,128,128]{2,1,0:T(8,128)S(1)}, f32[8,128,128]{2,1,0:T(8,128)S(1)}, u32[]{:S(2)}, u32[]{:S(2)}) %collective-permute-start.23) | collective-permute-done | bytes 524320 | tf_op jit(solution)/shard_map/ppermute | solution.py:184
  162.1 2.9 %shard_map.55 = (f32[8,128,128]{2,1,0:T(8,128)}, f32[8,128,128]{2,1,0:T(8,128)S(1)}, f32[8,2,128,128]{3,2,1,0:T(8,128)S(1)}, f32[2,128,128]{2,1,0:T(8,128)S(1)}) custom-call(s32[1]{0:T(128)} %bitcast.odd_ref, f32[48]{0:T(128)S(1)} %copy-done.1, f32[48]{0:T(128)S(1)} %copy-done.2, f32[48,2,128,128]{3,2,1,0:T(8,128)S(1)} %bitcast.48, ...), custom_call_target="tpu_custom_call", output_to_operand_aliasing={{3}: (10, {})} | custom-call | flops 7864320 | bytes 5242880 | tf_op jit(solution)/shard_map/pallas_call | solution.py:218
  165.0 2.7 %collective-permute-done.34.far = f32[8,128,128]{2,1,0:T(8,128)S(1)} collective-permute-done((f32[8,128,128]{2,1,0:T(8,128)S(1)}, f32[8,128,128]{2,1,0:T(8,128)S(1)}, u32[]{:S(2)}, u32[]{:S(2)}) %collective-permute-start.34) | collective-permute-done | bytes 524320 | tf_op jit(solution)/shard_map/ppermute | solution.py:184
  168.8 2.3 %shard_map.56 = (f32[8,128,128]{2,1,0:T(8,128)S(1)}, f32[8,128,128]{2,1,0:T(8,128)S(1)}, f32[8,2,128,128]{3,2,1,0:T(8,128)S(1)}, f32[2,128,128]{2,1,0:T(8,128)S(1)}) custom-call(s32[1]{0:T(128)} %bitcast.odd_ref, f32[48]{0:T(128)S(1)} %copy-done.1, f32[48]{0:T(128)S(1)} %copy-done.2, ...), custom_call_target="tpu_custom_call", output_to_operand_aliasing={{3}: (10, {})} | custom-call | flops 7864320 | bytes 5242880 | tf_op jit(solution)/shard_map/pallas_call | solution.py:218
  171.0 2.3 %shard_map.57 = (f32[8,128,128]{2,1,0:T(8,128)S(1)}, f32[8,128,128]{2,1,0:T(8,128)S(1)}, f32[8,2,128,128]{3,2,1,0:T(8,128)S(1)}, f32[2,128,128]{2,1,0:T(8,128)S(1)}) custom-call(s32[1]{0:T(128)} %bitcast.odd_ref, f32[48]{0:T(128)S(1)} %copy-done.1, f32[48]{0:T(128)S(1)} %copy-done.2, ...), custom_call_target="tpu_custom_call", output_to_operand_aliasing={{3}: (10, {})} | custom-call | flops 7864320 | bytes 5242880 | tf_op jit(solution)/shard_map/pallas_call | solution.py:218
  173.3 4.2 %collective-permute-done.36.far = f32[8,128,128]{2,1,0:T(8,128)S(1)} collective-permute-done((f32[8,128,128]{2,1,0:T(8,128)S(1)}, f32[8,128,128]{2,1,0:T(8,128)S(1)}, u32[]{:S(2)}, u32[]{:S(2)}) %collective-permute-start.36) | collective-permute-done | bytes 524320 | tf_op jit(solution)/shard_map/ppermute | solution.py:184
  178.7 2.9 %collective-permute-done.27 = f32[2,128,128]{2,1,0:T(8,128)S(1)} collective-permute-done((f32[2,128,128]{2,1,0:T(8,128)S(1)}, f32[2,128,128]{2,1,0:T(8,128)S(1)}, u32[]{:S(2)}, u32[]{:S(2)}) %collective-permute-start.27) | collective-permute-done | bytes 131104 | tf_op jit(solution)/shard_map/ppermute | solution.py:49
  181.6 2.9 %collective-permute-done.15.far = f32[8,128,128]{2,1,0:T(8,128)S(1)} collective-permute-done((f32[8,128,128]{2,1,0:T(8,128)S(1)}, f32[8,128,128]{2,1,0:T(8,128)S(1)}, u32[]{:S(2)}, u32[]{:S(2)}) %collective-permute-start.15) | collective-permute-done | bytes 524320 | tf_op jit(solution)/shard_map/ppermute | solution.py:184
  188.4 13.1 %collective-permute-done.32.far = f32[8,128,128]{2,1,0:T(8,128)S(1)} collective-permute-done((f32[8,128,128]{2,1,0:T(8,128)}, f32[8,128,128]{2,1,0:T(8,128)S(1)}, u32[]{:S(2)}, u32[]{:S(2)}) %collective-permute-start.32) | collective-permute-done | bytes 524320 | tf_op jit(solution)/shard_map/ppermute | solution.py:184
  209.1 3.6 %collective-permute-done.28.far = f32[8,128,128]{2,1,0:T(8,128)S(1)} collective-permute-done((f32[8,128,128]{2,1,0:T(8,128)S(1)}, f32[8,128,128]{2,1,0:T(8,128)S(1)}, u32[]{:S(2)}, u32[]{:S(2)}) %collective-permute-start.28) | collective-permute-done | bytes 524320 | tf_op jit(solution)/shard_map/ppermute | solution.py:184
  (91 shorter events, 43.9 us)
Async XLA Ops:
  2.4 32.1 %collective-permute-start = (f32[16,128,128]{2,1,0:T(8,128)}, f32[16,128,128]{2,1,0:T(8,128)S(1)}, u32[]{:S(2)}, u32[]{:S(2)}) collective-permute-start(f32[16,128,128]{2,1,0:T(8,128)} %dynamic-slice_bitcast_fusion), channel_id=1, source_target_pairs={{0,30},{2,4},{4,2},{6,8},{8,6},{10,12},{12,10},{14,16},{16,14},{18... | collective-permute-start | bytes 3145736 | tf_op jit(solution)/shard_map/ppermute | solution.py:184
  9.0 25.6 %collective-permute-start.1 = (f32[8,128,128]{2,1,0:T(8,128)S(1)}, f32[8,128,128]{2,1,0:T(8,128)S(1)}, u32[]{:S(2)}, u32[]{:S(2)}) collective-permute-start(f32[8,128,128]{2,1,0:T(8,128)S(1)} %get-tuple-element.64), channel_id=1, source_target_pairs={{0,2},{2,0},{4,6},{6,4},{8,10},{10,8},{12,14},{14,12},{16,18},{18,... | collective-permute-start | bytes 1572872 | tf_op jit(solution)/shard_map/ppermute | solution.py:187
  13.7 27.0 %collective-permute-start.6 = (f32[8,128,128]{2,1,0:T(8,128)S(1)}, f32[8,128,128]{2,1,0:T(8,128)S(1)}, u32[]{:S(2)}, u32[]{:S(2)}) collective-permute-start(f32[8,128,128]{2,1,0:T(8,128)S(1)} %get-tuple-element.68), channel_id=1, source_target_pairs={{0,2},{2,0},{4,6},{6,4},{8,10},{10,8},{12,14},{14,12},{16,18},{18,... | collective-permute-start | bytes 1572872 | tf_op jit(solution)/shard_map/ppermute | solution.py:187
  14.0 36.7 %collective-permute-start.4 = (f32[8,128,128]{2,1,0:T(8,128)S(1)}, f32[8,128,128]{2,1,0:T(8,128)S(1)}, u32[]{:S(2)}, u32[]{:S(2)}) collective-permute-start(f32[8,128,128]{2,1,0:T(8,128)S(1)} %get-tuple-element.142), channel_id=1, source_target_pairs={{0,30},{2,4},{4,2},{6,8},{8,6},{10,12},{12,10},{14,16},{16,14},{18... | collective-permute-start | bytes 1572872 | tf_op jit(solution)/shard_map/ppermute | solution.py:184
  17.6 33.1 %collective-permute-start.5 = (f32[8,128,128]{2,1,0:T(8,128)S(1)}, f32[8,128,128]{2,1,0:T(8,128)S(1)}, u32[]{:S(2)}, u32[]{:S(2)}) collective-permute-start(f32[8,128,128]{2,1,0:T(8,128)S(1)} %get-tuple-element.67), channel_id=1, source_target_pairs={{0,2},{2,0},{4,6},{6,4},{8,10},{10,8},{12,14},{14,12},{16,18},{18,... | collective-permute-start | bytes 1572872 | tf_op jit(solution)/shard_map/ppermute | solution.py:187
  34.6 18.6 %collective-permute-start.13 = (f32[8,128,128]{2,1,0:T(8,128)S(1)}, f32[8,128,128]{2,1,0:T(8,128)S(1)}, u32[]{:S(2)}, u32[]{:S(2)}) collective-permute-start(f32[8,128,128]{2,1,0:T(8,128)S(1)} %get-tuple-element.78), channel_id=1, source_target_pairs={{0,2},{2,0},{4,6},{6,4},{8,10},{10,8},{12,14},{14,12},{16,18},{18,... | collective-permute-start | bytes 1572872 | tf_op jit(solution)/shard_map/ppermute | solution.py:187
  34.6 28.1 %collective-permute-start.3 = (f32[8,128,128]{2,1,0:T(8,128)S(1)}, f32[8,128,128]{2,1,0:T(8,128)S(1)}, u32[]{:S(2)}, u32[]{:S(2)}) collective-permute-start(f32[8,128,128]{2,1,0:T(8,128)S(1)} %get-tuple-element.66), channel_id=1, source_target_pairs={{0,30},{2,4},{4,2},{6,8},{8,6},{10,12},{12,10},{14,16},{16,14},{18... | collective-permute-start | bytes 1572872 | tf_op jit(solution)/shard_map/ppermute | solution.py:184
  40.7 27.6 %collective-permute-start.11 = (f32[8,128,128]{2,1,0:T(8,128)S(1)}, f32[8,128,128]{2,1,0:T(8,128)S(1)}, u32[]{:S(2)}, u32[]{:S(2)}) collective-permute-start(f32[8,128,128]{2,1,0:T(8,128)S(1)} %get-tuple-element.76), channel_id=1, source_target_pairs={{0,30},{2,4},{4,2},{6,8},{8,6},{10,12},{12,10},{14,16},{16,14},{18... | collective-permute-start | bytes 1572872 | tf_op jit(solution)/shard_map/ppermute | solution.py:184
  50.7 19.2 %collective-permute-start.12 = (f32[8,128,128]{2,1,0:T(8,128)S(1)}, f32[8,128,128]{2,1,0:T(8,128)S(1)}, u32[]{:S(2)}, u32[]{:S(2)}) collective-permute-start(f32[8,128,128]{2,1,0:T(8,128)S(1)} %get-tuple-element.77), channel_id=1, source_target_pairs={{0,2},{2,0},{4,6},{6,4},{8,10},{10,8},{12,14},{14,12},{16,18},{18,... | collective-permute-start | bytes 1572872 | tf_op jit(solution)/shard_map/ppermute | solution.py:187
  50.7 23.2 %collective-permute-start.9 = (f32[8,128,128]{2,1,0:T(8,128)S(1)}, f32[8,128,128]{2,1,0:T(8,128)S(1)}, u32[]{:S(2)}, u32[]{:S(2)}) collective-permute-start(f32[8,128,128]{2,1,0:T(8,128)S(1)} %get-tuple-element.74), channel_id=1, source_target_pairs={{0,30},{2,4},{4,2},{6,8},{8,6},{10,12},{12,10},{14,16},{16,14},{18... | collective-permute-start | bytes 1572872 | tf_op jit(solution)/shard_map/ppermute | solution.py:184
  53.2 24.1 %collective-permute-start.10 = (f32[8,128,128]{2,1,0:T(8,128)}, f32[8,128,128]{2,1,0:T(8,128)S(1)}, u32[]{:S(2)}, u32[]{:S(2)}) collective-permute-start(f32[8,128,128]{2,1,0:T(8,128)} %get-tuple-element.75), channel_id=1, source_target_pairs={{0,2},{2,0},{4,6},{6,4},{8,10},{10,8},{12,14},{14,12},{16,18},{18,... | collective-permute-start | bytes 1572872 | tf_op jit(solution)/shard_map/ppermute | solution.py:187
  62.7 17.5 %collective-permute-start.8 = (f32[8,128,128]{2,1,0:T(8,128)}, f32[8,128,128]{2,1,0:T(8,128)S(1)}, u32[]{:S(2)}, u32[]{:S(2)}) collective-permute-start(f32[8,128,128]{2,1,0:T(8,128)} %get-tuple-element.73), channel_id=1, source_target_pairs={{0,2},{2,0},{4,6},{6,4},{8,10},{10,8},{12,14},{14,12},{16,18},{18,... | collective-permute-start | bytes 1572872 | tf_op jit(solution)/shard_map/ppermute | solution.py:187
  68.3 12.2 %collective-permute-start.26 = (f32[8,128,128]{2,1,0:T(8,128)}, f32[8,128,128]{2,1,0:T(8,128)S(1)}, u32[]{:S(2)}, u32[]{:S(2)}) collective-permute-start(f32[8,128,128]{2,1,0:T(8,128)} %get-tuple-element.98), channel_id=1, source_target_pairs={{0,2},{2,0},{4,6},{6,4},{8,10},{10,8},{12,14},{14,12},{16,18},{18,... | collective-permute-start | bytes 1572872 | tf_op jit(solution)/shard_map/ppermute | solution.py:187
  69.9 26.5 %collective-permute-start.7 = (f32[8,128,128]{2,1,0:T(8,128)}, f32[8,128,128]{2,1,0:T(8,128)S(1)}, u32[]{:S(2)}, u32[]{:S(2)}) collective-permute-start(f32[8,128,128]{2,1,0:T(8,128)} %get-tuple-element.72), channel_id=1, source_target_pairs={{0,30},{2,4},{4,2},{6,8},{8,6},{10,12},{12,10},{14,16},{16,14},{18... | collective-permute-start | bytes 1572872 | tf_op jit(solution)/shard_map/ppermute | solution.py:184
  73.9 28.1 %collective-permute-start.20 = (f32[8,128,128]{2,1,0:T(8,128)}, f32[8,128,128]{2,1,0:T(8,128)S(1)}, u32[]{:S(2)}, u32[]{:S(2)}) collective-permute-start(f32[8,128,128]{2,1,0:T(8,128)} %get-tuple-element.89), channel_id=1, source_target_pairs={{0,30},{2,4},{4,2},{6,8},{8,6},{10,12},{12,10},{14,16},{16,14},{18... | collective-permute-start | bytes 1572872 | tf_op jit(solution)/shard_map/ppermute | solution.py:184
  80.2 49.2 %collective-permute-start.17 = (f32[8,128,128]{2,1,0:T(8,128)S(1)}, f32[8,128,128]{2,1,0:T(8,128)S(1)}, u32[]{:S(2)}, u32[]{:S(2)}) collective-permute-start(f32[8,128,128]{2,1,0:T(8,128)S(1)} %copy-done.5), channel_id=1, source_target_pairs={{0,30},{2,4},{4,2},{6,8},{8,6},{10,12},{12,10},{14,16},{16,14},{18... | collective-permute-start | bytes 1572872 | tf_op jit(solution)/shard_map/ppermute | solution.py:184
  80.5 56.1 %collective-permute-start.19 = (f32[8,128,128]{2,1,0:T(8,128)}, f32[8,128,128]{2,1,0:T(8,128)S(1)}, u32[]{:S(2)}, u32[]{:S(2)}) collective-permute-start(f32[8,128,128]{2,1,0:T(8,128)} %get-tuple-element.87), channel_id=1, source_target_pairs={{0,2},{2,0},{4,6},{6,4},{8,10},{10,8},{12,14},{14,12},{16,18},{18,... | collective-permute-start | bytes 1572872 | tf_op jit(solution)/shard_map/ppermute | solution.py:187
  87.1 49.5 %collective-permute-start.25 = (f32[8,128,128]{2,1,0:T(8,128)}, f32[8,128,128]{2,1,0:T(8,128)S(1)}, u32[]{:S(2)}, u32[]{:S(2)}) collective-permute-start(f32[8,128,128]{2,1,0:T(8,128)} %get-tuple-element.96), channel_id=1, source_target_pairs={{0,2},{2,0},{4,6},{6,4},{8,10},{10,8},{12,14},{14,12},{16,18},{18,... | collective-permute-start | bytes 1572872 | tf_op jit(solution)/shard_map/ppermute | solution.py:187
  96.4 44.3 %collective-permute-start.22 = (f32[8,128,128]{2,1,0:T(8,128)}, f32[8,128,128]{2,1,0:T(8,128)S(1)}, u32[]{:S(2)}, u32[]{:S(2)}) collective-permute-start(f32[8,128,128]{2,1,0:T(8,128)} %get-tuple-element.91), channel_id=1, source_target_pairs={{0,2},{2,0},{4,6},{6,4},{8,10},{10,8},{12,14},{14,12},{16,18},{18,... | collective-permute-start | bytes 1572872 | tf_op jit(solution)/shard_map/ppermute | solution.py:187
  102.0 38.8 %collective-permute-start.24 = (f32[8,128,128]{2,1,0:T(8,128)}, f32[8,128,128]{2,1,0:T(8,128)S(1)}, u32[]{:S(2)}, u32[]{:S(2)}) collective-permute-start(f32[8,128,128]{2,1,0:T(8,128)} %get-tuple-element.94), channel_id=1, source_target_pairs={{0,2},{2,0},{4,6},{6,4},{8,10},{10,8},{12,14},{14,12},{16,18},{18,... | collective-permute-start | bytes 1572872 | tf_op jit(solution)/shard_map/ppermute | solution.py:187
  136.7 25.4 %collective-permute-start.23 = (f32[8,128,128]{2,1,0:T(8,128)S(1)}, f32[8,128,128]{2,1,0:T(8,128)S(1)}, u32[]{:S(2)}, u32[]{:S(2)}) collective-permute-start(f32[8,128,128]{2,1,0:T(8,128)S(1)} %copy-done.3), channel_id=1, source_target_pairs={{0,30},{2,4},{4,2},{6,8},{8,6},{10,12},{12,10},{14,16},{16,14},{18... | collective-permute-start | bytes 1572872 | tf_op jit(solution)/shard_map/ppermute | solution.py:184
  140.7 27.0 %collective-permute-start.34 = (f32[8,128,128]{2,1,0:T(8,128)S(1)}, f32[8,128,128]{2,1,0:T(8,128)S(1)}, u32[]{:S(2)}, u32[]{:S(2)}) collective-permute-start(f32[8,128,128]{2,1,0:T(8,128)S(1)} %get-tuple-element.116), channel_id=1, source_target_pairs={{0,30},{2,4},{4,2},{6,8},{8,6},{10,12},{12,10},{14,16},{16,14},{18... | collective-permute-start | bytes 1572872 | tf_op jit(solution)/shard_map/ppermute | solution.py:184
  140.8 26.9 %collective-permute-start.35 = (f32[8,128,128]{2,1,0:T(8,128)S(1)}, f32[8,128,128]{2,1,0:T(8,128)S(1)}, u32[]{:S(2)}, u32[]{:S(2)}) collective-permute-start(f32[8,128,128]{2,1,0:T(8,128)S(1)} %get-tuple-element.117), channel_id=1, source_target_pairs={{0,2},{2,0},{4,6},{6,4},{8,10},{10,8},{12,14},{14,12},{16,18},{18,... | collective-permute-start | bytes 1572872 | tf_op jit(solution)/shard_map/ppermute | solution.py:187
  140.9 36.6 %collective-permute-start.36 = (f32[8,128,128]{2,1,0:T(8,128)S(1)}, f32[8,128,128]{2,1,0:T(8,128)S(1)}, u32[]{:S(2)}, u32[]{:S(2)}) collective-permute-start(f32[8,128,128]{2,1,0:T(8,128)S(1)} %get-tuple-element.119), channel_id=1, source_target_pairs={{0,30},{2,4},{4,2},{6,8},{8,6},{10,12},{12,10},{14,16},{16,14},{18... | collective-permute-start | bytes 1572872 | tf_op jit(solution)/shard_map/ppermute | solution.py:184
  145.2 39.3 %collective-permute-start.15 = (f32[8,128,128]{2,1,0:T(8,128)S(1)}, f32[8,128,128]{2,1,0:T(8,128)S(1)}, u32[]{:S(2)}, u32[]{:S(2)}) collective-permute-start(f32[8,128,128]{2,1,0:T(8,128)S(1)} %get-tuple-element.82), channel_id=1, source_target_pairs={{0,30},{2,4},{4,2},{6,8},{8,6},{10,12},{12,10},{14,16},{16,14},{18... | collective-permute-start | bytes 1572872 | tf_op jit(solution)/shard_map/ppermute | solution.py:184
  162.1 23.5 %collective-permute-start.16 = (f32[8,128,128]{2,1,0:T(8,128)S(1)}, f32[8,128,128]{2,1,0:T(8,128)S(1)}, u32[]{:S(2)}, u32[]{:S(2)}) collective-permute-start(f32[8,128,128]{2,1,0:T(8,128)S(1)} %get-tuple-element.83), channel_id=1, source_target_pairs={{0,2},{2,0},{4,6},{6,4},{8,10},{10,8},{12,14},{14,12},{16,18},{18,... | collective-permute-start | bytes 1572872 | tf_op jit(solution)/shard_map/ppermute | solution.py:187
  167.7 20.6 %collective-permute-start.37 = (f32[8,128,128]{2,1,0:T(8,128)S(1)}, f32[8,128,128]{2,1,0:T(8,128)S(1)}, u32[]{:S(2)}, u32[]{:S(2)}) collective-permute-start(f32[8,128,128]{2,1,0:T(8,128)S(1)} %get-tuple-element.120), channel_id=1, source_target_pairs={{0,2},{2,0},{4,6},{6,4},{8,10},{10,8},{12,14},{14,12},{16,18},{18,... | collective-permute-start | bytes 1572872 | tf_op jit(solution)/shard_map/ppermute | solution.py:187
  167.7 33.7 %collective-permute-start.32 = (f32[8,128,128]{2,1,0:T(8,128)}, f32[8,128,128]{2,1,0:T(8,128)S(1)}, u32[]{:S(2)}, u32[]{:S(2)}) collective-permute-start(f32[8,128,128]{2,1,0:T(8,128)} %get-tuple-element.113), channel_id=1, source_target_pairs={{0,30},{2,4},{4,2},{6,8},{8,6},{10,12},{12,10},{14,16},{16,14},{18... | collective-permute-start | bytes 1572872 | tf_op jit(solution)/shard_map/ppermute | solution.py:184
  181.6 24.1 %collective-permute-start.33 = (f32[8,128,128]{2,1,0:T(8,128)S(1)}, f32[8,128,128]{2,1,0:T(8,128)S(1)}, u32[]{:S(2)}, u32[]{:S(2)}) collective-permute-start(f32[8,128,128]{2,1,0:T(8,128)S(1)} %get-tuple-element.114), channel_id=1, source_target_pairs={{0,2},{2,0},{4,6},{6,4},{8,10},{10,8},{12,14},{14,12},{16,18},{18,... | collective-permute-start | bytes 1572872 | tf_op jit(solution)/shard_map/ppermute | solution.py:187
  184.6 22.8 %collective-permute-start.30 = (f32[8,128,128]{2,1,0:T(8,128)S(1)}, f32[8,128,128]{2,1,0:T(8,128)S(1)}, u32[]{:S(2)}, u32[]{:S(2)}) collective-permute-start(f32[8,128,128]{2,1,0:T(8,128)S(1)} %get-tuple-element.110), channel_id=1, source_target_pairs={{0,30},{2,4},{4,2},{6,8},{8,6},{10,12},{12,10},{14,16},{16,14},{18... | collective-permute-start | bytes 1572872 | tf_op jit(solution)/shard_map/ppermute | solution.py:184
  185.6 21.8 %collective-permute-start.31 = (f32[8,128,128]{2,1,0:T(8,128)S(1)}, f32[8,128,128]{2,1,0:T(8,128)S(1)}, u32[]{:S(2)}, u32[]{:S(2)}) collective-permute-start(f32[8,128,128]{2,1,0:T(8,128)S(1)} %get-tuple-element.111), channel_id=1, source_target_pairs={{0,2},{2,0},{4,6},{6,4},{8,10},{10,8},{12,14},{14,12},{16,18},{18,... | collective-permute-start | bytes 1572872 | tf_op jit(solution)/shard_map/ppermute | solution.py:187
  188.3 20.8 %collective-permute-start.29 = (f32[8,128,128]{2,1,0:T(8,128)S(1)}, f32[8,128,128]{2,1,0:T(8,128)S(1)}, u32[]{:S(2)}, u32[]{:S(2)}) collective-permute-start(f32[8,128,128]{2,1,0:T(8,128)S(1)} %get-tuple-element.108), channel_id=1, source_target_pairs={{0,2},{2,0},{4,6},{6,4},{8,10},{10,8},{12,14},{14,12},{16,18},{18,... | collective-permute-start | bytes 1572872 | tf_op jit(solution)/shard_map/ppermute | solution.py:187
  (16 other events, 250.1 us)

commit v4 on v3

--- a/solution.py
+++ b/solution.py
@@ -19,7 +19,7 @@
 NEAR_LAG = 16
 FIRST = True
 BACK_GROUPS = (1, 1, 1, 1, 1, 1)
-AHEAD = 4
+AHEAD = 3
 CARRY = True
 EARLY = True
 FAR_FIRST = 2

time: 214 us -> 211 us (0.986)
  waiting for transfers between devices: 132 us -> 117 us
  starting transfers between devices: 35.8 us -> 48.8 us
    ppermute x17, waiting for transfers between devices: 123 us -> 114 us  [send_far(): return lax.ppermute(plane, 'gz', outer_pairs(ring))]
    ppermute x18, starting transfers between devices: 11 us -> 19.3 us  [send_near(): return lax.ppermute(plane, 'gz', inner_pairs(ring))]
    ppermute x3, waiting for transfers between devices: 9.4 us -> 2.68 us  [order_sum(): lax.ppermute(values, 'ord', [(i, i ^ step) for i in range(count)])]
    ppermute x17, starting transfers between devices: 21 us -> 25.6 us  [send_far(): return lax.ppermute(plane, 'gz', outer_pairs(ring))]
  transfers between devices with their start and end apart: 38 -> 38, of which waited for: 18 -> 15; matrix products, arithmetic and copies ran while one was open for 3% -> 3% of each run, Pallas kernels for 15% -> 15%
where the time goes in v4:
time: 211 us; the launch traced here: 210 us
  waiting for transfers between devices  117 us (55%)
  starting transfers between devices  48.8 us (23%)
  Pallas kernels  33.5 us (16%)
  local copies, waits for them, and re-layouts  10.7 us (5%)
    ppermute x17, waiting for transfers between devices, send_far(): return lax.ppermute(plane, 'gz', outer_pairs(ring))  114 us
    pallas_call x18, Pallas kernels, call(): pl.pallas_call(functools.partial(kernel, piece * size, planes, coupling,...  33.5 us
    ppermute x17, starting transfers between devices, send_far(): return lax.ppermute(plane, 'gz', outer_pairs(ring))  25.6 us
    ppermute x18, starting transfers between devices, send_near(): return lax.ppermute(plane, 'gz', inner_pairs(ring))  19.3 us
    reshape x3, local copies, waits for them, and re-layouts, cut(): lax.dynamic_slice(array, (start, plane, 0, 0), (length, 1, rows, columns))  7.86 us
  transfers between devices with their start and end apart: 38, of which 15 were waited for; matrix products, arithmetic and copies ran while one was open for 3% of the time, Pallas kernels for 15%

profile of v4, /device:TPU:1, one launch (start us, length us, event | category | flops | bytes accessed | tf_op | source)
XLA Modules:
  0.0 210.4 jit_solution(1956376116247396976)
XLA Ops:
  0.0 2.4 %dynamic-slice_bitcast_fusion = f32[16,128,128]{2,1,0:T(8,128)} fusion(f32[48,2,128,128]{3,2,1,0:T(8,128)} %field.35, s32[]{:T(128)S(6)} %select_n.4), kind=kLoop, calls=%fused_computation.1 | loop fusion | bytes 2097156 | tf_op jit(solution)/shard_map/reshape | solution.py:190
  2.4 2.6 %collective-permute-start = (f32[16,128,128]{2,1,0:T(8,128)}, f32[16,128,128]{2,1,0:T(8,128)S(1)}, u32[]{:S(2)}, u32[]{:S(2)}) collective-permute-start(f32[16,128,128]{2,1,0:T(8,128)} %dynamic-slice_bitcast_fusion), channel_id=1, source_target_pairs={{0,30},{2,4},{4,2},{6,8},{8,6},{10,12},{12,10},{14,16},{16,14},{18... | collective-permute-start | bytes 3145736 | tf_op jit(solution)/shard_map/ppermute | solution.py:184
  5.1 3.2 %dynamic-slice_bitcast_fusion.11 = (f32[8,128,128]{2,1,0:T(8,128)S(1)}, f32[8,128,128]{2,1,0:T(8,128)S(1)}, f32[8,128,128]{2,1,0:T(8,128)S(1)}, f32[8,128,128]{2...) fusion(f32[48,2,128,128]{3,2,1,0:T(8,128)} %field.35, ...), kind=kLoop, calls=%fused_computation.12 | loop fusion | bytes 10485768 | tf_op jit(solution)/shard_map/reshape | solution.py:190
  8.2 2.9 %collective-permute-start.1 = (f32[8,128,128]{2,1,0:T(8,128)S(1)}, f32[8,128,128]{2,1,0:T(8,128)S(1)}, u32[]{:S(2)}, u32[]{:S(2)}) collective-permute-start(f32[8,128,128]{2,1,0:T(8,128)S(1)} %get-tuple-element.66), channel_id=1, source_target_pairs={{0,2},{2,0},{4,6},{6,4},{8,10},{10,8},{12,14},{14,12},{16,18},{18,... | collective-permute-start | bytes 1572872 | tf_op jit(solution)/shard_map/ppermute | solution.py:187
  13.8 2.7 %collective-permute-done.2 = f32[2,128,128]{2,1,0:T(8,128)S(1)} collective-permute-done((f32[2,128,128]{2,1,0:T(8,128)S(1)}, f32[2,128,128]{2,1,0:T(8,128)S(1)}, u32[]{:S(2)}, u32[]{:S(2)}) %collective-permute-start.2) | collective-permute-done | bytes 131104 | tf_op jit(solution)/shard_map/ppermute | solution.py:49
  17.8 16.8 %collective-permute-done.far = f32[16,128,128]{2,1,0:T(8,128)S(1)} collective-permute-done((f32[16,128,128]{2,1,0:T(8,128)}, f32[16,128,128]{2,1,0:T(8,128)S(1)}, u32[]{:S(2)}, u32[]{:S(2)}) %collective-permute-start) | collective-permute-done | bytes 1048608 | tf_op jit(solution)/shard_map/ppermute | solution.py:184
  36.4 3.6 %collective-permute-start.13 = (f32[8,128,128]{2,1,0:T(8,128)S(1)}, f32[8,128,128]{2,1,0:T(8,128)S(1)}, u32[]{:S(2)}, u32[]{:S(2)}) collective-permute-start(f32[8,128,128]{2,1,0:T(8,128)S(1)} %get-tuple-element.81), channel_id=1, source_target_pairs={{0,2},{2,0},{4,6},{6,4},{8,10},{10,8},{12,14},{14,12},{16,18},{18,... | collective-permute-start | bytes 1572872 | tf_op jit(solution)/shard_map/ppermute | solution.py:187
  40.0 2.8 %copy-done = f32[48,2,128,128]{3,2,1,0:T(8,128)S(1)} copy-done((f32[48,2,128,128]{3,2,1,0:T(8,128)S(1)}, f32[48,2,128,128]{3,2,1,0:T(8,128)}, u32[]{:S(2)}) %copy-start) | copy-done | bytes 6291480
  44.3 12.0 %collective-permute-done.7.far = f32[8,128,128]{2,1,0:T(8,128)S(1)} collective-permute-done((f32[8,128,128]{2,1,0:T(8,128)S(1)}, f32[8,128,128]{2,1,0:T(8,128)S(1)}, u32[]{:S(2)}, u32[]{:S(2)}) %collective-permute-start.7) | collective-permute-done | bytes 524320 | tf_op jit(solution)/shard_map/ppermute | solution.py:184
  56.3 2.5 %collective-permute-start.4 = (f32[8,128,128]{2,1,0:T(8,128)S(1)}, f32[8,128,128]{2,1,0:T(8,128)S(1)}, u32[]{:S(2)}, u32[]{:S(2)}) collective-permute-start(f32[8,128,128]{2,1,0:T(8,128)S(1)} %get-tuple-element.70), channel_id=1, source_target_pairs={{0,30},{2,4},{4,2},{6,8},{8,6},{10,12},{12,10},{14,16},{16,14},{18... | collective-permute-start | bytes 1572872 | tf_op jit(solution)/shard_map/ppermute | solution.py:184
  60.5 2.3 %dynamic-slice_bitcast_fusion.1 = (f32[8,128,128]{2,1,0:T(8,128)}, f32[8,128,128]{2,1,0:T(8,128)}, f32[8,128,128]{2,1,0:T(8,128)}, f32[8,128,128]{2,1,0:T(8,128)...) fusion(f32[48,2,128,128]{3,2,1,0:T(8,128)S(1)} %copy-done, ...), kind=kLoop, calls=%fused_computation.2 | loop fusion | bytes 12582920 | tf_op jit(solution)/shard_map/reshape | solution.py:190
  71.2 19.6 %collective-permute-done.11.far = f32[8,128,128]{2,1,0:T(8,128)S(1)} collective-permute-done((f32[8,128,128]{2,1,0:T(8,128)S(1)}, f32[8,128,128]{2,1,0:T(8,128)S(1)}, u32[]{:S(2)}, u32[]{:S(2)}) %collective-permute-start.11) | collective-permute-done | bytes 524320 | tf_op jit(solution)/shard_map/ppermute | solution.py:184
  94.3 2.1 %collective-permute-done.15.far = f32[8,128,128]{2,1,0:T(8,128)S(1)} collective-permute-done((f32[8,128,128]{2,1,0:T(8,128)S(1)}, f32[8,128,128]{2,1,0:T(8,128)S(1)}, u32[]{:S(2)}, u32[]{:S(2)}) %collective-permute-start.15) | collective-permute-done | bytes 524320 | tf_op jit(solution)/shard_map/ppermute | solution.py:184
  98.0 1.8 collective-permute-start.24
  99.8 2.2 %collective-permute-done.9.far = f32[8,128,128]{2,1,0:T(8,128)S(1)} collective-permute-done((f32[8,128,128]{2,1,0:T(8,128)}, f32[8,128,128]{2,1,0:T(8,128)S(1)}, u32[]{:S(2)}, u32[]{:S(2)}) %collective-permute-start.9) | collective-permute-done | bytes 524320 | tf_op jit(solution)/shard_map/ppermute | solution.py:184
  103.2 15.6 %collective-permute-done.19.far = f32[8,128,128]{2,1,0:T(8,128)S(1)} collective-permute-done((f32[8,128,128]{2,1,0:T(8,128)}, f32[8,128,128]{2,1,0:T(8,128)S(1)}, u32[]{:S(2)}, u32[]{:S(2)}) %collective-permute-start.19) | collective-permute-done | bytes 524320 | tf_op jit(solution)/shard_map/ppermute | solution.py:184
  120.8 3.0 %shard_map.52 = (f32[8,128,128]{2,1,0:T(8,128)}, f32[8,128,128]{2,1,0:T(8,128)}, f32[8,2,128,128]{3,2,1,0:T(8,128)S(1)}, f32[2,128,128]{2,1,0:T(8,128)S(1)}) custom-call(s32[1]{0:T(128)} %bitcast.odd_ref, f32[48]{0:T(128)S(1)} %copy-done.1, f32[48]{0:T(128)S(1)} %copy-done.2, f32[48,2,128,128]{3,2,1,0:T(8,128)S(1)} %bitcast.48, ...), custom_call_target="tpu_custom_call" | custom-call | flops 7864320 | bytes 5242880 | tf_op jit(solution)/shard_map/pallas_call | solution.py:218
  123.8 2.3 %shard_map.53 = (f32[8,128,128]{2,1,0:T(8,128)S(1)}, f32[8,128,128]{2,1,0:T(8,128)S(1)}, f32[8,2,128,128]{3,2,1,0:T(8,128)S(1)}, f32[2,128,128]{2,1,0:T(8,128)S(1)}) custom-call(s32[1]{0:T(128)} %bitcast.odd_ref, f32[48]{0:T(128)S(1)} %copy-done.1, f32[48]{0:T(128)S(1)} %copy-done.2, ...), custom_call_target="tpu_custom_call", output_to_operand_aliasing={{3}: (10, {})} | custom-call | flops 7864320 | bytes 5242880 | tf_op jit(solution)/shard_map/pallas_call | solution.py:218
  126.1 2.3 %shard_map.54 = (f32[8,128,128]{2,1,0:T(8,128)S(1)}, f32[8,128,128]{2,1,0:T(8,128)S(1)}, f32[8,2,128,128]{3,2,1,0:T(8,128)S(1)}, f32[2,128,128]{2,1,0:T(8,128)S(1)}) custom-call(s32[1]{0:T(128)} %bitcast.odd_ref, f32[48]{0:T(128)S(1)} %copy-done.1, f32[48]{0:T(128)S(1)} %copy-done.2, ...), custom_call_target="tpu_custom_call", output_to_operand_aliasing={{3}: (10, {})} | custom-call | flops 7864320 | bytes 5242880 | tf_op jit(solution)/shard_map/pallas_call | solution.py:218
  131.8 2.3 %shard_map.55 = (f32[8,128,128]{2,1,0:T(8,128)S(1)}, f32[8,128,128]{2,1,0:T(8,128)S(1)}, f32[8,2,128,128]{3,2,1,0:T(8,128)S(1)}, f32[2,128,128]{2,1,0:T(8,128)S(1)}) custom-call(s32[1]{0:T(128)} %bitcast.odd_ref, f32[48]{0:T(128)S(1)} %copy-done.1, f32[48]{0:T(128)S(1)} %copy-done.2, ...), custom_call_target="tpu_custom_call", output_to_operand_aliasing={{3}: (10, {})} | custom-call | flops 7864320 | bytes 5242880 | tf_op jit(solution)/shard_map/pallas_call | solution.py:218
  134.1 12.2 %collective-permute-done.22.far = f32[8,128,128]{2,1,0:T(8,128)S(1)} collective-permute-done((f32[8,128,128]{2,1,0:T(8,128)}, f32[8,128,128]{2,1,0:T(8,128)S(1)}, u32[]{:S(2)}, u32[]{:S(2)}) %collective-permute-start.22) | collective-permute-done | bytes 524320 | tf_op jit(solution)/shard_map/ppermute | solution.py:184
  146.3 2.2 %shard_map.56 = (f32[8,128,128]{2,1,0:T(8,128)S(1)}, f32[8,128,128]{2,1,0:T(8,128)S(1)}, f32[8,2,128,128]{3,2,1,0:T(8,128)S(1)}, f32[2,128,128]{2,1,0:T(8,128)S(1)}) custom-call(s32[1]{0:T(128)} %bitcast.odd_ref, f32[48]{0:T(128)S(1)} %copy-done.1, f32[48]{0:T(128)S(1)} %copy-done.2, ...), custom_call_target="tpu_custom_call", output_to_operand_aliasing={{3}: (10, {})} | custom-call | flops 7864320 | bytes 5242880 | tf_op jit(solution)/shard_map/pallas_call | solution.py:218
  148.6 4.0 %collective-permute-done.20.far = f32[8,128,128]{2,1,0:T(8,128)S(1)} collective-permute-done((f32[8,128,128]{2,1,0:T(8,128)}, f32[8,128,128]{2,1,0:T(8,128)S(1)}, u32[]{:S(2)}, u32[]{:S(2)}) %collective-permute-start.20) | collective-permute-done | bytes 524320 | tf_op jit(solution)/shard_map/ppermute | solution.py:184
  152.6 2.3 %shard_map.57 = (f32[8,128,128]{2,1,0:T(8,128)S(1)}, f32[8,128,128]{2,1,0:T(8,128)S(1)}, f32[8,2,128,128]{3,2,1,0:T(8,128)S(1)}, f32[2,128,128]{2,1,0:T(8,128)S(1)}) custom-call(s32[1]{0:T(128)} %bitcast.odd_ref, f32[48]{0:T(128)S(1)} %copy-done.1, f32[48]{0:T(128)S(1)} %copy-done.2, ...), custom_call_target="tpu_custom_call", output_to_operand_aliasing={{3}: (10, {})} | custom-call | flops 7864320 | bytes 5242880 | tf_op jit(solution)/shard_map/pallas_call | solution.py:218
  156.1 2.0 collective-permute-start.17
  158.2 3.5 %collective-permute-start.18 = (f32[8,128,128]{2,1,0:T(8,128)S(1)}, f32[8,128,128]{2,1,0:T(8,128)S(1)}, u32[]{:S(2)}, u32[]{:S(2)}) collective-permute-start(f32[8,128,128]{2,1,0:T(8,128)S(1)} %get-tuple-element.89), channel_id=1, source_target_pairs={{0,2},{2,0},{4,6},{6,4},{8,10},{10,8},{12,14},{14,12},{16,18},{18,... | collective-permute-start | bytes 1572872 | tf_op jit(solution)/shard_map/ppermute | solution.py:187
  161.7 7.7 %collective-permute-done.28.far = f32[8,128,128]{2,1,0:T(8,128)S(1)} collective-permute-done((f32[8,128,128]{2,1,0:T(8,128)}, f32[8,128,128]{2,1,0:T(8,128)S(1)}, u32[]{:S(2)}, u32[]{:S(2)}) %collective-permute-start.28) | collective-permute-done | bytes 524320 | tf_op jit(solution)/shard_map/ppermute | solution.py:184
  171.2 3.6 %collective-permute-start.35 = (f32[8,128,128]{2,1,0:T(8,128)S(1)}, f32[8,128,128]{2,1,0:T(8,128)S(1)}, u32[]{:S(2)}, u32[]{:S(2)}) collective-permute-start(f32[8,128,128]{2,1,0:T(8,128)S(1)} %get-tuple-element.121), channel_id=1, source_target_pairs={{0,2},{2,0},{4,6},{6,4},{8,10},{10,8},{12,14},{14,12},{16,18},{18,... | collective-permute-start | bytes 1572872 | tf_op jit(solution)/shard_map/ppermute | solution.py:187
  176.4 3.5 %collective-permute-done.17.far = f32[8,128,128]{2,1,0:T(8,128)S(1)} collective-permute-done((f32[8,128,128]{2,1,0:T(8,128)S(1)}, f32[8,128,128]{2,1,0:T(8,128)S(1)}, u32[]{:S(2)}, u32[]{:S(2)}) %collective-permute-start.17) | collective-permute-done | bytes 524320 | tf_op jit(solution)/shard_map/ppermute | solution.py:184
  179.9 2.5 %collective-permute-start.32 = (f32[8,128,128]{2,1,0:T(8,128)S(1)}, f32[8,128,128]{2,1,0:T(8,128)S(1)}, u32[]{:S(2)}, u32[]{:S(2)}) collective-permute-start(f32[8,128,128]{2,1,0:T(8,128)S(1)} %get-tuple-element.117), channel_id=1, source_target_pairs={{0,30},{2,4},{4,2},{6,8},{8,6},{10,12},{12,10},{14,16},{16,14},{18... | collective-permute-start | bytes 1572872 | tf_op jit(solution)/shard_map/ppermute | solution.py:184
  185.7 11.8 %collective-permute-done.34.far = f32[8,128,128]{2,1,0:T(8,128)S(1)} collective-permute-done((f32[8,128,128]{2,1,0:T(8,128)S(1)}, f32[8,128,128]{2,1,0:T(8,128)S(1)}, u32[]{:S(2)}, u32[]{:S(2)}) %collective-permute-start.34) | collective-permute-done | bytes 524320 | tf_op jit(solution)/shard_map/ppermute | solution.py:184
  204.8 4.0 %collective-permute-done.30.far = f32[8,128,128]{2,1,0:T(8,128)S(1)} collective-permute-done((f32[8,128,128]{2,1,0:T(8,128)S(1)}, f32[8,128,128]{2,1,0:T(8,128)S(1)}, u32[]{:S(2)}, u32[]{:S(2)}) %collective-permute-start.30) | collective-permute-done | bytes 524320 | tf_op jit(solution)/shard_map/ppermute | solution.py:184
  (85 shorter events, 45.9 us)
Async XLA Ops:
  2.4 32.1 %collective-permute-start = (f32[16,128,128]{2,1,0:T(8,128)}, f32[16,128,128]{2,1,0:T(8,128)S(1)}, u32[]{:S(2)}, u32[]{:S(2)}) collective-permute-start(f32[16,128,128]{2,1,0:T(8,128)} %dynamic-slice_bitcast_fusion), channel_id=1, source_target_pairs={{0,30},{2,4},{4,2},{6,8},{8,6},{10,12},{12,10},{14,16},{16,14},{18... | collective-permute-start | bytes 3145736 | tf_op jit(solution)/shard_map/ppermute | solution.py:184
  11.2 23.4 %collective-permute-start.3 = (f32[8,128,128]{2,1,0:T(8,128)S(1)}, f32[8,128,128]{2,1,0:T(8,128)S(1)}, u32[]{:S(2)}, u32[]{:S(2)}) collective-permute-start(f32[8,128,128]{2,1,0:T(8,128)S(1)} %get-tuple-element.67), channel_id=1, source_target_pairs={{0,2},{2,0},{4,6},{6,4},{8,10},{10,8},{12,14},{14,12},{16,18},{18,... | collective-permute-start | bytes 1572872 | tf_op jit(solution)/shard_map/ppermute | solution.py:187
  13.1 23.2 %collective-permute-start.6 = (f32[8,128,128]{2,1,0:T(8,128)S(1)}, f32[8,128,128]{2,1,0:T(8,128)S(1)}, u32[]{:S(2)}, u32[]{:S(2)}) collective-permute-start(f32[8,128,128]{2,1,0:T(8,128)S(1)} %get-tuple-element.72), channel_id=1, source_target_pairs={{0,2},{2,0},{4,6},{6,4},{8,10},{10,8},{12,14},{14,12},{16,18},{18,... | collective-permute-start | bytes 1572872 | tf_op jit(solution)/shard_map/ppermute | solution.py:187
  16.5 39.8 %collective-permute-start.7 = (f32[8,128,128]{2,1,0:T(8,128)S(1)}, f32[8,128,128]{2,1,0:T(8,128)S(1)}, u32[]{:S(2)}, u32[]{:S(2)}) collective-permute-start(f32[8,128,128]{2,1,0:T(8,128)S(1)} %get-tuple-element.143), channel_id=1, source_target_pairs={{0,30},{2,4},{4,2},{6,8},{8,6},{10,12},{12,10},{14,16},{16,14},{18... | collective-permute-start | bytes 1572872 | tf_op jit(solution)/shard_map/ppermute | solution.py:184
  16.5 43.9 %collective-permute-start.8 = (f32[8,128,128]{2,1,0:T(8,128)S(1)}, f32[8,128,128]{2,1,0:T(8,128)S(1)}, u32[]{:S(2)}, u32[]{:S(2)}) collective-permute-start(f32[8,128,128]{2,1,0:T(8,128)S(1)} %get-tuple-element.73), channel_id=1, source_target_pairs={{0,2},{2,0},{4,6},{6,4},{8,10},{10,8},{12,14},{14,12},{16,18},{18,... | collective-permute-start | bytes 1572872 | tf_op jit(solution)/shard_map/ppermute | solution.py:187
  34.6 28.1 %collective-permute-start.12 = (f32[8,128,128]{2,1,0:T(8,128)S(1)}, f32[8,128,128]{2,1,0:T(8,128)S(1)}, u32[]{:S(2)}, u32[]{:S(2)}) collective-permute-start(f32[8,128,128]{2,1,0:T(8,128)S(1)} %get-tuple-element.80), channel_id=1, source_target_pairs={{0,2},{2,0},{4,6},{6,4},{8,10},{10,8},{12,14},{14,12},{16,18},{18,... | collective-permute-start | bytes 1572872 | tf_op jit(solution)/shard_map/ppermute | solution.py:187
  34.6 28.1 %collective-permute-start.5 = (f32[8,128,128]{2,1,0:T(8,128)S(1)}, f32[8,128,128]{2,1,0:T(8,128)S(1)}, u32[]{:S(2)}, u32[]{:S(2)}) collective-permute-start(f32[8,128,128]{2,1,0:T(8,128)S(1)} %get-tuple-element.71), channel_id=1, source_target_pairs={{0,30},{2,4},{4,2},{6,8},{8,6},{10,12},{12,10},{14,16},{16,14},{18... | collective-permute-start | bytes 1572872 | tf_op jit(solution)/shard_map/ppermute | solution.py:184
  36.4 28.4 %collective-permute-start.13 = (f32[8,128,128]{2,1,0:T(8,128)S(1)}, f32[8,128,128]{2,1,0:T(8,128)S(1)}, u32[]{:S(2)}, u32[]{:S(2)}) collective-permute-start(f32[8,128,128]{2,1,0:T(8,128)S(1)} %get-tuple-element.81), channel_id=1, source_target_pairs={{0,2},{2,0},{4,6},{6,4},{8,10},{10,8},{12,14},{14,12},{16,18},{18,... | collective-permute-start | bytes 1572872 | tf_op jit(solution)/shard_map/ppermute | solution.py:187
  60.4 30.4 %collective-permute-start.11 = (f32[8,128,128]{2,1,0:T(8,128)S(1)}, f32[8,128,128]{2,1,0:T(8,128)S(1)}, u32[]{:S(2)}, u32[]{:S(2)}) collective-permute-start(f32[8,128,128]{2,1,0:T(8,128)S(1)} %get-tuple-element.79), channel_id=1, source_target_pairs={{0,30},{2,4},{4,2},{6,8},{8,6},{10,12},{12,10},{14,16},{16,14},{18... | collective-permute-start | bytes 1572872 | tf_op jit(solution)/shard_map/ppermute | solution.py:184
  62.7 31.4 %collective-permute-start.10 = (f32[8,128,128]{2,1,0:T(8,128)S(1)}, f32[8,128,128]{2,1,0:T(8,128)S(1)}, u32[]{:S(2)}, u32[]{:S(2)}) collective-permute-start(f32[8,128,128]{2,1,0:T(8,128)S(1)} %get-tuple-element.78), channel_id=1, source_target_pairs={{0,2},{2,0},{4,6},{6,4},{8,10},{10,8},{12,14},{14,12},{16,18},{18,... | collective-permute-start | bytes 1572872 | tf_op jit(solution)/shard_map/ppermute | solution.py:187
  62.7 31.4 %collective-permute-start.16 = (f32[8,128,128]{2,1,0:T(8,128)S(1)}, f32[8,128,128]{2,1,0:T(8,128)S(1)}, u32[]{:S(2)}, u32[]{:S(2)}) collective-permute-start(f32[8,128,128]{2,1,0:T(8,128)S(1)} %get-tuple-element.86), channel_id=1, source_target_pairs={{0,2},{2,0},{4,6},{6,4},{8,10},{10,8},{12,14},{14,12},{16,18},{18,... | collective-permute-start | bytes 1572872 | tf_op jit(solution)/shard_map/ppermute | solution.py:187
  64.8 31.6 %collective-permute-start.15 = (f32[8,128,128]{2,1,0:T(8,128)S(1)}, f32[8,128,128]{2,1,0:T(8,128)S(1)}, u32[]{:S(2)}, u32[]{:S(2)}) collective-permute-start(f32[8,128,128]{2,1,0:T(8,128)S(1)} %get-tuple-element.85), channel_id=1, source_target_pairs={{0,30},{2,4},{4,2},{6,8},{8,6},{10,12},{12,10},{14,16},{16,14},{18... | collective-permute-start | bytes 1572872 | tf_op jit(solution)/shard_map/ppermute | solution.py:184
  68.3 29.7 %collective-permute-start.23 = (f32[8,128,128]{2,1,0:T(8,128)}, f32[8,128,128]{2,1,0:T(8,128)S(1)}, u32[]{:S(2)}, u32[]{:S(2)}) collective-permute-start(f32[8,128,128]{2,1,0:T(8,128)} %get-tuple-element.96), channel_id=1, source_target_pairs={{0,2},{2,0},{4,6},{6,4},{8,10},{10,8},{12,14},{14,12},{16,18},{18,... | collective-permute-start | bytes 1572872 | tf_op jit(solution)/shard_map/ppermute | solution.py:187
  94.1 24.8 %collective-permute-start.19 = (f32[8,128,128]{2,1,0:T(8,128)}, f32[8,128,128]{2,1,0:T(8,128)S(1)}, u32[]{:S(2)}, u32[]{:S(2)}) collective-permute-start(f32[8,128,128]{2,1,0:T(8,128)} %get-tuple-element.91), channel_id=1, source_target_pairs={{0,30},{2,4},{4,2},{6,8},{8,6},{10,12},{12,10},{14,16},{16,14},{18... | collective-permute-start | bytes 1572872 | tf_op jit(solution)/shard_map/ppermute | solution.py:184
  94.2 26.4 %collective-permute-start.26 = (f32[8,128,128]{2,1,0:T(8,128)}, f32[8,128,128]{2,1,0:T(8,128)S(1)}, u32[]{:S(2)}, u32[]{:S(2)}) collective-permute-start(f32[8,128,128]{2,1,0:T(8,128)} %get-tuple-element.101), channel_id=1, source_target_pairs={{0,2},{2,0},{4,6},{6,4},{8,10},{10,8},{12,14},{14,12},{16,18},{18,... | collective-permute-start | bytes 1572872 | tf_op jit(solution)/shard_map/ppermute | solution.py:187
  96.4 32.0 %collective-permute-start.25 = (f32[8,128,128]{2,1,0:T(8,128)}, f32[8,128,128]{2,1,0:T(8,128)S(1)}, u32[]{:S(2)}, u32[]{:S(2)}) collective-permute-start(f32[8,128,128]{2,1,0:T(8,128)} %get-tuple-element.99), channel_id=1, source_target_pairs={{0,2},{2,0},{4,6},{6,4},{8,10},{10,8},{12,14},{14,12},{16,18},{18,... | collective-permute-start | bytes 1572872 | tf_op jit(solution)/shard_map/ppermute | solution.py:187
  98.0 32.2 %collective-permute-start.24 = (f32[8,128,128]{2,1,0:T(8,128)}, f32[8,128,128]{2,1,0:T(8,128)S(1)}, u32[]{:S(2)}, u32[]{:S(2)}) collective-permute-start(f32[8,128,128]{2,1,0:T(8,128)} %get-tuple-element.98), channel_id=1, source_target_pairs={{0,30},{2,4},{4,2},{6,8},{8,6},{10,12},{12,10},{14,16},{16,14},{18... | collective-permute-start | bytes 1572872 | tf_op jit(solution)/shard_map/ppermute | solution.py:184
  102.0 18.6 %collective-permute-start.14 = (f32[2,2,128,128]{3,2,1,0:T(8,128)S(1)}, f32[2,2,128,128]{3,2,1,0:T(8,128)S(1)}, u32[]{:S(2)}, u32[]{:S(2)}) collective-permute-start(f32[2,2,128,128]{3,2,1,0:T(8,128)S(1)} %get-tuple-element.83), channel_id=1, source_target_pairs={{0,1},{1,0},{2,3},{3,2},{4,5},{5,4},{6,7},{7,6},{8,9},{9,8},{10,11... | collective-permute-start | bytes 786440 | tf_op jit(solution)/shard_map/ppermute | solution.py:49
  118.9 27.5 %collective-permute-start.22 = (f32[8,128,128]{2,1,0:T(8,128)}, f32[8,128,128]{2,1,0:T(8,128)S(1)}, u32[]{:S(2)}, u32[]{:S(2)}) collective-permute-start(f32[8,128,128]{2,1,0:T(8,128)} %get-tuple-element.95), channel_id=1, source_target_pairs={{0,30},{2,4},{4,2},{6,8},{8,6},{10,12},{12,10},{14,16},{16,14},{18... | collective-permute-start | bytes 1572872 | tf_op jit(solution)/shard_map/ppermute | solution.py:184
  120.6 28.0 %collective-permute-start.21 = (f32[8,128,128]{2,1,0:T(8,128)}, f32[8,128,128]{2,1,0:T(8,128)S(1)}, u32[]{:S(2)}, u32[]{:S(2)}) collective-permute-start(f32[8,128,128]{2,1,0:T(8,128)} %get-tuple-element.93), channel_id=1, source_target_pairs={{0,2},{2,0},{4,6},{6,4},{8,10},{10,8},{12,14},{14,12},{16,18},{18,... | collective-permute-start | bytes 1572872 | tf_op jit(solution)/shard_map/ppermute | solution.py:187
  120.6 31.9 %collective-permute-start.20 = (f32[8,128,128]{2,1,0:T(8,128)}, f32[8,128,128]{2,1,0:T(8,128)S(1)}, u32[]{:S(2)}, u32[]{:S(2)}) collective-permute-start(f32[8,128,128]{2,1,0:T(8,128)} %get-tuple-element.92), channel_id=1, source_target_pairs={{0,30},{2,4},{4,2},{6,8},{8,6},{10,12},{12,10},{14,16},{16,14},{18... | collective-permute-start | bytes 1572872 | tf_op jit(solution)/shard_map/ppermute | solution.py:184
  128.3 29.8 %collective-permute-start.36 = (f32[8,128,128]{2,1,0:T(8,128)S(1)}, f32[8,128,128]{2,1,0:T(8,128)S(1)}, u32[]{:S(2)}, u32[]{:S(2)}) collective-permute-start(f32[8,128,128]{2,1,0:T(8,128)S(1)} %get-tuple-element.123), channel_id=1, source_target_pairs={{0,30},{2,4},{4,2},{6,8},{8,6},{10,12},{12,10},{14,16},{16,14},{18... | collective-permute-start | bytes 1572872 | tf_op jit(solution)/shard_map/ppermute | solution.py:184
  130.1 39.3 %collective-permute-start.28 = (f32[8,128,128]{2,1,0:T(8,128)}, f32[8,128,128]{2,1,0:T(8,128)S(1)}, u32[]{:S(2)}, u32[]{:S(2)}) collective-permute-start(f32[8,128,128]{2,1,0:T(8,128)} %get-tuple-element.108), channel_id=1, source_target_pairs={{0,30},{2,4},{4,2},{6,8},{8,6},{10,12},{12,10},{14,16},{16,14},{18... | collective-permute-start | bytes 1572872 | tf_op jit(solution)/shard_map/ppermute | solution.py:184
  156.1 15.1 %collective-permute-start.29 = (f32[8,128,128]{2,1,0:T(8,128)}, f32[8,128,128]{2,1,0:T(8,128)S(1)}, u32[]{:S(2)}, u32[]{:S(2)}) collective-permute-start(f32[8,128,128]{2,1,0:T(8,128)} %get-tuple-element.109), channel_id=1, source_target_pairs={{0,2},{2,0},{4,6},{6,4},{8,10},{10,8},{12,14},{14,12},{16,18},{18,... | collective-permute-start | bytes 1572872 | tf_op jit(solution)/shard_map/ppermute | solution.py:187
  156.1 23.8 %collective-permute-start.17 = (f32[8,128,128]{2,1,0:T(8,128)S(1)}, f32[8,128,128]{2,1,0:T(8,128)S(1)}, u32[]{:S(2)}, u32[]{:S(2)}) collective-permute-start(f32[8,128,128]{2,1,0:T(8,128)S(1)} %get-tuple-element.88), channel_id=1, source_target_pairs={{0,30},{2,4},{4,2},{6,8},{8,6},{10,12},{12,10},{14,16},{16,14},{18... | collective-permute-start | bytes 1572872 | tf_op jit(solution)/shard_map/ppermute | solution.py:184
  158.2 21.7 %collective-permute-start.18 = (f32[8,128,128]{2,1,0:T(8,128)S(1)}, f32[8,128,128]{2,1,0:T(8,128)S(1)}, u32[]{:S(2)}, u32[]{:S(2)}) collective-permute-start(f32[8,128,128]{2,1,0:T(8,128)S(1)} %get-tuple-element.89), channel_id=1, source_target_pairs={{0,2},{2,0},{4,6},{6,4},{8,10},{10,8},{12,14},{14,12},{16,18},{18,... | collective-permute-start | bytes 1572872 | tf_op jit(solution)/shard_map/ppermute | solution.py:187
  169.4 14.6 %collective-permute-start.37 = (f32[8,128,128]{2,1,0:T(8,128)S(1)}, f32[8,128,128]{2,1,0:T(8,128)S(1)}, u32[]{:S(2)}, u32[]{:S(2)}) collective-permute-start(f32[8,128,128]{2,1,0:T(8,128)S(1)} %get-tuple-element.124), channel_id=1, source_target_pairs={{0,2},{2,0},{4,6},{6,4},{8,10},{10,8},{12,14},{14,12},{16,18},{18,... | collective-permute-start | bytes 1572872 | tf_op jit(solution)/shard_map/ppermute | solution.py:187
  169.4 28.1 %collective-permute-start.34 = (f32[8,128,128]{2,1,0:T(8,128)S(1)}, f32[8,128,128]{2,1,0:T(8,128)S(1)}, u32[]{:S(2)}, u32[]{:S(2)}) collective-permute-start(f32[8,128,128]{2,1,0:T(8,128)S(1)} %get-tuple-element.120), channel_id=1, source_target_pairs={{0,30},{2,4},{4,2},{6,8},{8,6},{10,12},{12,10},{14,16},{16,14},{18... | collective-permute-start | bytes 1572872 | tf_op jit(solution)/shard_map/ppermute | solution.py:184
  171.2 29.7 %collective-permute-start.35 = (f32[8,128,128]{2,1,0:T(8,128)S(1)}, f32[8,128,128]{2,1,0:T(8,128)S(1)}, u32[]{:S(2)}, u32[]{:S(2)}) collective-permute-start(f32[8,128,128]{2,1,0:T(8,128)S(1)} %get-tuple-element.121), channel_id=1, source_target_pairs={{0,2},{2,0},{4,6},{6,4},{8,10},{10,8},{12,14},{14,12},{16,18},{18,... | collective-permute-start | bytes 1572872 | tf_op jit(solution)/shard_map/ppermute | solution.py:187
  179.9 22.6 %collective-permute-start.33 = (f32[8,128,128]{2,1,0:T(8,128)S(1)}, f32[8,128,128]{2,1,0:T(8,128)S(1)}, u32[]{:S(2)}, u32[]{:S(2)}) collective-permute-start(f32[8,128,128]{2,1,0:T(8,128)S(1)} %get-tuple-element.118), channel_id=1, source_target_pairs={{0,2},{2,0},{4,6},{6,4},{8,10},{10,8},{12,14},{14,12},{16,18},{18,... | collective-permute-start | bytes 1572872 | tf_op jit(solution)/shard_map/ppermute | solution.py:187
  179.9 23.2 %collective-permute-start.32 = (f32[8,128,128]{2,1,0:T(8,128)S(1)}, f32[8,128,128]{2,1,0:T(8,128)S(1)}, u32[]{:S(2)}, u32[]{:S(2)}) collective-permute-start(f32[8,128,128]{2,1,0:T(8,128)S(1)} %get-tuple-element.117), channel_id=1, source_target_pairs={{0,30},{2,4},{4,2},{6,8},{8,6},{10,12},{12,10},{14,16},{16,14},{18... | collective-permute-start | bytes 1572872 | tf_op jit(solution)/shard_map/ppermute | solution.py:184
  184.1 20.7 %collective-permute-start.31 = (f32[8,128,128]{2,1,0:T(8,128)S(1)}, f32[8,128,128]{2,1,0:T(8,128)S(1)}, u32[]{:S(2)}, u32[]{:S(2)}) collective-permute-start(f32[8,128,128]{2,1,0:T(8,128)S(1)} %get-tuple-element.115), channel_id=1, source_target_pairs={{0,2},{2,0},{4,6},{6,4},{8,10},{10,8},{12,14},{14,12},{16,18},{18,... | collective-permute-start | bytes 1572872 | tf_op jit(solution)/shard_map/ppermute | solution.py:187
  (13 other events, 205.1 us)

commit v5 on v4

--- a/solution.py
+++ b/solution.py
@@ -19,7 +19,7 @@
 NEAR_LAG = 16
 FIRST = True
 BACK_GROUPS = (1, 1, 1, 1, 1, 1)
-AHEAD = 3
+AHEAD = 2
 CARRY = True
 EARLY = True
 FAR_FIRST = 2

time: 211 us -> 212 us (level)
  waiting for transfers between devices: 117 us -> 126 us
  starting transfers between devices: 48.8 us -> 40.1 us
    ppermute x17, waiting for transfers between devices: 114 us -> 123 us  [send_far(): return lax.ppermute(plane, 'gz', outer_pairs(ring))]
    ppermute x18, starting transfers between devices: 19.3 us -> 13.3 us  [send_near(): return lax.ppermute(plane, 'gz', inner_pairs(ring))]
    ppermute x17, starting transfers between devices: 25.6 us -> 23 us  [send_far(): return lax.ppermute(plane, 'gz', outer_pairs(ring))]
  transfers between devices with their start and end apart: 38 -> 38, of which waited for: 15 -> 14; matrix products, arithmetic and copies ran while one was open for 3% -> 3% of each run, Pallas kernels for 15% -> 15%
where the time goes in v5:
time: 212 us
  waiting for transfers between devices  126 us (59%)
  starting transfers between devices  40.1 us (19%)
  Pallas kernels  34.2 us (16%)
  local copies, waits for them, and re-layouts  10.7 us (5%)
    ppermute x17, waiting for transfers between devices, send_far(): return lax.ppermute(plane, 'gz', outer_pairs(ring))  123 us
    pallas_call x18, Pallas kernels, call(): pl.pallas_call(functools.partial(kernel, piece * size, planes, coupling,...  34.2 us
    ppermute x17, starting transfers between devices, send_far(): return lax.ppermute(plane, 'gz', outer_pairs(ring))  23 us
    ppermute x18, starting transfers between devices, send_near(): return lax.ppermute(plane, 'gz', inner_pairs(ring))  13.3 us
    reshape x3, local copies, waits for them, and re-layouts, cut(): lax.dynamic_slice(array, (start, plane, 0, 0), (length, 1, rows, columns))  7.91 us
  transfers between devices with their start and end apart: 38, of which 14 were waited for; matrix products, arithmetic and copies ran while one was open for 3% of the time, Pallas kernels for 15%

profile of v5, /device:TPU:1, one launch (start us, length us, event | category | flops | bytes accessed | tf_op | source)
XLA Modules:
  0.0 211.6 jit_solution(8274782151277835452)
XLA Ops:
  0.0 2.4 %dynamic-slice_bitcast_fusion = f32[16,128,128]{2,1,0:T(8,128)} fusion(f32[48,2,128,128]{3,2,1,0:T(8,128)} %field.35, s32[]{:T(128)S(6)} %select_n.4), kind=kLoop, calls=%fused_computation.1 | loop fusion | bytes 2097156 | tf_op jit(solution)/shard_map/reshape | solution.py:190
  2.4 2.6 %collective-permute-start.3 = (f32[16,128,128]{2,1,0:T(8,128)}, f32[16,128,128]{2,1,0:T(8,128)S(1)}, u32[]{:S(2)}, u32[]{:S(2)}) collective-permute-start(f32[16,128,128]{2,1,0:T(8,128)} %dynamic-slice_bitcast_fusion), channel_id=1, source_target_pairs={{0,30},{2,4},{4,2},{6,8},{8,6},{10,12},{12,10},{14,16},{16,14},{18... | collective-permute-start | bytes 3145736 | tf_op jit(solution)/shard_map/ppermute | solution.py:184
  5.1 3.2 %dynamic-slice_bitcast_fusion.11 = (f32[8,128,128]{2,1,0:T(8,128)S(1)}, f32[8,128,128]{2,1,0:T(8,128)S(1)}, f32[8,128,128]{2,1,0:T(8,128)S(1)}, f32[8,128,128]{2...) fusion(f32[48,2,128,128]{3,2,1,0:T(8,128)} %field.35, ...), kind=kLoop, calls=%fused_computation.12 | loop fusion | bytes 10485768 | tf_op jit(solution)/shard_map/reshape | solution.py:190
  8.3 2.9 %collective-permute-start.1 = (f32[8,128,128]{2,1,0:T(8,128)S(1)}, f32[8,128,128]{2,1,0:T(8,128)S(1)}, u32[]{:S(2)}, u32[]{:S(2)}) collective-permute-start(f32[8,128,128]{2,1,0:T(8,128)S(1)} %get-tuple-element.68), channel_id=1, source_target_pairs={{0,2},{2,0},{4,6},{6,4},{8,10},{10,8},{12,14},{14,12},{16,18},{18,... | collective-permute-start | bytes 1572872 | tf_op jit(solution)/shard_map/ppermute | solution.py:187
  13.8 2.6 %collective-permute-done.2 = f32[2,128,128]{2,1,0:T(8,128)S(1)} collective-permute-done((f32[2,128,128]{2,1,0:T(8,128)S(1)}, f32[2,128,128]{2,1,0:T(8,128)S(1)}, u32[]{:S(2)}, u32[]{:S(2)}) %collective-permute-start.2) | collective-permute-done | bytes 131104 | tf_op jit(solution)/shard_map/ppermute | solution.py:49
  16.5 18.1 %collective-permute-done.3.far = f32[16,128,128]{2,1,0:T(8,128)S(1)} collective-permute-done((f32[16,128,128]{2,1,0:T(8,128)}, f32[16,128,128]{2,1,0:T(8,128)S(1)}, u32[]{:S(2)}, u32[]{:S(2)}) %collective-permute-start.3) | collective-permute-done | bytes 1048608 | tf_op jit(solution)/shard_map/ppermute | solution.py:184
  34.6 1.7 collective-permute-start.9
  36.4 3.5 %collective-permute-start.10 = (f32[8,128,128]{2,1,0:T(8,128)S(1)}, f32[8,128,128]{2,1,0:T(8,128)S(1)}, u32[]{:S(2)}, u32[]{:S(2)}) collective-permute-start(f32[8,128,128]{2,1,0:T(8,128)S(1)} %get-tuple-element.78), channel_id=1, source_target_pairs={{0,2},{2,0},{4,6},{6,4},{8,10},{10,8},{12,14},{14,12},{16,18},{18,... | collective-permute-start | bytes 1572872 | tf_op jit(solution)/shard_map/ppermute | solution.py:187
  39.9 2.8 %copy-done = f32[48,2,128,128]{3,2,1,0:T(8,128)S(1)} copy-done((f32[48,2,128,128]{3,2,1,0:T(8,128)S(1)}, f32[48,2,128,128]{3,2,1,0:T(8,128)}, u32[]{:S(2)}) %copy-start) | copy-done | bytes 6291480
  44.4 12.0 %collective-permute-done.far = f32[8,128,128]{2,1,0:T(8,128)S(1)} collective-permute-done((f32[8,128,128]{2,1,0:T(8,128)S(1)}, f32[8,128,128]{2,1,0:T(8,128)S(1)}, u32[]{:S(2)}, u32[]{:S(2)}) %collective-permute-start) | collective-permute-done | bytes 524320 | tf_op jit(solution)/shard_map/ppermute | solution.py:184
  56.3 2.5 %collective-permute-start.7 = (f32[8,128,128]{2,1,0:T(8,128)S(1)}, f32[8,128,128]{2,1,0:T(8,128)S(1)}, u32[]{:S(2)}, u32[]{:S(2)}) collective-permute-start(f32[8,128,128]{2,1,0:T(8,128)S(1)} %get-tuple-element.75), channel_id=1, source_target_pairs={{0,30},{2,4},{4,2},{6,8},{8,6},{10,12},{12,10},{14,16},{16,14},{18... | collective-permute-start | bytes 1572872 | tf_op jit(solution)/shard_map/ppermute | solution.py:184
  60.5 2.2 %dynamic-slice_bitcast_fusion.1 = (f32[8,128,128]{2,1,0:T(8,128)}, f32[8,128,128]{2,1,0:T(8,128)}, f32[8,128,128]{2,1,0:T(8,128)}, f32[8,128,128]{2,1,0:T(8,128)...) fusion(f32[48,2,128,128]{3,2,1,0:T(8,128)S(1)} %copy-done, ...), kind=kLoop, calls=%fused_computation.2 | loop fusion | bytes 12582920 | tf_op jit(solution)/shard_map/reshape | solution.py:190
  64.3 1.8 collective-permute-start.17
  66.1 3.5 %collective-permute-start.16 = (f32[8,128,128]{2,1,0:T(8,128)S(1)}, f32[8,128,128]{2,1,0:T(8,128)S(1)}, u32[]{:S(2)}, u32[]{:S(2)}) collective-permute-start(f32[8,128,128]{2,1,0:T(8,128)S(1)} %get-tuple-element.88), channel_id=1, source_target_pairs={{0,2},{2,0},{4,6},{6,4},{8,10},{10,8},{12,14},{14,12},{16,18},{18,... | collective-permute-start | bytes 1572872 | tf_op jit(solution)/shard_map/ppermute | solution.py:187
  71.3 19.5 %collective-permute-done.6.far = f32[8,128,128]{2,1,0:T(8,128)S(1)} collective-permute-done((f32[8,128,128]{2,1,0:T(8,128)S(1)}, f32[8,128,128]{2,1,0:T(8,128)S(1)}, u32[]{:S(2)}, u32[]{:S(2)}) %collective-permute-start.6) | collective-permute-done | bytes 524320 | tf_op jit(solution)/shard_map/ppermute | solution.py:184
  94.2 2.2 %collective-permute-done.17.far = f32[8,128,128]{2,1,0:T(8,128)S(1)} collective-permute-done((f32[8,128,128]{2,1,0:T(8,128)S(1)}, f32[8,128,128]{2,1,0:T(8,128)S(1)}, u32[]{:S(2)}, u32[]{:S(2)}) %collective-permute-start.17) | collective-permute-done | bytes 524320 | tf_op jit(solution)/shard_map/ppermute | solution.py:184
  103.2 15.6 %collective-permute-done.11.far = f32[8,128,128]{2,1,0:T(8,128)S(1)} collective-permute-done((f32[8,128,128]{2,1,0:T(8,128)}, f32[8,128,128]{2,1,0:T(8,128)S(1)}, u32[]{:S(2)}, u32[]{:S(2)}) %collective-permute-start.11) | collective-permute-done | bytes 524320 | tf_op jit(solution)/shard_map/ppermute | solution.py:184
  120.8 3.0 %shard_map.52 = (f32[8,128,128]{2,1,0:T(8,128)}, f32[8,128,128]{2,1,0:T(8,128)}, f32[8,2,128,128]{3,2,1,0:T(8,128)S(1)}, f32[2,128,128]{2,1,0:T(8,128)S(1)}) custom-call(s32[1]{0:T(128)} %bitcast.odd_ref, f32[48]{0:T(128)S(1)} %copy-done.1, f32[48]{0:T(128)S(1)} %copy-done.2, f32[48,2,128,128]{3,2,1,0:T(8,128)S(1)} %bitcast.48, ...), custom_call_target="tpu_custom_call" | custom-call | flops 7864320 | bytes 5242880 | tf_op jit(solution)/shard_map/pallas_call | solution.py:218
  125.5 9.5 %collective-permute-done.25.far = f32[8,128,128]{2,1,0:T(8,128)S(1)} collective-permute-done((f32[8,128,128]{2,1,0:T(8,128)S(1)}, f32[8,128,128]{2,1,0:T(8,128)S(1)}, u32[]{:S(2)}, u32[]{:S(2)}) %collective-permute-start.25) | collective-permute-done | bytes 524320 | tf_op jit(solution)/shard_map/ppermute | solution.py:184
  135.0 2.9 %shard_map.53 = (f32[8,128,128]{2,1,0:T(8,128)S(1)}, f32[8,128,128]{2,1,0:T(8,128)}, f32[8,2,128,128]{3,2,1,0:T(8,128)S(1)}, f32[2,128,128]{2,1,0:T(8,128)S(1)}) custom-call(s32[1]{0:T(128)} %bitcast.odd_ref, f32[48]{0:T(128)S(1)} %copy-done.1, f32[48]{0:T(128)S(1)} %copy-done.2, f32[48,2,128,128]{3,2,1,0:T(8,128)S(1)} %bitcast.48, ...), custom_call_target="tpu_custom_call", output_to_operand_aliasing={{3}: (10, {})} | custom-call | flops 7864320 | bytes 5242880 | tf_op jit(solution)/shard_map/pallas_call | solution.py:218
  137.9 2.3 %shard_map.54 = (f32[8,128,128]{2,1,0:T(8,128)S(1)}, f32[8,128,128]{2,1,0:T(8,128)S(1)}, f32[8,2,128,128]{3,2,1,0:T(8,128)S(1)}, f32[2,128,128]{2,1,0:T(8,128)S(1)}) custom-call(s32[1]{0:T(128)} %bitcast.odd_ref, f32[48]{0:T(128)S(1)} %copy-done.1, f32[48]{0:T(128)S(1)} %copy-done.2, ...), custom_call_target="tpu_custom_call", output_to_operand_aliasing={{3}: (10, {})} | custom-call | flops 7864320 | bytes 5242880 | tf_op jit(solution)/shard_map/pallas_call | solution.py:218
  140.1 2.3 %shard_map.55 = (f32[8,128,128]{2,1,0:T(8,128)S(1)}, f32[8,128,128]{2,1,0:T(8,128)S(1)}, f32[8,2,128,128]{3,2,1,0:T(8,128)S(1)}, f32[2,128,128]{2,1,0:T(8,128)S(1)}) custom-call(s32[1]{0:T(128)} %bitcast.odd_ref, f32[48]{0:T(128)S(1)} %copy-done.1, f32[48]{0:T(128)S(1)} %copy-done.2, ...), custom_call_target="tpu_custom_call", output_to_operand_aliasing={{3}: (10, {})} | custom-call | flops 7864320 | bytes 5242880 | tf_op jit(solution)/shard_map/pallas_call | solution.py:218
  142.4 2.3 %shard_map.56 = (f32[8,128,128]{2,1,0:T(8,128)S(1)}, f32[8,128,128]{2,1,0:T(8,128)S(1)}, f32[8,2,128,128]{3,2,1,0:T(8,128)S(1)}, f32[2,128,128]{2,1,0:T(8,128)S(1)}) custom-call(s32[1]{0:T(128)} %bitcast.odd_ref, f32[48]{0:T(128)S(1)} %copy-done.1, f32[48]{0:T(128)S(1)} %copy-done.2, ...), custom_call_target="tpu_custom_call", output_to_operand_aliasing={{3}: (10, {})} | custom-call | flops 7864320 | bytes 5242880 | tf_op jit(solution)/shard_map/pallas_call | solution.py:218
  144.8 2.2 %collective-permute-done.21.far = f32[8,128,128]{2,1,0:T(8,128)S(1)} collective-permute-done((f32[8,128,128]{2,1,0:T(8,128)}, f32[8,128,128]{2,1,0:T(8,128)S(1)}, u32[]{:S(2)}, u32[]{:S(2)}) %collective-permute-start.21) | collective-permute-done | bytes 524320 | tf_op jit(solution)/shard_map/ppermute | solution.py:184
  146.9 2.3 %shard_map.57 = (f32[8,128,128]{2,1,0:T(8,128)S(1)}, f32[8,128,128]{2,1,0:T(8,128)S(1)}, f32[8,2,128,128]{3,2,1,0:T(8,128)S(1)}, f32[2,128,128]{2,1,0:T(8,128)S(1)}) custom-call(s32[1]{0:T(128)} %bitcast.odd_ref, f32[48]{0:T(128)S(1)} %copy-done.1, f32[48]{0:T(128)S(1)} %copy-done.2, ...), custom_call_target="tpu_custom_call", output_to_operand_aliasing={{3}: (10, {})} | custom-call | flops 7864320 | bytes 5242880 | tf_op jit(solution)/shard_map/pallas_call | solution.py:218
  150.5 2.0 collective-permute-start.28
  154.3 1.8 collective-permute-start.20
  157.9 12.7 %collective-permute-done.28.far = f32[8,128,128]{2,1,0:T(8,128)S(1)} collective-permute-done((f32[8,128,128]{2,1,0:T(8,128)S(1)}, f32[8,128,128]{2,1,0:T(8,128)S(1)}, u32[]{:S(2)}, u32[]{:S(2)}) %collective-permute-start.28) | collective-permute-done | bytes 524320 | tf_op jit(solution)/shard_map/ppermute | solution.py:184
  173.9 8.2 %collective-permute-done.19.far = f32[8,128,128]{2,1,0:T(8,128)S(1)} collective-permute-done((f32[8,128,128]{2,1,0:T(8,128)S(1)}, f32[8,128,128]{2,1,0:T(8,128)S(1)}, u32[]{:S(2)}, u32[]{:S(2)}) %collective-permute-start.19) | collective-permute-done | bytes 524320 | tf_op jit(solution)/shard_map/ppermute | solution.py:184
  185.5 12.4 %collective-permute-done.36.far = f32[8,128,128]{2,1,0:T(8,128)S(1)} collective-permute-done((f32[8,128,128]{2,1,0:T(8,128)S(1)}, f32[8,128,128]{2,1,0:T(8,128)S(1)}, u32[]{:S(2)}, u32[]{:S(2)}) %collective-permute-start.36) | collective-permute-done | bytes 524320 | tf_op jit(solution)/shard_map/ppermute | solution.py:184
  199.5 4.8 %collective-permute-done.34.far = f32[8,128,128]{2,1,0:T(8,128)S(1)} collective-permute-done((f32[8,128,128]{2,1,0:T(8,128)S(1)}, f32[8,128,128]{2,1,0:T(8,128)S(1)}, u32[]{:S(2)}, u32[]{:S(2)}) %collective-permute-start.34) | collective-permute-done | bytes 524320 | tf_op jit(solution)/shard_map/ppermute | solution.py:184
  206.0 4.0 %collective-permute-done.32.far = f32[8,128,128]{2,1,0:T(8,128)S(1)} collective-permute-done((f32[8,128,128]{2,1,0:T(8,128)S(1)}, f32[8,128,128]{2,1,0:T(8,128)S(1)}, u32[]{:S(2)}, u32[]{:S(2)}) %collective-permute-start.32) | collective-permute-done | bytes 524320 | tf_op jit(solution)/shard_map/ppermute | solution.py:184
  (87 shorter events, 39.5 us)
Async XLA Ops:
  2.4 32.1 %collective-permute-start.3 = (f32[16,128,128]{2,1,0:T(8,128)}, f32[16,128,128]{2,1,0:T(8,128)S(1)}, u32[]{:S(2)}, u32[]{:S(2)}) collective-permute-start(f32[16,128,128]{2,1,0:T(8,128)} %dynamic-slice_bitcast_fusion), channel_id=1, source_target_pairs={{0,30},{2,4},{4,2},{6,8},{8,6},{10,12},{12,10},{14,16},{16,14},{18... | collective-permute-start | bytes 3145736 | tf_op jit(solution)/shard_map/ppermute | solution.py:184
  8.3 26.3 %collective-permute-start.1 = (f32[8,128,128]{2,1,0:T(8,128)S(1)}, f32[8,128,128]{2,1,0:T(8,128)S(1)}, u32[]{:S(2)}, u32[]{:S(2)}) collective-permute-start(f32[8,128,128]{2,1,0:T(8,128)S(1)} %get-tuple-element.68), channel_id=1, source_target_pairs={{0,2},{2,0},{4,6},{6,4},{8,10},{10,8},{12,14},{14,12},{16,18},{18,... | collective-permute-start | bytes 1572872 | tf_op jit(solution)/shard_map/ppermute | solution.py:187
  13.1 23.2 %collective-permute-start.5 = (f32[8,128,128]{2,1,0:T(8,128)S(1)}, f32[8,128,128]{2,1,0:T(8,128)S(1)}, u32[]{:S(2)}, u32[]{:S(2)}) collective-permute-start(f32[8,128,128]{2,1,0:T(8,128)S(1)} %get-tuple-element.70), channel_id=1, source_target_pairs={{0,2},{2,0},{4,6},{6,4},{8,10},{10,8},{12,14},{14,12},{16,18},{18,... | collective-permute-start | bytes 1572872 | tf_op jit(solution)/shard_map/ppermute | solution.py:187
  13.8 30.4 %collective-permute-start.4 = (f32[8,128,128]{2,1,0:T(8,128)S(1)}, f32[8,128,128]{2,1,0:T(8,128)S(1)}, u32[]{:S(2)}, u32[]{:S(2)}) collective-permute-start(f32[8,128,128]{2,1,0:T(8,128)S(1)} %get-tuple-element.69), channel_id=1, source_target_pairs={{0,2},{2,0},{4,6},{6,4},{8,10},{10,8},{12,14},{14,12},{16,18},{18,... | collective-permute-start | bytes 1572872 | tf_op jit(solution)/shard_map/ppermute | solution.py:187
  16.5 39.9 %collective-permute-start = (f32[8,128,128]{2,1,0:T(8,128)S(1)}, f32[8,128,128]{2,1,0:T(8,128)S(1)}, u32[]{:S(2)}, u32[]{:S(2)}) collective-permute-start(f32[8,128,128]{2,1,0:T(8,128)S(1)} %get-tuple-element.152), channel_id=1, source_target_pairs={{0,30},{2,4},{4,2},{6,8},{8,6},{10,12},{12,10},{14,16},{16,14},{18... | collective-permute-start | bytes 1572872 | tf_op jit(solution)/shard_map/ppermute | solution.py:184
  34.6 25.8 %collective-permute-start.8 = (f32[8,128,128]{2,1,0:T(8,128)S(1)}, f32[8,128,128]{2,1,0:T(8,128)S(1)}, u32[]{:S(2)}, u32[]{:S(2)}) collective-permute-start(f32[8,128,128]{2,1,0:T(8,128)S(1)} %get-tuple-element.76), channel_id=1, source_target_pairs={{0,2},{2,0},{4,6},{6,4},{8,10},{10,8},{12,14},{14,12},{16,18},{18,... | collective-permute-start | bytes 1572872 | tf_op jit(solution)/shard_map/ppermute | solution.py:187
  34.6 28.1 %collective-permute-start.9 = (f32[8,128,128]{2,1,0:T(8,128)S(1)}, f32[8,128,128]{2,1,0:T(8,128)S(1)}, u32[]{:S(2)}, u32[]{:S(2)}) collective-permute-start(f32[8,128,128]{2,1,0:T(8,128)S(1)} %get-tuple-element.77), channel_id=1, source_target_pairs={{0,30},{2,4},{4,2},{6,8},{8,6},{10,12},{12,10},{14,16},{16,14},{18... | collective-permute-start | bytes 1572872 | tf_op jit(solution)/shard_map/ppermute | solution.py:184
  36.4 27.9 %collective-permute-start.10 = (f32[8,128,128]{2,1,0:T(8,128)S(1)}, f32[8,128,128]{2,1,0:T(8,128)S(1)}, u32[]{:S(2)}, u32[]{:S(2)}) collective-permute-start(f32[8,128,128]{2,1,0:T(8,128)S(1)} %get-tuple-element.78), channel_id=1, source_target_pairs={{0,2},{2,0},{4,6},{6,4},{8,10},{10,8},{12,14},{14,12},{16,18},{18,... | collective-permute-start | bytes 1572872 | tf_op jit(solution)/shard_map/ppermute | solution.py:187
  44.3 21.8 %collective-permute-start.13 = (f32[8,128,128]{2,1,0:T(8,128)S(1)}, f32[8,128,128]{2,1,0:T(8,128)S(1)}, u32[]{:S(2)}, u32[]{:S(2)}) collective-permute-start(f32[8,128,128]{2,1,0:T(8,128)S(1)} %get-tuple-element.84), channel_id=1, source_target_pairs={{0,2},{2,0},{4,6},{6,4},{8,10},{10,8},{12,14},{14,12},{16,18},{18,... | collective-permute-start | bytes 1572872 | tf_op jit(solution)/shard_map/ppermute | solution.py:187
  60.4 30.4 %collective-permute-start.6 = (f32[8,128,128]{2,1,0:T(8,128)S(1)}, f32[8,128,128]{2,1,0:T(8,128)S(1)}, u32[]{:S(2)}, u32[]{:S(2)}) collective-permute-start(f32[8,128,128]{2,1,0:T(8,128)S(1)} %get-tuple-element.74), channel_id=1, source_target_pairs={{0,30},{2,4},{4,2},{6,8},{8,6},{10,12},{12,10},{14,16},{16,14},{18... | collective-permute-start | bytes 1572872 | tf_op jit(solution)/shard_map/ppermute | solution.py:184
  62.7 31.4 %collective-permute-start.12 = (f32[8,128,128]{2,1,0:T(8,128)S(1)}, f32[8,128,128]{2,1,0:T(8,128)S(1)}, u32[]{:S(2)}, u32[]{:S(2)}) collective-permute-start(f32[8,128,128]{2,1,0:T(8,128)S(1)} %get-tuple-element.83), channel_id=1, source_target_pairs={{0,2},{2,0},{4,6},{6,4},{8,10},{10,8},{12,14},{14,12},{16,18},{18,... | collective-permute-start | bytes 1572872 | tf_op jit(solution)/shard_map/ppermute | solution.py:187
  64.3 32.1 %collective-permute-start.17 = (f32[8,128,128]{2,1,0:T(8,128)S(1)}, f32[8,128,128]{2,1,0:T(8,128)S(1)}, u32[]{:S(2)}, u32[]{:S(2)}) collective-permute-start(f32[8,128,128]{2,1,0:T(8,128)S(1)} %get-tuple-element.90), channel_id=1, source_target_pairs={{0,30},{2,4},{4,2},{6,8},{8,6},{10,12},{12,10},{14,16},{16,14},{18... | collective-permute-start | bytes 1572872 | tf_op jit(solution)/shard_map/ppermute | solution.py:184
  66.1 31.9 %collective-permute-start.16 = (f32[8,128,128]{2,1,0:T(8,128)S(1)}, f32[8,128,128]{2,1,0:T(8,128)S(1)}, u32[]{:S(2)}, u32[]{:S(2)}) collective-permute-start(f32[8,128,128]{2,1,0:T(8,128)S(1)} %get-tuple-element.88), channel_id=1, source_target_pairs={{0,2},{2,0},{4,6},{6,4},{8,10},{10,8},{12,14},{14,12},{16,18},{18,... | collective-permute-start | bytes 1572872 | tf_op jit(solution)/shard_map/ppermute | solution.py:187
  69.6 28.9 %collective-permute-start.18 = (f32[8,128,128]{2,1,0:T(8,128)}, f32[8,128,128]{2,1,0:T(8,128)S(1)}, u32[]{:S(2)}, u32[]{:S(2)}) collective-permute-start(f32[8,128,128]{2,1,0:T(8,128)} %get-tuple-element.91), channel_id=1, source_target_pairs={{0,2},{2,0},{4,6},{6,4},{8,10},{10,8},{12,14},{14,12},{16,18},{18,... | collective-permute-start | bytes 1572872 | tf_op jit(solution)/shard_map/ppermute | solution.py:187
  94.1 24.8 %collective-permute-start.11 = (f32[8,128,128]{2,1,0:T(8,128)}, f32[8,128,128]{2,1,0:T(8,128)S(1)}, u32[]{:S(2)}, u32[]{:S(2)}) collective-permute-start(f32[8,128,128]{2,1,0:T(8,128)} %get-tuple-element.82), channel_id=1, source_target_pairs={{0,30},{2,4},{4,2},{6,8},{8,6},{10,12},{12,10},{14,16},{16,14},{18... | collective-permute-start | bytes 1572872 | tf_op jit(solution)/shard_map/ppermute | solution.py:184
  96.4 24.2 %collective-permute-start.24 = (f32[8,128,128]{2,1,0:T(8,128)}, f32[8,128,128]{2,1,0:T(8,128)S(1)}, u32[]{:S(2)}, u32[]{:S(2)}) collective-permute-start(f32[8,128,128]{2,1,0:T(8,128)} %get-tuple-element.101), channel_id=1, source_target_pairs={{0,2},{2,0},{4,6},{6,4},{8,10},{10,8},{12,14},{14,12},{16,18},{18,... | collective-permute-start | bytes 1572872 | tf_op jit(solution)/shard_map/ppermute | solution.py:187
  98.0 25.8 %collective-permute-start.26 = (f32[8,128,128]{2,1,0:T(8,128)}, f32[8,128,128]{2,1,0:T(8,128)S(1)}, u32[]{:S(2)}, u32[]{:S(2)}) collective-permute-start(f32[8,128,128]{2,1,0:T(8,128)} %get-tuple-element.104), channel_id=1, source_target_pairs={{0,2},{2,0},{4,6},{6,4},{8,10},{10,8},{12,14},{14,12},{16,18},{18,... | collective-permute-start | bytes 1572872 | tf_op jit(solution)/shard_map/ppermute | solution.py:187
  98.5 36.4 %collective-permute-start.25 = (f32[8,128,128]{2,1,0:T(8,128)S(1)}, f32[8,128,128]{2,1,0:T(8,128)S(1)}, u32[]{:S(2)}, u32[]{:S(2)}) collective-permute-start(f32[8,128,128]{2,1,0:T(8,128)S(1)} %copy-done.3), channel_id=1, source_target_pairs={{0,30},{2,4},{4,2},{6,8},{8,6},{10,12},{12,10},{14,16},{16,14},{18... | collective-permute-start | bytes 1572872 | tf_op jit(solution)/shard_map/ppermute | solution.py:184
  102.0 18.6 %collective-permute-start.14 = (f32[2,2,128,128]{3,2,1,0:T(8,128)S(1)}, f32[2,2,128,128]{3,2,1,0:T(8,128)S(1)}, u32[]{:S(2)}, u32[]{:S(2)}) collective-permute-start(f32[2,2,128,128]{3,2,1,0:T(8,128)S(1)} %get-tuple-element.85), channel_id=1, source_target_pairs={{0,1},{1,0},{2,3},{3,2},{4,5},{5,4},{6,7},{7,6},{8,9},{9,8},{10,11... | collective-permute-start | bytes 786440 | tf_op jit(solution)/shard_map/ppermute | solution.py:49
  118.9 23.6 %collective-permute-start.23 = (f32[8,128,128]{2,1,0:T(8,128)}, f32[8,128,128]{2,1,0:T(8,128)S(1)}, u32[]{:S(2)}, u32[]{:S(2)}) collective-permute-start(f32[8,128,128]{2,1,0:T(8,128)} %get-tuple-element.100), channel_id=1, source_target_pairs={{0,30},{2,4},{4,2},{6,8},{8,6},{10,12},{12,10},{14,16},{16,14},{18... | collective-permute-start | bytes 1572872 | tf_op jit(solution)/shard_map/ppermute | solution.py:184
  120.6 24.1 %collective-permute-start.22 = (f32[8,128,128]{2,1,0:T(8,128)}, f32[8,128,128]{2,1,0:T(8,128)S(1)}, u32[]{:S(2)}, u32[]{:S(2)}) collective-permute-start(f32[8,128,128]{2,1,0:T(8,128)} %get-tuple-element.98), channel_id=1, source_target_pairs={{0,2},{2,0},{4,6},{6,4},{8,10},{10,8},{12,14},{14,12},{16,18},{18,... | collective-permute-start | bytes 1572872 | tf_op jit(solution)/shard_map/ppermute | solution.py:187
  120.6 26.3 %collective-permute-start.21 = (f32[8,128,128]{2,1,0:T(8,128)}, f32[8,128,128]{2,1,0:T(8,128)S(1)}, u32[]{:S(2)}, u32[]{:S(2)}) collective-permute-start(f32[8,128,128]{2,1,0:T(8,128)} %get-tuple-element.97), channel_id=1, source_target_pairs={{0,30},{2,4},{4,2},{6,8},{8,6},{10,12},{12,10},{14,16},{16,14},{18... | collective-permute-start | bytes 1572872 | tf_op jit(solution)/shard_map/ppermute | solution.py:184
  123.8 28.8 %collective-permute-start.30 = (f32[8,128,128]{2,1,0:T(8,128)}, f32[8,128,128]{2,1,0:T(8,128)S(1)}, u32[]{:S(2)}, u32[]{:S(2)}) collective-permute-start(f32[8,128,128]{2,1,0:T(8,128)} %get-tuple-element.113), channel_id=1, source_target_pairs={{0,30},{2,4},{4,2},{6,8},{8,6},{10,12},{12,10},{14,16},{16,14},{18... | collective-permute-start | bytes 1572872 | tf_op jit(solution)/shard_map/ppermute | solution.py:184
  135.0 19.3 %collective-permute-start.31 = (f32[8,128,128]{2,1,0:T(8,128)}, f32[8,128,128]{2,1,0:T(8,128)S(1)}, u32[]{:S(2)}, u32[]{:S(2)}) collective-permute-start(f32[8,128,128]{2,1,0:T(8,128)} %get-tuple-element.114), channel_id=1, source_target_pairs={{0,2},{2,0},{4,6},{6,4},{8,10},{10,8},{12,14},{14,12},{16,18},{18,... | collective-permute-start | bytes 1572872 | tf_op jit(solution)/shard_map/ppermute | solution.py:187
  150.5 20.1 %collective-permute-start.28 = (f32[8,128,128]{2,1,0:T(8,128)S(1)}, f32[8,128,128]{2,1,0:T(8,128)S(1)}, u32[]{:S(2)}, u32[]{:S(2)}) collective-permute-start(f32[8,128,128]{2,1,0:T(8,128)S(1)} %get-tuple-element.110), channel_id=1, source_target_pairs={{0,30},{2,4},{4,2},{6,8},{8,6},{10,12},{12,10},{14,16},{16,14},{18... | collective-permute-start | bytes 1572872 | tf_op jit(solution)/shard_map/ppermute | solution.py:184
  152.6 29.5 %collective-permute-start.19 = (f32[8,128,128]{2,1,0:T(8,128)S(1)}, f32[8,128,128]{2,1,0:T(8,128)S(1)}, u32[]{:S(2)}, u32[]{:S(2)}) collective-permute-start(f32[8,128,128]{2,1,0:T(8,128)S(1)} %get-tuple-element.94), channel_id=1, source_target_pairs={{0,30},{2,4},{4,2},{6,8},{8,6},{10,12},{12,10},{14,16},{16,14},{18... | collective-permute-start | bytes 1572872 | tf_op jit(solution)/shard_map/ppermute | solution.py:184
  154.3 27.8 %collective-permute-start.20 = (f32[8,128,128]{2,1,0:T(8,128)S(1)}, f32[8,128,128]{2,1,0:T(8,128)S(1)}, u32[]{:S(2)}, u32[]{:S(2)}) collective-permute-start(f32[8,128,128]{2,1,0:T(8,128)S(1)} %get-tuple-element.95), channel_id=1, source_target_pairs={{0,2},{2,0},{4,6},{6,4},{8,10},{10,8},{12,14},{14,12},{16,18},{18,... | collective-permute-start | bytes 1572872 | tf_op jit(solution)/shard_map/ppermute | solution.py:187
  156.1 29.1 %collective-permute-start.37 = (f32[8,128,128]{2,1,0:T(8,128)S(1)}, f32[8,128,128]{2,1,0:T(8,128)S(1)}, u32[]{:S(2)}, u32[]{:S(2)}) collective-permute-start(f32[8,128,128]{2,1,0:T(8,128)S(1)} %get-tuple-element.128), channel_id=1, source_target_pairs={{0,2},{2,0},{4,6},{6,4},{8,10},{10,8},{12,14},{14,12},{16,18},{18,... | collective-permute-start | bytes 1572872 | tf_op jit(solution)/shard_map/ppermute | solution.py:187
  170.6 35.4 %collective-permute-start.33 = (f32[8,128,128]{2,1,0:T(8,128)S(1)}, f32[8,128,128]{2,1,0:T(8,128)S(1)}, u32[]{:S(2)}, u32[]{:S(2)}) collective-permute-start(f32[8,128,128]{2,1,0:T(8,128)S(1)} %get-tuple-element.122), channel_id=1, source_target_pairs={{0,2},{2,0},{4,6},{6,4},{8,10},{10,8},{12,14},{14,12},{16,18},{18,... | collective-permute-start | bytes 1572872 | tf_op jit(solution)/shard_map/ppermute | solution.py:187
  170.7 27.2 %collective-permute-start.36 = (f32[8,128,128]{2,1,0:T(8,128)S(1)}, f32[8,128,128]{2,1,0:T(8,128)S(1)}, u32[]{:S(2)}, u32[]{:S(2)}) collective-permute-start(f32[8,128,128]{2,1,0:T(8,128)S(1)} %get-tuple-element.127), channel_id=1, source_target_pairs={{0,30},{2,4},{4,2},{6,8},{8,6},{10,12},{12,10},{14,16},{16,14},{18... | collective-permute-start | bytes 1572872 | tf_op jit(solution)/shard_map/ppermute | solution.py:184
  182.1 22.3 %collective-permute-start.34 = (f32[8,128,128]{2,1,0:T(8,128)S(1)}, f32[8,128,128]{2,1,0:T(8,128)S(1)}, u32[]{:S(2)}, u32[]{:S(2)}) collective-permute-start(f32[8,128,128]{2,1,0:T(8,128)S(1)} %get-tuple-element.124), channel_id=1, source_target_pairs={{0,30},{2,4},{4,2},{6,8},{8,6},{10,12},{12,10},{14,16},{16,14},{18... | collective-permute-start | bytes 1572872 | tf_op jit(solution)/shard_map/ppermute | solution.py:184
  185.2 24.8 %collective-permute-start.32 = (f32[8,128,128]{2,1,0:T(8,128)S(1)}, f32[8,128,128]{2,1,0:T(8,128)S(1)}, u32[]{:S(2)}, u32[]{:S(2)}) collective-permute-start(f32[8,128,128]{2,1,0:T(8,128)S(1)} %get-tuple-element.121), channel_id=1, source_target_pairs={{0,30},{2,4},{4,2},{6,8},{8,6},{10,12},{12,10},{14,16},{16,14},{18... | collective-permute-start | bytes 1572872 | tf_op jit(solution)/shard_map/ppermute | solution.py:184
  (14 other events, 216.3 us)
